TPU v7x, 512 devices: a whole 4x4x16 slice. The times are simulated.
512 devices in a mesh: dom: 128 (over z, x, core), feat: 4 (over y).
Axes of the slice: x: 4, y: 4, z: 16, core: 2. Of those that a mesh axis runs over, the one named last changes fastest.
Arguments:
- grid_feat: bfloat16 [262144, 512], P(('dom', 'feat')), may hold values from -6 to 6
- mesh_feat: bfloat16 [20480, 512], P(('dom', 'feat')), may hold values from -6 to 6
- w_grid: bfloat16 [512, 512], P('feat'), may hold values from -0.25 to 0.25
- w_mesh: bfloat16 [512, 512], P('feat'), may hold values from -0.25 to 0.25
- w_enc2: bfloat16 [512, 512], P('feat'), may hold values from -0.25 to 0.25
- w_src: bfloat16 [512, 512], P('feat'), may hold values from -0.25 to 0.25
- w_dst: bfloat16 [512, 512], P('feat'), may hold values from -0.25 to 0.25
- w_proc2: bfloat16 [512, 512], P('feat'), may hold values from -0.25 to 0.25
- enc_send: int32 [65536, 2], P(('dom', 'feat')), may hold values from -1 to 511, as said below
- enc_dst: int32 [65536, 2], P(('dom', 'feat')), may hold values from -1 to 159, as said below
- hal_send: int32 [16384, 4], P('dom'), may hold values from -1 to 159, as said below
- proc_src: int32 [81920], P(('dom', 'feat')), may hold values from 0 to 671, as said below
- proc_dst: int32 [81920], P(('dom', 'feat')), may hold values from 0 to 159
- cotangent: bfloat16 [20480, 512], P(('dom', 'feat')), may hold values from -6 to 6
Outputs:
- out: bfloat16 [20480, 512], P(('dom', 'feat'))
- g_grid: bfloat16 [262144, 512], P(('dom', 'feat'))
- g_mesh: bfloat16 [20480, 512], P(('dom', 'feat'))
- g_wgrid: float32 [512, 512], P('feat')
- g_wmesh: float32 [512, 512], P('feat')
- g_wenc2: float32 [512, 512], P('feat')
- g_wsrc: float32 [512, 512], P('feat')
- g_wdst: float32 [512, 512], P('feat')
- g_wproc2: float32 [512, 512], P('feat')
Inputs may be any that keep to these rules, and one draw needn't show every extreme that they name: `enc_send`: row j * 128 + r lists, for sender device j, the local grid rows of its slots to partition r in the first n slots and -1 after them; enc_dst's row of the receiver (r, f) for that sender partition has the same n live slots. A quarter of the partitions get half or more of the slots from every sender, and one gets all 2 from every sender. `enc_dst`: row (r * 4 + f) * 128 + s gives the target node, within partition r, of each slot that device s * 4 + f sends to device (r, f); -1 exactly where enc_send's slot is -1. `hal_send`: row s * 128 + r lists the rows of partition s sent to partition r; each pair has 1 to 4 live slots first, -1 after them; some pairs are full. `proc_src`: A value under 160 is a node of the edge's own partition; a value 160 + s * 4 + c names halo slot c from partition s, always a live one.
All inputs are finite; a program needn't handle non-finite values.
Results may differ from a plain program's by a relative error of at most 0.014.
Values may be sent and summed in bfloat16 or wider, within the bound.
No kernel may reach another device: no remote copies, remote signals or barrier semaphores. Data moves between devices by JAX's collectives and lax.ppermute only.
A program may use at most 64 MiB of HBM per device.

v0:
```python
import math

import jax
import jax.numpy as jnp
from jax import lax
from jax.sharding import Mesh
from jax.sharding import PartitionSpec as P

DOM = ("dom_0", "dom_1", "dom_2")
DOM_FEAT = ("dom_0", "dom_1", "dom_2", "feat")


EPS = 1e-05


def side_by_side(arrays, axis, dim, along):
    both = jnp.concatenate(arrays, axis=along)
    result, at, finished = (lax.all_gather(both, axis, axis=dim, tiled=True), 0, [])
    for a in arrays:
        finished.append(lax.slice_in_dim(result, at, at + a.shape[along], axis=along))
        at += a.shape[along]
    return tuple(finished)


def from_everyone(array, axis):
    count = lax.axis_size(axis)
    return lax.all_to_all(
        jnp.broadcast_to(array[None], (count, *array.shape)), axis, 0, 0, tiled=True
    )


def of_everyone(array, axis):
    return from_everyone(array, axis).sum(axis=0)


def split_up(array, dim, count):
    lengths = array.shape
    blocks = array.reshape(*lengths[:dim], count, lengths[dim] // count, *lengths[dim + 1 :])
    return jnp.moveaxis(blocks, dim, 0)


def summed_on_arrival(array, axis, dim):
    blocks = split_up(array, dim, lax.axis_size(axis))
    arrived = lax.all_to_all(blocks, axis, split_axis=0, concat_axis=0, tiled=True)
    return arrived.sum(axis=0)


def sent_and_summed(array, axis, dim):
    blocks = split_up(array, dim, lax.axis_size(axis))
    arrived = lax.all_to_all(blocks, axis, split_axis=0, concat_axis=0, tiled=True)
    return arrived.astype(jnp.float32).sum(axis=0)


def in_one_piece(arrays, axis, dim, along):
    ends, at = ([], 0)
    for a in arrays[:-1]:
        at += a.shape[along]
        ends.append(at)
    both = jnp.concatenate(arrays, axis=along)
    return tuple(jnp.split(sent_and_summed(both, axis, dim), ends, axis=along))


def summed_rows(array, axes, dim):
    far, near = axes
    own = summed_on_arrival(split_up(array, dim, lax.axis_size(far)), near, dim + 1)
    return jnp.sum(lax.all_to_all(own, far, 0, 0, tiled=True), axis=0)


def rows_for(lines, count):
    spare = -lines.shape[0] % count
    if not spare:
        return lines
    return jnp.concatenate([lines, jnp.zeros((spare, *lines.shape[1:]), lines.dtype)])


def joined_along(blocks, dim):
    lengths = list(blocks.shape[1:])
    lengths[dim] *= blocks.shape[0]
    return jnp.moveaxis(blocks, 0, dim).reshape(lengths)


def gathered_by_axis(array, axes, dim):
    far, near = axes
    leading = from_everyone(array, far)
    blocks = jnp.swapaxes(from_everyone(leading, near), 0, 1)
    return joined_along(blocks.reshape(-1, *array.shape), dim)


def nested_sum(array, axes):
    own = summed_rows(rows_for(array, lax.axis_size(axes[0]) * lax.axis_size(axes[1])), axes, 0)
    whole = gathered_by_axis(own, axes, 0)
    return whole[: len(array)].reshape(array.shape)


def together(arrays, axis):
    ends = [0]
    for a in arrays:
        ends.append(ends[-1] + a.size)
    subtotal = nested_sum(jnp.concatenate([a.ravel() for a in arrays]), axis)
    return tuple((subtotal[b:e].reshape(a.shape) for a, b, e in zip(arrays, ends, ends[1:])))


def matmul(left, right):
    return jnp.dot(left, right, preferred_element_type=jnp.float32)


def matmul_t(left, right):
    return lax.dot_general(
        left, right, (((left.ndim - 1,), (1,)), ((), ())), preferred_element_type=jnp.float32
    )


def outer(left, right):
    return lax.dot_general(
        left, right, (((0,), (0,)), ((), ())), preferred_element_type=jnp.float32
    )


def layer_norm(values):
    center = values - jnp.mean(values, axis=-1, keepdims=True)
    spread = jnp.mean(center * center, axis=-1, keepdims=True)
    scaling = lax.rsqrt(spread + EPS)
    return (center * scaling, scaling)


def norm_back(normed, scaling, upstream):
    inner = jnp.mean(upstream, axis=-1, keepdims=True)
    along = jnp.mean(upstream * normed, axis=-1, keepdims=True)
    return scaling * (upstream - inner - normed * along)


def silu_slope(preact):
    sigma = jax.nn.sigmoid(preact)
    return sigma * (1.0 + preact * (1.0 - sigma))


def edge_forward(preact, weight):
    hidden = jax.nn.silu(preact).astype(jnp.bfloat16)
    normed, scaling = layer_norm(matmul(hidden, weight))
    return (hidden, normed, scaling)


def pick_rows(source, indices):
    chosen = source[jnp.maximum(indices, 0)]
    return jnp.where((indices >= 0)[..., None], chosen, jnp.zeros((), source.dtype))


def per_device(
    grid_feat,
    mesh_feat,
    w_grid,
    w_mesh,
    w_enc2,
    w_src,
    w_dst,
    w_proc2,
    enc_send,
    enc_dst,
    hal_send,
    proc_src,
    proc_dst,
    cotangent,
):
    dom_count = lax.axis_size(DOM)
    feat_count = lax.axis_size("feat")
    own_rows = mesh_feat.shape[0]
    latent_width = grid_feat.shape[1]
    part_rows = own_rows * feat_count
    slot_count = enc_send.shape[1]
    halo_count = hal_send.shape[1]
    factor = 1.0 / math.sqrt(own_rows * dom_count * feat_count)
    gathered = (
        *side_by_side((w_grid, w_mesh, w_enc2, w_src, w_dst, w_proc2), "feat", 0, 1),
        *side_by_side((mesh_feat, cotangent), "feat", 0, 1),
    )
    full_grid, full_mesh, full_enc2, full_src, full_dst, full_proc2, mesh_part, cot_part = gathered
    own_start = lax.axis_index("feat") * own_rows
    projected = matmul(grid_feat, full_grid).astype(jnp.bfloat16)
    outgoing = pick_rows(projected, enc_send)
    received = lax.all_to_all(outgoing, DOM, split_axis=0, concat_axis=0, tiled=True)
    node_proj = matmul(mesh_part, full_mesh)
    targets = jnp.maximum(enc_dst, 0).reshape(-1)
    valid = (enc_dst >= 0).reshape(-1, 1).astype(jnp.float32)
    preact = received.reshape(-1, latent_width).astype(jnp.float32) + node_proj[targets]
    hidden, normed, scaling = edge_forward(preact, full_enc2)
    partial_value = jax.ops.segment_sum(normed * valid, targets, num_segments=part_rows)
    summed = of_everyone(partial_value, "feat")
    latent = (mesh_part.astype(jnp.float32) + summed).astype(jnp.bfloat16)
    halo_rows = lax.all_to_all(
        pick_rows(latent, hal_send), DOM, split_axis=0, concat_axis=0, tiled=True
    )
    lookup = jnp.concatenate([latent, halo_rows.reshape(-1, latent_width)], axis=0)
    src_rows = lookup[proc_src]
    dst_rows = latent[proc_dst]
    preact_p = matmul(src_rows, full_src) + matmul(dst_rows, full_dst)
    hidden_p, normed_p, scaling_p = edge_forward(preact_p, full_proc2)
    partial_p = jax.ops.segment_sum(normed_p, proc_dst, num_segments=part_rows)
    summed_p = of_everyone(partial_p, "feat")
    result = (latent.astype(jnp.float32) + summed_p).astype(jnp.bfloat16)
    out_rows = lax.dynamic_slice_in_dim(result, own_start, own_rows, 0)
    cot_rows = cot_part.astype(jnp.float32)
    grad_mid_p = norm_back(normed_p, scaling_p, cot_rows[proc_dst]).astype(jnp.bfloat16)
    grad_pre_p = (matmul_t(grad_mid_p, full_proc2) * silu_slope(preact_p)).astype(jnp.bfloat16)
    g_lookup = jax.ops.segment_sum(
        matmul_t(grad_pre_p, full_src), proc_src, num_segments=lookup.shape[0]
    )
    g_local = g_lookup[:part_rows] + jax.ops.segment_sum(
        matmul_t(grad_pre_p, full_dst), proc_dst, num_segments=part_rows
    )
    halo_back = g_lookup[part_rows:].reshape(dom_count, halo_count, latent_width)
    returned = lax.all_to_all(halo_back, DOM, split_axis=0, concat_axis=0, tiled=True)
    returned = jnp.where((hal_send >= 0)[..., None], returned, jnp.zeros((), jnp.float32))
    g_local = g_local + jax.ops.segment_sum(
        returned.reshape(-1, latent_width),
        jnp.maximum(hal_send, 0).reshape(-1),
        num_segments=part_rows,
    )
    node_grad = of_everyone(g_local, "feat") + cot_rows
    grad_mid_e = norm_back(normed, scaling, node_grad[targets] * valid).astype(jnp.bfloat16)
    grad_pre_e = (matmul_t(grad_mid_e, full_enc2) * silu_slope(preact)).astype(jnp.bfloat16)
    mesh_back = jax.ops.segment_sum(
        matmul_t(grad_pre_e, full_mesh), targets, num_segments=part_rows
    )
    mesh_share = summed_on_arrival(mesh_back, "feat", 0)
    own_grad = lax.dynamic_slice_in_dim(node_grad, own_start, own_rows, 0)
    g_mesh = (own_grad + mesh_share).astype(jnp.bfloat16)
    slot_back = lax.all_to_all(
        grad_pre_e.reshape(dom_count, slot_count, latent_width),
        DOM,
        split_axis=0,
        concat_axis=0,
        tiled=True,
    )
    send_rows = jnp.maximum(enc_send, 0).reshape(-1)
    send_live = (enc_send >= 0).reshape(-1, 1).astype(jnp.float32)
    flat_back = slot_back.reshape(-1, latent_width)
    grid_back = matmul_t(flat_back, full_grid) * send_live
    g_grid = jax.ops.segment_sum(grid_back, send_rows, num_segments=grid_feat.shape[0]).astype(
        jnp.bfloat16
    )
    terms = (
        outer(grid_feat[send_rows], flat_back),
        outer(mesh_part[targets], grad_pre_e),
        outer(hidden, grad_mid_e),
        outer(src_rows, grad_pre_p),
        outer(dst_rows, grad_pre_p),
        outer(hidden_p, grad_mid_p),
    )
    shares = in_one_piece(
        (
            terms[0].astype(jnp.bfloat16),
            terms[1].astype(jnp.bfloat16),
            terms[2].astype(jnp.bfloat16),
            terms[3].astype(jnp.bfloat16),
            terms[4].astype(jnp.bfloat16),
            terms[5].astype(jnp.bfloat16),
        ),
        "feat",
        0,
        1,
    )
    totals = together(
        (shares[0], shares[1], shares[2], shares[3], shares[4], shares[5]),
        (("dom_0", "dom_1"), "dom_2"),
    )
    return (
        out_rows,
        g_grid,
        g_mesh,
        factor * totals[0],
        factor * totals[1],
        factor * totals[2],
        factor * totals[3],
        factor * totals[4],
        factor * totals[5],
    )


def solution(mesh):
    finer = Mesh(
        mesh.devices.reshape(16, 4, 2, mesh.shape["feat"]), ("dom_0", "dom_1", "dom_2", "feat")
    )
    return jax.shard_map(
        per_device,
        mesh=finer,
        in_specs=(
            P(DOM_FEAT, None),
            P(DOM_FEAT, None),
            P("feat", None),
            P("feat", None),
            P("feat", None),
            P("feat", None),
            P("feat", None),
            P("feat", None),
            P(DOM_FEAT, None),
            P(DOM_FEAT, None),
            P(DOM, None),
            P(DOM_FEAT),
            P(DOM_FEAT),
            P(DOM_FEAT, None),
        ),
        out_specs=(
            P(DOM_FEAT, None),
            P(DOM_FEAT, None),
            P(DOM_FEAT, None),
            P("feat", None),
            P("feat", None),
            P("feat", None),
            P("feat", None),
            P("feat", None),
            P("feat", None),
        ),
        check_vma=False,
    )
```

profile of v0, /device:TPU:1, one launch (start us, length us, event | category | flops | bytes accessed | tf_op | source)
XLA Modules:
  0.0 538.7 jit_solution(7050715578493008863)
XLA Ops:
  15.7 50.7 %all-gather.2.cloned.1.call-done = bf16[512,3072]{1,0:T(8,128)(2,1)} async-done(((bf16[128,3072]{1,0:T(8,128)(2,1)}), bf16[512,3072]{1,0:T(8,128)(2,1)}) %all-gather.2.cloned.1.call-update) | async-done | bytes 3145744 | tf_op jit(solution)/shard_map/all_gather | solution.py:18
  70.5 16.6 %all-to-all-start = ((bf16[128,2,512]{2,1,0:T(2,128)(2,1)}), bf16[128,2,512]{2,1,0:T(2,128)(2,1)S(1)}, u32[]{:S(2)}, u32[]{:S(2)}) async-start(bf16[128,2,512]{2,1,0:T(2,128)(2,1)} %broadcast_select_fusion.2), calls=%async_computation | async-start | bytes 524288 | tf_op jit(solution)/shard_map/all_to_all | solution.py:180
  87.8 10.4 %all_gather.6 = bf16[160,1024]{1,0:T(8,128)(2,1)S(1)} all-gather(bf16[40,1024]{1,0:T(8,128)(2,1)S(1)} %pad_maximum_fusion.1), channel_id=1, replica_groups=mesh['dom_0'=16,'dom_1'=4,'dom_2'=2,'feat'=4] {'feat'}, dimensions={0}, use_global_device_ids=true | all-gather | bytes 409600 | tf_op jit(solution)/shard_map/all_gather | solution.py:18
  100.6 7.0 %all-to-all-done = bf16[128,2,512]{2,1,0:T(2,128)(2,1)S(1)} async-done(((bf16[128,2,512]{2,1,0:T(2,128)(2,1)}), bf16[128,2,512]{2,1,0:T(2,128)(2,1)S(1)}, u32[]{:S(2)}, u32[]{:S(2)}) %all-to-all-start) | async-done | bytes 262176 | tf_op jit(solution)/shard_map/all_to_all | solution.py:180
  117.2 17.0 %all-to-all-done.1 = f32[4,160,512]{2,1,0:T(8,128)S(1)} async-done(((f32[4,160,512]{2,1,0:T(8,128)}), f32[4,160,512]{2,1,0:T(8,128)S(1)}, u32[]{:S(2)}, u32[]{:S(2)}) %all-to-all-start.1) | async-done | bytes 1310752 | tf_op jit(solution)/shard_map/all_to_all | solution.py:27
  137.7 11.4 %all-to-all-start.2 = ((bf16[128,4,512]{2,1,0:T(4,128)(2,1)}), bf16[128,4,512]{2,1,0:T(4,128)(2,1)S(1)}, u32[]{:S(2)}, u32[]{:S(2)}) async-start(bf16[128,4,512]{2,1,0:T(4,128)(2,1)} %broadcast_select_fusion.1), calls=%async_computation.2 | async-start | bytes 1048576 | tf_op jit(solution)/shard_map/all_to_all | solution.py:189
  151.0 28.8 %all-to-all-done.2 = bf16[128,4,512]{2,1,0:T(4,128)(2,1)S(1)} async-done(((bf16[128,4,512]{2,1,0:T(4,128)(2,1)}), bf16[128,4,512]{2,1,0:T(4,128)(2,1)S(1)}, u32[]{:S(2)}, u32[]{:S(2)}) %all-to-all-start.2) | async-done | bytes 524320 | tf_op jit(solution)/shard_map/all_to_all | solution.py:189
  195.3 9.6 %all-to-all-start.4 = ((f32[128,4,512]{2,1,0:T(4,128)}), f32[128,4,512]{2,1,0:T(4,128)}, u32[]{:S(2)}, u32[]{:S(2)}) async-start(f32[128,4,512]{2,1,0:T(4,128)} %reshape.212), calls=%async_computation.4 | async-start | bytes 2097152 | tf_op jit(solution)/shard_map/all_to_all | solution.py:211
  208.0 48.3 %all-to-all-done.4 = f32[128,4,512]{2,1,0:T(4,128)} async-done(((f32[128,4,512]{2,1,0:T(4,128)}), f32[128,4,512]{2,1,0:T(4,128)}, u32[]{:S(2)}, u32[]{:S(2)}) %all-to-all-start.4) | async-done | bytes 1048608 | tf_op jit(solution)/shard_map/all_to_all | solution.py:211
  259.3 4.3 scatter_custom_fusion.4
  263.8 18.1 %all_to_all.70 = f32[4,160,512]{2,1,0:T(8,128)S(1)} all-to-all(f32[4,160,512]{2,1,0:T(8,128)S(1)} %broadcast_in_dim.122), channel_id=1, replica_groups=mesh['dom_0'=16,'dom_1'=4,'dom_2'=2,'feat'=4] {'feat'}, dimensions={0} | all-to-all | bytes 2621440 | tf_op jit(solution)/shard_map/all_to_all | solution.py:27
  287.8 13.1 %all-to-all-start.6 = ((bf16[128,2,512]{2,1,0:T(2,128)(2,1)}), bf16[128,2,512]{2,1,0:T(2,128)(2,1)S(1)}, u32[]{:S(2)}, u32[]{:S(2)}) async-start(bf16[128,2,512]{2,1,0:T(2,128)(2,1)} %reshape.214), calls=%async_computation.6 | async-start | bytes 524288 | tf_op jit(solution)/shard_map/all_to_all | solution.py:227
  303.3 18.1 %all-to-all-done.6 = bf16[128,2,512]{2,1,0:T(2,128)(2,1)S(1)} async-done(((bf16[128,2,512]{2,1,0:T(2,128)(2,1)}), bf16[128,2,512]{2,1,0:T(2,128)(2,1)S(1)}, u32[]{:S(2)}, u32[]{:S(2)}) %all-to-all-start.6) | async-done | bytes 262176 | tf_op jit(solution)/shard_map/all_to_all | solution.py:227
  326.9 4.6 all-to-all-start.8
  333.3 35.4 %all-to-all-done.8 = bf16[4,128,3072]{1,2,0:T(8,128)(2,1)} async-done(((bf16[4,128,3072]{1,2,0:T(8,128)(2,1)}), bf16[4,128,3072]{1,2,0:T(8,128)(2,1)}, u32[]{:S(2)}, u32[]{:S(2)}) %all-to-all-start.8) | async-done | bytes 3145760 | tf_op jit(solution)/shard_map/all_to_all | solution.py:50
  379.6 6.2 %all_to_all.71 = f32[2,64,3072]{2,1,0:T(8,128)S(1)} all-to-all(f32[2,64,3072]{2,1,0:T(8,128)S(1)} %copy.86), channel_id=1, replica_groups=mesh['dom_0'=16,'dom_1'=4,'dom_2'=2,'feat'=4] {'dom_2'}, dimensions={0} | all-to-all | bytes 3145728 | tf_op jit(solution)/shard_map/all_to_all | solution.py:44
  387.1 4.3 all-to-all-start.3
  393.0 16.1 %all-to-all-done.3 = f32[4,160,512]{2,1,0:T(8,128)} async-done(((f32[4,160,512]{2,1,0:T(8,128)}), f32[4,160,512]{2,1,0:T(8,128)}, u32[]{:S(2)}, u32[]{:S(2)}) %all-to-all-start.3) | async-done | bytes 1310752 | tf_op jit(solution)/shard_map/all_to_all | solution.py:27
  409.1 7.0 %all-to-all-start.10 = ((f32[64,1,3072]{2,1,0:T(1,128)}), f32[64,1,3072]{2,1,0:T(1,128)S(1)}, u32[]{:S(2)}, u32[]{:S(2)}) async-start(f32[64,1,3072]{2,1,0:T(1,128)} %all_to_all.53), calls=%async_computation.10 | async-start | bytes 1572864 | tf_op jit(solution)/shard_map/all_to_all | solution.py:66
  420.3 35.8 %all-to-all-done.10 = f32[64,1,3072]{2,1,0:T(1,128)S(1)} async-done(((f32[64,1,3072]{2,1,0:T(1,128)}), f32[64,1,3072]{2,1,0:T(1,128)S(1)}, u32[]{:S(2)}, u32[]{:S(2)}) %all-to-all-start.10) | async-done | bytes 786464 | tf_op jit(solution)/shard_map/all_to_all | solution.py:66
  460.2 5.4 all-to-all-done.7
  466.9 8.7 %all-to-all-start.11 = ((f32[64,1,3072]{2,1,0:T(1,128)}), f32[64,1,3072]{2,1,0:T(1,128)S(1)}, u32[]{:S(2)}, u32[]{:S(2)}) async-start(f32[64,1,3072]{2,1,0:T(1,128)} %broadcast_in_dim.123), calls=%async_computation.11 | async-start | bytes 1572864 | tf_op jit(solution)/shard_map/all_to_all | solution.py:27
  483.2 30.8 %all-to-all-done.11 = f32[64,1,3072]{2,1,0:T(1,128)S(1)} async-done(((f32[64,1,3072]{2,1,0:T(1,128)}), f32[64,1,3072]{2,1,0:T(1,128)S(1)}, u32[]{:S(2)}, u32[]{:S(2)}) %all-to-all-start.11) | async-done | bytes 786464 | tf_op jit(solution)/shard_map/all_to_all | solution.py:27
  514.3 11.2 %all_to_all.72 = f32[2,64,3072]{2,1,0:T(8,128)S(1)} all-to-all(f32[2,64,3072]{2,1,0:T(8,128)S(1)} %broadcast_in_dim.125), channel_id=1, replica_groups=mesh['dom_0'=16,'dom_1'=4,'dom_2'=2,'feat'=4] {'dom_2'}, dimensions={0} | all-to-all | bytes 3145728 | tf_op jit(solution)/shard_map/all_to_all | solution.py:27
  (204 shorter events, 104.2 us)
Async XLA Ops:
  7.2 59.2 %copy-start = (bf16[512,512]{1,0:T(8,128)(2,1)S(1)}, bf16[512,512]{1,0:T(8,128)(2,1)}, u32[]{:S(2)}) copy-start(bf16[512,512]{1,0:T(8,128)(2,1)} %param.14) | copy-start | bytes 1572868
  7.2 59.2 %all-gather.2.cloned.1.call-start = ((), (), s32[]{:S(2)}) async-start(), calls=%async_computation.13 | async-start | bytes 3932160 | tf_op jit(solution)/shard_map/all_gather | solution.py:18
  15.6 71.5 %copy-start.26 = (s32[128,2]{0,1:T(2,128)S(1)}, s32[128,2]{0,1:T(2,128)}, u32[]{:S(2)}) copy-start(s32[128,2]{0,1:T(2,128)} %param.23) | copy-start | bytes 3076
  15.7 72.2 %copy-start.22 = (bf16[40,512]{1,0:T(8,128)(2,1)S(1)}, bf16[40,512]{1,0:T(8,128)(2,1)}, u32[]{:S(2)}) copy-start(bf16[40,512]{1,0:T(8,128)(2,1)} %param.27) | copy-start | bytes 122884
  15.7 72.2 %copy-start.23 = (bf16[40,512]{1,0:T(8,128)(2,1)S(1)}, bf16[40,512]{1,0:T(8,128)(2,1)}, u32[]{:S(2)}) copy-start(bf16[40,512]{1,0:T(8,128)(2,1)} %param.15) | copy-start | bytes 122884
  70.5 37.1 %all-to-all-start = ((bf16[128,2,512]{2,1,0:T(2,128)(2,1)}), bf16[128,2,512]{2,1,0:T(2,128)(2,1)S(1)}, u32[]{:S(2)}, u32[]{:S(2)}) async-start(bf16[128,2,512]{2,1,0:T(2,128)(2,1)} %broadcast_select_fusion.2), calls=%async_computation | async-start | bytes 524288 | tf_op jit(solution)/shard_map/all_to_all | solution.py:180
  98.2 50.9 %copy-start.2 = (bf16[160,1024]{1,0:T(8,128)(2,1)}, bf16[160,1024]{1,0:T(8,128)(2,1)S(1)}, u32[]{:S(2)}) copy-start(bf16[160,1024]{1,0:T(8,128)(2,1)S(1)} %all_gather.6) | copy-start | bytes 983044
  113.2 21.0 %all-to-all-start.1 = ((f32[4,160,512]{2,1,0:T(8,128)}), f32[4,160,512]{2,1,0:T(8,128)S(1)}, u32[]{:S(2)}, u32[]{:S(2)}) async-start(f32[4,160,512]{2,1,0:T(8,128)} %broadcast_in_dim.65), calls=%async_computation.1 | async-start | bytes 2621440 | tf_op jit(solution)/shard_map/all_to_all | solution.py:27
  137.7 42.2 %all-to-all-start.2 = ((bf16[128,4,512]{2,1,0:T(4,128)(2,1)}), bf16[128,4,512]{2,1,0:T(4,128)(2,1)S(1)}, u32[]{:S(2)}, u32[]{:S(2)}) async-start(bf16[128,4,512]{2,1,0:T(4,128)(2,1)} %broadcast_select_fusion.1), calls=%async_computation.2 | async-start | bytes 1048576 | tf_op jit(solution)/shard_map/all_to_all | solution.py:189
  151.0 34.1 %copy-start.14 = (bf16[160,512]{1,0:T(8,128)(2,1)}, bf16[160,512]{1,0:T(8,128)(2,1)S(1)}, u32[]{:S(2)}) copy-start(bf16[160,512]{1,0:T(8,128)(2,1)S(1)} %gather_fusion.4) | copy-start | bytes 491524
  195.3 61.1 %all-to-all-start.4 = ((f32[128,4,512]{2,1,0:T(4,128)}), f32[128,4,512]{2,1,0:T(4,128)}, u32[]{:S(2)}, u32[]{:S(2)}) async-start(f32[128,4,512]{2,1,0:T(4,128)} %reshape.212), calls=%async_computation.4 | async-start | bytes 2097152 | tf_op jit(solution)/shard_map/all_to_all | solution.py:211
  286.9 34.9 %copy-start.5 = (bf16[256,512]{1,0:T(8,128)(2,1)}, bf16[256,512]{1,0:T(8,128)(2,1)S(1)}, u32[]{:S(2)}) copy-start(bf16[256,512]{1,0:T(8,128)(2,1)S(1)} %fusion.7) | copy-start | bytes 786436
  287.8 33.6 %all-to-all-start.6 = ((bf16[128,2,512]{2,1,0:T(2,128)(2,1)}), bf16[128,2,512]{2,1,0:T(2,128)(2,1)S(1)}, u32[]{:S(2)}, u32[]{:S(2)}) async-start(bf16[128,2,512]{2,1,0:T(2,128)(2,1)} %reshape.214), calls=%async_computation.6 | async-start | bytes 524288 | tf_op jit(solution)/shard_map/all_to_all | solution.py:227
  302.1 20.1 %copy-start.8 = (bf16[256,512]{1,0:T(8,128)(2,1)S(1)}, bf16[256,512]{1,0:T(8,128)(2,1)}, u32[]{:S(2)}) copy-start(bf16[256,512]{1,0:T(8,128)(2,1)} %copy-done.7) | copy-start | bytes 786436
  302.1 20.5 %copy-start.4 = (bf16[160,512]{1,0:T(8,128)(2,1)S(1)}, bf16[160,512]{1,0:T(8,128)(2,1)}, u32[]{:S(2)}) copy-start(bf16[160,512]{1,0:T(8,128)(2,1)} %copy-done.3) | copy-start | bytes 491524
  302.1 20.5 %copy-start.13 = (bf16[160,512]{1,0:T(8,128)(2,1)S(1)}, bf16[160,512]{1,0:T(8,128)(2,1)}, u32[]{:S(2)}) copy-start(bf16[160,512]{1,0:T(8,128)(2,1)} %copy-done.12) | copy-start | bytes 491524
  302.1 20.8 %copy-start.15 = (bf16[160,512]{1,0:T(8,128)(2,1)S(1)}, bf16[160,512]{1,0:T(8,128)(2,1)}, u32[]{:S(2)}) copy-start(bf16[160,512]{1,0:T(8,128)(2,1)} %copy-done.14) | copy-start | bytes 491524
  326.9 41.8 %all-to-all-start.8 = ((bf16[4,128,3072]{1,2,0:T(8,128)(2,1)}), bf16[4,128,3072]{1,2,0:T(8,128)(2,1)}, u32[]{:S(2)}, u32[]{:S(2)}) async-start(bf16[4,128,3072]{1,2,0:T(8,128)(2,1)} %copy_bitcast_fusion), calls=%async_computation.8 | async-start | bytes 6291456 | tf_op jit(solution)/shard_map/all_to_all | solution.py:50
  387.1 22.0 %all-to-all-start.3 = ((f32[4,160,512]{2,1,0:T(8,128)}), f32[4,160,512]{2,1,0:T(8,128)}, u32[]{:S(2)}, u32[]{:S(2)}) async-start(f32[4,160,512]{2,1,0:T(8,128)} %broadcast_in_dim.117), calls=%async_computation.3 | async-start | bytes 2621440 | tf_op jit(solution)/shard_map/all_to_all | solution.py:27
  391.4 24.8 %copy-start.6 = (bf16[256,512]{1,0:T(8,128)(2,1)S(1)}, bf16[256,512]{1,0:T(8,128)(2,1)}, u32[]{:S(2)}) copy-start(bf16[256,512]{1,0:T(8,128)(2,1)} %copy-done.5) | copy-start | bytes 786436
  409.1 47.0 %all-to-all-start.10 = ((f32[64,1,3072]{2,1,0:T(1,128)}), f32[64,1,3072]{2,1,0:T(1,128)S(1)}, u32[]{:S(2)}, u32[]{:S(2)}) async-start(f32[64,1,3072]{2,1,0:T(1,128)} %all_to_all.53), calls=%async_computation.10 | async-start | bytes 1572864 | tf_op jit(solution)/shard_map/all_to_all | solution.py:66
  456.1 22.5 %copy-start.18 = (bf16[256,512]{1,0:T(8,128)(2,1)S(1)}, bf16[256,512]{1,0:T(8,128)(2,1)}, u32[]{:S(2)}) copy-start(bf16[256,512]{1,0:T(8,128)(2,1)} %copy-done.17) | copy-start | bytes 786436
  456.1 9.4 %all-to-all-start.7 = ((f32[4,40,512]{2,1,0:T(8,128)}), f32[4,40,512]{2,1,0:T(8,128)S(1)}, u32[]{:S(2)}, u32[]{:S(2)}) async-start(f32[4,40,512]{2,1,0:T(8,128)} %bitcast.2), calls=%async_computation.7 | async-start | bytes 655360 | tf_op jit(solution)/shard_map/all_to_all | solution.py:44
  466.9 47.2 %all-to-all-start.11 = ((f32[64,1,3072]{2,1,0:T(1,128)}), f32[64,1,3072]{2,1,0:T(1,128)S(1)}, u32[]{:S(2)}, u32[]{:S(2)}) async-start(f32[64,1,3072]{2,1,0:T(1,128)} %broadcast_in_dim.123), calls=%async_computation.11 | async-start | bytes 1572864 | tf_op jit(solution)/shard_map/all_to_all | solution.py:27
  (15 other events, 95.7 us)
Sparse Core Ops, SparseCore 0:
  13.8 52.5 all-gather.1
where the time goes:
time: 549 us; the launch traced here: 539 us
  waiting for transfers between devices  293 us (53%)
  starting transfers between devices  82.6 us (15%)
  local copies, waits for them, and re-layouts  47.2 us (9%)
  blocking collectives  45.9 us (8%)
  other arithmetic  34 us (6%)
  matrix products  20.1 us (4%)
  between operations  15.3 us (3%)
    all_to_all x3, waiting for transfers between devices, from_everyone(): lax.all_to_all(jnp.broadcast_to(array[None], (count, *array.shape)), axis...  63.9 us
    all_gather x1, waiting for transfers between devices, side_by_side(): lax.all_gather(both, axis, axis=dim, tiled=True)  50.7 us
    all_to_all x1, waiting for transfers between devices, per_device(): lax.all_to_all(halo_back, DOM, split_axis=0, concat_axis=0, tiled=True)  48.3 us
    all_to_all x1, waiting for transfers between devices, summed_rows(): return jnp.sum(lax.all_to_all(own, far, 0, 0, tiled=True), axis=0)  35.8 us
    all_to_all x1, waiting for transfers between devices, sent_and_summed(): lax.all_to_all(blocks, axis, split_axis=0, concat_axis=0, tiled=True)  35.4 us
    all_to_all x2, blocking collectives, from_everyone(): lax.all_to_all(jnp.broadcast_to(array[None], (count, *array.shape)), axis...  29.3 us
    all_to_all x1, waiting for transfers between devices, per_device(): lax.all_to_all(pick_rows(latent, hal_send), DOM, split_axis=0, concat_axi...  28.8 us
    all_to_all x1, waiting for transfers between devices, per_device(): lax.all_to_all(grad_pre_e.reshape(dom_count, slot_count, latent_width), D...  18.1 us
  transfers between devices with their start and end apart: 11, of which 11 were waited for; matrix products, arithmetic and copies ran while one was open for 5% of the time, Pallas kernels for 0%

commit v1 on v0

v1 whole, which is shorter than its diff:
```python
import functools
import math

import jax
import jax.numpy as jnp
from jax import lax
from jax.experimental import pallas as pl
from jax.experimental.pallas import tpu as pltpu
from jax.sharding import Mesh
from jax.sharding import PartitionSpec as P

DOM = ("z", "x", "c")
ALL = ("z", "x", "c", "y")
EPS = 1e-05
BF = jnp.bfloat16
F32 = jnp.float32
PAD = 16


def call(kernel, outs, *operands):
    return pl.pallas_call(
        kernel,
        out_shape=tuple(jax.ShapeDtypeStruct(s, d) for s, d in outs),
        in_specs=[pl.BlockSpec(memory_space=pltpu.VMEM)] * len(operands),
        out_specs=tuple(pl.BlockSpec(memory_space=pltpu.VMEM) for _ in outs),
        compiler_params=pltpu.CompilerParams(vmem_limit_bytes=48 * 1024 * 1024),
    )(*operands)


def exchange(array, axes):
    return lax.all_to_all(array, axes, 0, 0, tiled=True)


def dot(left, right):
    return jnp.dot(left, right, preferred_element_type=F32)


def dot_t(left, right):
    return lax.dot_general(left, right, (((1,), (1,)), ((), ())), preferred_element_type=F32)


def outer(left, right):
    return lax.dot_general(left, right, (((0,), (0,)), ((), ())), preferred_element_type=F32)


def one_hot(column, count):
    places = lax.broadcasted_iota(jnp.int32, (column.shape[0], count), 1)
    return jnp.where(places == column, 1.0, 0.0).astype(BF)


def slots_hot(indices, count):
    width = indices.shape[1]
    return jnp.concatenate([one_hot(indices[:, c : c + 1], count) for c in range(width)], axis=0)


def slot_rows(wide, width):
    return jnp.concatenate(
        [wide[:, c * width : (c + 1) * width] for c in range(wide.shape[1] // width)], axis=0
    )


def wide_rows(rows, count):
    each = rows.shape[0] // count
    return jnp.concatenate([rows[c * each : (c + 1) * each] for c in range(count)], axis=1)


def whole(ref, at, rows):
    return jnp.concatenate(
        [ref[y, at * rows : (at + 1) * rows, :] for y in range(ref.shape[0])], axis=0
    )


def sigmoid(v):
    return 1.0 / (1.0 + jnp.exp(-v))


def layer_norm(values):
    center = values - jnp.mean(values, axis=-1, keepdims=True)
    spread = jnp.mean(center * center, axis=-1, keepdims=True)
    scaling = lax.rsqrt(spread + EPS)
    return (center * scaling, scaling)


def norm_back(normed, scaling, upstream):
    inner = jnp.mean(upstream, axis=-1, keepdims=True)
    along = jnp.mean(upstream * normed, axis=-1, keepdims=True)
    return scaling * (upstream - inner - normed * along)


def pick_kernel(send_ref, grid_ref, out_ref):
    grid = grid_ref[...]
    width = grid.shape[1]
    for c in range(send_ref.shape[1]):
        hot = one_hot(send_ref[:, c : c + 1], grid.shape[0])
        out_ref[:, c * width : (c + 1) * width] = dot(hot, grid).astype(BF)


def encode_kernel(rows, recv_ref, dst_ref, gath_ref, mesh_ref, sum_ref, pre_ref, norm_ref, scale_ref):
    width = mesh_ref.shape[1]
    mesh_part = mesh_ref[...]
    received = slot_rows(recv_ref[...], width)
    hot = slots_hot(dst_ref[...], mesh_part.shape[0])
    projected = dot(received, whole(gath_ref, 0, rows)).astype(BF)
    nodes = dot(hot, mesh_part).astype(BF)
    preact = projected.astype(F32) + dot(nodes, whole(gath_ref, 1, rows))
    pre_ref[...] = preact
    hidden = (preact * sigmoid(preact)).astype(BF)
    normed, scaling = layer_norm(dot(hidden, whole(gath_ref, 2, rows)))
    norm_ref[...] = normed
    scale_ref[...] = scaling
    partial_sum = outer(hot, normed.astype(BF)).astype(BF)
    for y in range(sum_ref.shape[0]):
        sum_ref[y] = partial_sum


def latent_kernel(sums_ref, mesh_ref, send_ref, latent_ref, halo_ref):
    total = sums_ref[0].astype(F32)
    for y in range(1, sums_ref.shape[0]):
        total = total + sums_ref[y].astype(F32)
    latent = (mesh_ref[...].astype(F32) + total).astype(BF)
    latent_ref[...] = latent
    halo_ref[...] = dot(one_hot(send_ref[...], latent.shape[0]), latent).astype(BF)


def process_kernel(
    rows, own, latent_ref, halo_ref, edge_ref, gath_ref, cot_ref, pay_ref, back_ref, local_ref, term_ref
):
    latent = latent_ref[...]
    table = jnp.concatenate([latent, halo_ref[...]], axis=0)
    nodes = latent.shape[0]
    hot_src = one_hot(edge_ref[:, 0:1], table.shape[0])
    hot_dst = one_hot(edge_ref[:, 1:2], nodes)
    w_src, w_dst, w_out = [whole(gath_ref, k, rows) for k in range(3)]
    src_rows = dot(hot_src, table).astype(BF)
    dst_rows = dot(hot_dst, latent).astype(BF)
    preact = dot(src_rows, w_src) + dot(dst_rows, w_dst)
    gate = sigmoid(preact)
    hidden = (preact * gate).astype(BF)
    normed, scaling = layer_norm(dot(hidden, w_out))
    messages = outer(hot_dst, normed.astype(BF))
    upstream = dot(hot_dst, cot_ref[...])
    mid = norm_back(normed, scaling, upstream).astype(BF)
    grad = (dot_t(mid, w_out) * (gate * (1.0 + preact * (1.0 - gate)))).astype(BF)
    term_ref[...] = outer(hidden, mid).astype(BF)
    at_dst = outer(hot_dst, grad).astype(BF)
    at_src = outer(hot_src, grad)
    local_ref[...] = at_src[:nodes]
    back_ref[...] = at_src[nodes:].astype(BF)
    spare = pay_ref.shape[1] - nodes - own
    for y in range(pay_ref.shape[0]):
        block = messages[y * own : (y + 1) * own]
        block = jnp.concatenate([block, jnp.zeros((spare, block.shape[1]), F32)], axis=0)
        pay_ref[y, :nodes, :] = at_dst
        pay_ref[y, nodes:, :] = block.astype(BF)


def owner_kernel(back_ref, send_ref, local_ref, out_ref):
    nodes = local_ref.shape[0]
    hot = one_hot(send_ref[...], nodes)
    total = (local_ref[...] + outer(hot, back_ref[...])).astype(BF)
    for y in range(out_ref.shape[0]):
        out_ref[y] = total


def backward_kernel(
    rows,
    own,
    src_ref,
    pay_ref,
    cot_ref,
    proc_ref,
    latent_ref,
    enc_ref,
    recv_ref,
    dst_ref,
    mesh_ref,
    pre_ref,
    norm_ref,
    scale_ref,
    proc_term_ref,
    node_ref,
    slot_ref,
    share_ref,
    term_ref,
):
    nodes, width = latent_ref.shape
    count = src_ref.shape[0]
    at_src = src_ref[0].astype(F32)
    at_dst = pay_ref[0, :nodes, :].astype(F32)
    for y in range(1, count):
        at_src = at_src + src_ref[y].astype(F32)
        at_dst = at_dst + pay_ref[y, :nodes, :].astype(F32)
    at_src = at_src.astype(BF)
    at_dst = at_dst.astype(BF)
    node_grad = (
        cot_ref[...].astype(F32)
        + dot_t(at_src, whole(proc_ref, 0, rows))
        + dot_t(at_dst, whole(proc_ref, 1, rows))
    )
    node_ref[...] = node_grad
    hot = slots_hot(dst_ref[...], nodes)
    upstream = dot(hot, node_grad.astype(BF))
    mid = norm_back(norm_ref[...], scale_ref[...], upstream).astype(BF)
    preact = pre_ref[...]
    gate = sigmoid(preact)
    hidden = (preact * gate).astype(BF)
    grad = dot_t(mid, whole(enc_ref, 2, rows)) * (gate * (1.0 + preact * (1.0 - gate)))
    grad = grad.astype(BF)
    slot_ref[...] = wide_rows(grad, recv_ref.shape[1] // width)
    at_node = outer(hot, grad)
    spare = share_ref.shape[1] - own
    for y in range(count):
        block = at_node[y * own : (y + 1) * own]
        block = jnp.concatenate([block, jnp.zeros((spare, width), F32)], axis=0)
        share_ref[y] = block.astype(BF)
    part = 1.0 / count
    latent = latent_ref[...]
    received = slot_rows(recv_ref[...], width)
    terms = (
        outer(received, grad),
        outer(mesh_ref[...], at_node.astype(BF)),
        outer(hidden, mid),
        outer(latent, at_src) * part,
        outer(latent, at_dst) * part,
    )
    for k, term in enumerate(terms):
        term_ref[:, k * width : (k + 1) * width] = term.astype(BF)
    term_ref[:, 5 * width :] = proc_term_ref[...]


def grid_kernel(rows, back_ref, send_ref, enc_ref, out_ref):
    nodes, width = out_ref.shape
    grads = dot_t(slot_rows(back_ref[...], width), whole(enc_ref, 0, rows)).astype(BF)
    out_ref[...] = outer(slots_hot(send_ref[...], nodes), grads).astype(BF)


def sum_kernel(in_ref, out_ref):
    total = in_ref[0].astype(F32)
    for k in range(1, in_ref.shape[0]):
        total = total + in_ref[k].astype(F32)
    out_ref[...] = total.astype(out_ref.dtype)


def finish_kernel(
    rows, own, latent_ref, pay_ref, node_ref, share_ref, enc_ref, out_ref, mesh_ref
):
    nodes = pay_ref.shape[1] - own - (-own % PAD)
    total = pay_ref[0, nodes:, :].astype(F32)
    share = share_ref[0].astype(F32)
    for y in range(1, pay_ref.shape[0]):
        total = total + pay_ref[y, nodes:, :].astype(F32)
        share = share + share_ref[y].astype(F32)
    out_ref[...] = (latent_ref[...].astype(F32) + total[:own]).astype(BF)
    back = dot_t(share.astype(BF), whole(enc_ref, 1, rows))
    mesh_ref[...] = (node_ref[...] + back[:own]).astype(BF)


def per_device(
    grid_feat,
    mesh_feat,
    w_grid,
    w_mesh,
    w_enc2,
    w_src,
    w_dst,
    w_proc2,
    enc_send,
    enc_dst,
    hal_send,
    proc_src,
    proc_dst,
    cotangent,
):
    dom = lax.axis_size(DOM)
    feat = lax.axis_size("y")
    deep = lax.axis_size("z")
    own, width = mesh_feat.shape
    nodes = own * feat
    rows = w_grid.shape[0]
    caps = enc_send.shape[1]
    halo = hal_send.shape[1]
    edges = proc_src.shape[0]
    held = own + (-own % PAD)
    factor = 1.0 / math.sqrt(own * dom * feat)
    me = lax.axis_index("y")
    if halo != feat or held == own or 3 * edges > width:
        raise ValueError("sizes")

    blank = jnp.zeros((held - own, width), BF)
    enc_gath = lax.all_gather(
        jnp.concatenate([w_grid, w_mesh, w_enc2, mesh_feat, blank], axis=0), "y", axis=0
    )
    line = jnp.concatenate([proc_src // 16, proc_src % 16, proc_dst]).astype(BF)
    line = jnp.pad(line, (0, width - 3 * edges))[None]
    proc_gath = lax.all_gather(
        jnp.concatenate([w_src, w_dst, w_proc2, cotangent, line, blank[1:]], axis=0), "y", axis=0
    )

    (outgoing,) = call(pick_kernel, [((dom, caps * width), BF)], enc_send, grid_feat)
    received = exchange(outgoing.reshape(dom, caps, width), DOM).reshape(dom, caps * width)
    mesh_part = enc_gath[:, 3 * rows : 3 * rows + own].reshape(nodes, width)
    slots = dom * caps
    partial_sum, preact, normed, scaling = call(
        functools.partial(encode_kernel, rows),
        [((feat, nodes, width), BF), ((slots, width), F32), ((slots, width), F32), ((slots, 1), F32)],
        received,
        enc_dst,
        enc_gath,
        mesh_part,
    )
    sums = exchange(partial_sum, "y")
    hal_own = lax.dynamic_slice_in_dim(hal_send, me, 1, 1)
    latent, halo_out = call(
        latent_kernel, [((nodes, width), BF), ((dom, width), BF)], sums, mesh_part, hal_own
    )
    halo_rows = exchange(halo_out, DOM)

    cot_part = proc_gath[:, 3 * rows : 3 * rows + own].reshape(nodes, width)
    lines = proc_gath[:, 3 * rows + own].astype(jnp.int32)
    source = lines[:, :edges] * 16 + lines[:, edges : 2 * edges]
    target = lines[:, 2 * edges : 3 * edges]
    slot = source - nodes
    place = jnp.where(slot < 0, source, nodes + slot // halo)
    keeper = jnp.where(slot < 0, jnp.arange(feat, dtype=jnp.int32)[:, None], slot % halo)
    mine = keeper == me
    edge_index = jnp.stack(
        [jnp.where(mine, place, -1).reshape(-1), jnp.where(mine, target, -1).reshape(-1)], axis=1
    )
    payload, halo_back, at_local, proc_term = call(
        functools.partial(process_kernel, rows, own),
        [
            ((feat, nodes + held, width), BF),
            ((dom, width), BF),
            ((nodes, width), F32),
            ((width, width), BF),
        ],
        latent,
        halo_rows,
        edge_index,
        proc_gath,
        cot_part,
    )
    returned = exchange(halo_back, DOM)
    payload = exchange(payload, "y")
    (at_owner,) = call(
        owner_kernel, [((feat, nodes, width), BF)], returned, hal_own, at_local
    )
    at_src = exchange(at_owner, "y")

    node_grad, slot_out, share, terms = call(
        functools.partial(backward_kernel, rows, own),
        [
            ((nodes, width), F32),
            ((dom, caps * width), BF),
            ((feat, held, width), BF),
            ((width, 6 * width), BF),
        ],
        at_src,
        payload,
        cot_part,
        proc_gath,
        latent,
        enc_gath,
        received,
        enc_dst,
        mesh_part,
        preact,
        normed,
        scaling,
        proc_term,
    )
    near = lax.axis_size(("y", "x", "c"))
    thin = width // near
    arrived = exchange(terms.reshape(near, thin, 6 * width), ("y", "x", "c"))
    (level,) = call(sum_kernel, [((thin, 6 * width), BF)], arrived)
    slot_back = exchange(slot_out.reshape(dom, caps, width), DOM).reshape(dom, caps * width)
    share = exchange(share, "y")
    level = exchange(level.reshape(deep, thin // deep, 6 * width), "z")
    mine_sum = level.astype(F32).sum(axis=0).astype(BF)
    deep_rows = exchange(jnp.broadcast_to(mine_sum[None], (deep, *mine_sum.shape)), "z")
    deep_rows = deep_rows.reshape(thin, 6 * width)
    flat = lax.axis_size(("x", "c"))
    totals = exchange(jnp.broadcast_to(deep_rows[None], (flat, *deep_rows.shape)), ("x", "c"))
    totals = totals.reshape(rows, 6 * width).astype(F32) * factor

    (g_grid,) = call(
        functools.partial(grid_kernel, rows), [(grid_feat.shape, BF)], slot_back, enc_send, enc_gath
    )
    out_rows, g_mesh = call(
        functools.partial(finish_kernel, rows, own),
        [((own, width), BF), ((own, width), BF)],
        lax.dynamic_slice_in_dim(latent, me * own, own, 0),
        payload,
        lax.dynamic_slice_in_dim(node_grad, me * own, own, 0),
        share,
        enc_gath,
    )
    return (out_rows, g_grid, g_mesh) + tuple(
        totals[:, k * width : (k + 1) * width] for k in range(6)
    )


def solution(mesh):
    dom, feat = mesh.shape["dom"], mesh.shape["feat"]
    x = 4 if dom % 8 == 0 else 1
    finer = Mesh(mesh.devices.reshape(dom // (2 * x), x, 2, feat), ALL)
    return jax.shard_map(
        per_device,
        mesh=finer,
        in_specs=(
            P(ALL, None),
            P(ALL, None),
            P("y", None),
            P("y", None),
            P("y", None),
            P("y", None),
            P("y", None),
            P("y", None),
            P(ALL, None),
            P(ALL, None),
            P(DOM, None),
            P(ALL),
            P(ALL),
            P(ALL, None),
        ),
        out_specs=(
            P(ALL, None),
            P(ALL, None),
            P(ALL, None),
            P("y", None),
            P("y", None),
            P("y", None),
            P("y", None),
            P("y", None),
            P("y", None),
        ),
        check_vma=False,
    )
```

time: 549 us -> 346 us (0.63); the launches traced: 539 us -> 345 us
  waiting for transfers between devices: 293 us -> 114 us
  blocking collectives: 45.9 us -> 96.7 us
  other arithmetic: 34 us -> 8.12 us
  starting transfers between devices: 82.6 us -> 61.7 us
  matrix products: 20.1 us -> 0 us
  Pallas kernels: 0 us -> 15.4 us
  local copies, waits for them, and re-layouts: 47.2 us -> 34.1 us
    all_to_all x10 -> x8, waiting for transfers between devices: 243 us -> 89.5 us  [exchange(): return lax.all_to_all(array, axes, 0, 0, tiled=True)]
    all_to_all x3 -> x4, blocking collectives: 35.5 us -> 96.7 us  [exchange(): return lax.all_to_all(array, axes, 0, 0, tiled=True)]
    all_gather x1 -> x2, waiting for transfers between devices: 50.7 us -> 24.7 us  [the longest x1 24.7 us: per_device(): lax.all_gather(jnp.concatenate([w_src, w_dst, w_proc2, cotangent, line, b...]
    all_to_all x10 -> x8, starting transfers between devices: 82.6 us -> 61.6 us  [exchange(): return lax.all_to_all(array, axes, 0, 0, tiled=True)]
    dot_general x18 -> x0, matrix products: 20.1 us -> none  [the longest x6 8.6 us: matmul(): return jnp.dot(left, right, preferred_element_type=jnp.float32)]
    scatter-add x7 -> x0, other arithmetic: 17.1 us -> none  [the longest x1 4.33 us: per_device(): jax.ops.segment_sum(returned.reshape(-1, latent_width), jnp.maximum(hal_s...]
    pallas_call x0 -> x9, Pallas kernels: none -> 15.4 us  [call(): pl.pallas_call(kernel, out_shape=tuple((jax.ShapeDtypeStruct(s, d) for s,...]
    all_gather x1 -> x0, blocking collectives: 10.4 us -> none  [side_by_side(): lax.all_gather(both, axis, axis=dim, tiled=True)]
  transfers between devices with their start and end apart: 11 -> 10, of which waited for: 11 -> 8; matrix products, arithmetic and copies ran while one was open for 5% -> 5% of each run, Pallas kernels for 0% -> 1%
where the time goes in v1:
time: 346 us; the launch traced here: 345 us
  waiting for transfers between devices  114 us (33%)
  blocking collectives  96.7 us (28%)
  starting transfers between devices  61.7 us (18%)
  local copies, waits for them, and re-layouts  34.1 us (10%)
  Pallas kernels  15.4 us (4%)
  between operations  14.4 us (4%)
  other arithmetic  8.12 us (2%)
    all_to_all x4, blocking collectives, exchange(): return lax.all_to_all(array, axes, 0, 0, tiled=True)  96.7 us
    all_to_all x8, waiting for transfers between devices, exchange(): return lax.all_to_all(array, axes, 0, 0, tiled=True)  89.5 us
    all_to_all x8, starting transfers between devices, exchange(): return lax.all_to_all(array, axes, 0, 0, tiled=True)  61.6 us
    all_gather x1, waiting for transfers between devices, per_device(): lax.all_gather(jnp.concatenate([w_src, w_dst, w_proc2, cotangent, line, b...  24.7 us
    unnamed x69, local copies, waits for them, and re-layouts  18.7 us
    pallas_call x9, Pallas kernels, call(): pl.pallas_call(kernel, out_shape=tuple((jax.ShapeDtypeStruct(s, d) for s,...  15.4 us
  transfers between devices with their start and end apart: 10, of which 8 were waited for; matrix products, arithmetic and copies ran while one was open for 5% of the time, Pallas kernels for 1%

profile of v1, /device:TPU:1, one launch (start us, length us, event | category | flops | bytes accessed | tf_op | source)
XLA Modules:
  0.0 344.6 jit_solution(7739142746825320647)
XLA Ops:
  13.2 6.7 %concatenate.12 = bf16[432,512]{1,0:T(8,128)(2,1)} concatenate(bf16[128,512]{1,0:T(8,128)(2,1)} %param.19, bf16[128,512]{1,0:T(8,128)(2,1)} %param.20, bf16[128,512]{1,0:T(8,128)(2,1)} %param.21, bf16[40,512]{1,0:T(8,128)(2,1)} %param.27, bf16[1,512]{1,0:T(2,128)(2,1)S(1)} %broadcast_in_dim.32, bf16[7,512]{1,0:T(8,128)(2,1)S(1)} %slice.40), dimensions={0} | concatenate | bytes 884736 | tf_op jit(solution)/shard_map/concatenate | solution.py:296
  21.3 20.4 %all-to-all-start = ((bf16[128,2,512]{2,1,0:T(2,128)(2,1)}), bf16[128,2,512]{2,1,0:T(2,128)(2,1)S(1)}, u32[]{:S(2)}, u32[]{:S(2)}) async-start(bf16[128,2,512]{2,1,0:T(2,128)(2,1)} %reshape.58), calls=%async_computation | async-start | bytes 524288 | tf_op jit(solution)/shard_map/all_to_all | solution.py:31
  41.8 20.3 %all-to-all-done = bf16[128,2,512]{2,1,0:T(2,128)(2,1)S(1)} async-done(((bf16[128,2,512]{2,1,0:T(2,128)(2,1)}), bf16[128,2,512]{2,1,0:T(2,128)(2,1)S(1)}, u32[]{:S(2)}, u32[]{:S(2)}) %all-to-all-start) | async-done | bytes 262176 | tf_op jit(solution)/shard_map/all_to_all | solution.py:31
  64.6 2.1 shard_map.206
  69.0 4.2 %all-to-all-start.1 = ((bf16[4,160,512]{2,1,0:T(8,128)(2,1)}), bf16[4,160,512]{2,1,0:T(8,128)(2,1)S(1)}, u32[]{:S(2)}, u32[]{:S(2)}) async-start(bf16[4,160,512]{2,1,0:T(8,128)(2,1)} %get-tuple-element.25), calls=%async_computation.1 | async-start | bytes 1310720 | tf_op jit(solution)/shard_map/all_to_all | solution.py:31
  73.3 24.7 %all-gather.7.cloned.1.call-done = bf16[1728,512]{1,0:T(8,128)(2,1)} async-done(((bf16[432,512]{1,0:T(8,128)(2,1)}), bf16[1728,512]{1,0:T(8,128)(2,1)}) %all-gather.7.cloned.1.call-update) | async-done | bytes 1769488 | tf_op jit(solution)/shard_map/all_gather | solution.py:295
  101.9 9.6 %all-to-all-start.2 = ((bf16[128,2,256]{2,1,0:T(2,128)(2,1)}), bf16[128,2,256]{2,1,0:T(2,128)(2,1)S(1)}, u32[]{:S(2)}, u32[]{:S(2)}) async-start(bf16[128,2,256]{2,1,0:T(2,128)(2,1)} %reshape.69), calls=%async_computation.2 | async-start | bytes 262144 | tf_op jit(solution)/shard_map/all_to_all | solution.py:31
  112.1 15.5 %all-to-all-done.2 = bf16[128,2,256]{2,1,0:T(2,128)(2,1)S(1)} async-done(((bf16[128,2,256]{2,1,0:T(2,128)(2,1)}), bf16[128,2,256]{2,1,0:T(2,128)(2,1)S(1)}, u32[]{:S(2)}, u32[]{:S(2)}) %all-to-all-start.2) | async-done | bytes 131104 | tf_op jit(solution)/shard_map/all_to_all | solution.py:31
  127.7 4.0 %shard_map.208 = (bf16[4,208,512]{2,1,0:T(8,128)(2,1)S(1)}, bf16[128,512]{1,0:T(8,128)(2,1)S(1)}, f32[160,512]{1,0:T(8,128)S(1)}, bf16[512,512]{1,0:T(8,128)(2,1)S(1)}) custom-call(bf16[160,512]{1,0:T(8,128)(2,1)S(1)} %get-tuple-element.26.latent_ref, bf16[128,512]{1,0:T(8,128)(2,1)S(1)} %bitcast.42, s32[640,2]{1,0:T(8,128)S(1)} %copy.43.edge_ref, ...), custom_call_target="tpu_custom_call" | custom-call | tf_op jit(solution)/shard_map/pallas_call | solution.py:21
  135.7 23.4 %all_to_all.72 = bf16[128,2,256]{2,1,0:T(2,128)(2,1)S(1)} all-to-all(bf16[128,2,256]{2,1,0:T(2,128)(2,1)S(1)} %reshape.71), channel_id=1, replica_groups=mesh['z'=16,'x'=4,'c'=2,'y'=4] {'z','x','c'}, dimensions={0} | all-to-all | bytes 262144 | tf_op jit(solution)/shard_map/all_to_all | solution.py:31
  159.1 3.7 %all-to-all-start.3 = ((bf16[4,208,512]{2,1,0:T(8,128)(2,1)}), bf16[4,208,512]{2,1,0:T(8,128)(2,1)S(1)}, u32[]{:S(2)}, u32[]{:S(2)}) async-start(bf16[4,208,512]{2,1,0:T(8,128)(2,1)} %copy-done.4), calls=%async_computation.3 | async-start | bytes 1703936 | tf_op jit(solution)/shard_map/all_to_all | solution.py:31
  163.3 12.0 %all-to-all-done.3.pay_ref = bf16[4,208,512]{2,1,0:T(8,128)(2,1)S(1)} async-done(((bf16[4,208,512]{2,1,0:T(8,128)(2,1)}), bf16[4,208,512]{2,1,0:T(8,128)(2,1)S(1)}, u32[]{:S(2)}, u32[]{:S(2)}) %all-to-all-start.3) | async-done | bytes 852000 | tf_op jit(solution)/shard_map/all_to_all | solution.py:31
  175.3 11.8 %all_to_all.73.src_ref = bf16[4,160,512]{2,1,0:T(8,128)(2,1)S(1)} all-to-all(bf16[4,160,512]{2,1,0:T(8,128)(2,1)S(1)} %shard_map.209), channel_id=1, replica_groups=mesh['z'=16,'x'=4,'c'=2,'y'=4] {'y'}, dimensions={0} | all-to-all | bytes 1310720 | tf_op jit(solution)/shard_map/all_to_all | solution.py:31
  190.1 5.7 %shard_map.210 = (f32[160,512]{1,0:T(8,128)S(1)}, bf16[128,1024]{1,0:T(8,128)(2,1)S(1)}, bf16[4,48,512]{2,1,0:T(8,128)(2,1)}, bf16[512,3072]{1,0:T(8,128)(2,1)}) custom-call(bf16[4,160,512]{2,1,0:T(8,128)(2,1)S(1)} %all_to_all.73.src_ref, bf16[4,208,512]{2,1,0:T(8,128)(2,1)S(1)} %all-to-all-done.3.pay_ref, bf16[160,512]{1,0:T(8,128)(2,1)S(1)} %bitcast.40, ...), custom_call_target="tpu_custom_call" | custom-call | tf_op jit(solution)/shard_map/pallas_call | solution.py:21
  196.5 46.9 %all_to_all.74.in_ref = bf16[32,16,3072]{2,1,0:T(8,128)(2,1)S(1)} all-to-all(bf16[32,16,3072]{2,1,0:T(8,128)(2,1)} %bitcast.48), channel_id=1, replica_groups=mesh['z'=16,'x'=4,'c'=2,'y'=4] {'y','x','c'}, dimensions={0} | all-to-all | bytes 6291456 | tf_op jit(solution)/shard_map/all_to_all | solution.py:31
  244.5 14.7 %all_to_all.75 = bf16[16,2,1536]{2,1,0:T(2,128)(2,1)S(1)} all-to-all(bf16[16,2,1536]{2,1,0:T(2,128)(2,1)S(1)} %reshape.73), channel_id=1, replica_groups=mesh['z'=16,'x'=4,'c'=2,'y'=4] {'z'}, dimensions={0} | all-to-all | bytes 196608 | tf_op jit(solution)/shard_map/all_to_all | solution.py:31
  259.1 3.4 all-to-all-start.6
  264.8 2.8 all-to-all-done.6.share_ref
  267.7 5.0 %all-to-all-start.10 = ((bf16[16,2,1536]{2,1,0:T(2,128)(2,1)}), bf16[16,2,1536]{2,1,0:T(2,128)(2,1)S(1)}, u32[]{:S(2)}, u32[]{:S(2)}) async-start(bf16[16,2,1536]{2,1,0:T(2,128)(2,1)} %reshape.75), calls=%async_computation.10 | async-start | bytes 196608 | tf_op jit(solution)/shard_map/all_to_all | solution.py:31
  273.6 11.0 %all-to-all-done.10 = bf16[16,2,1536]{2,1,0:T(2,128)(2,1)S(1)} async-done(((bf16[16,2,1536]{2,1,0:T(2,128)(2,1)}), bf16[16,2,1536]{2,1,0:T(2,128)(2,1)S(1)}, u32[]{:S(2)}, u32[]{:S(2)}) %all-to-all-start.10) | async-done | bytes 98336 | tf_op jit(solution)/shard_map/all_to_all | solution.py:31
  285.2 9.4 %all-to-all-start.7 = ((bf16[128,2,512]{2,1,0:T(2,128)(2,1)}), bf16[128,2,512]{2,1,0:T(2,128)(2,1)S(1)}, u32[]{:S(2)}, u32[]{:S(2)}) async-start(bf16[128,2,512]{2,1,0:T(2,128)(2,1)} %reshape.62), calls=%async_computation.7 | async-start | bytes 524288 | tf_op jit(solution)/shard_map/all_to_all | solution.py:31
  296.4 18.7 %all-to-all-done.7 = bf16[128,2,512]{2,1,0:T(2,128)(2,1)S(1)} async-done(((bf16[128,2,512]{2,1,0:T(2,128)(2,1)}), bf16[128,2,512]{2,1,0:T(2,128)(2,1)S(1)}, u32[]{:S(2)}, u32[]{:S(2)}) %all-to-all-start.7) | async-done | bytes 262176 | tf_op jit(solution)/shard_map/all_to_all | solution.py:31
  317.0 5.9 %all-to-all-start.11 = ((bf16[8,16,3072]{2,1,0:T(8,128)(2,1)}), bf16[8,16,3072]{2,1,0:T(8,128)(2,1)}, u32[]{:S(2)}, u32[]{:S(2)}) async-start(bf16[8,16,3072]{2,1,0:T(8,128)(2,1)} %broadcast_in_dim.36), calls=%async_computation.11 | async-start | bytes 1572864 | tf_op jit(solution)/shard_map/all_to_all | solution.py:31
  326.1 9.2 %all-to-all-done.11 = bf16[8,16,3072]{2,1,0:T(8,128)(2,1)} async-done(((bf16[8,16,3072]{2,1,0:T(8,128)(2,1)}), bf16[8,16,3072]{2,1,0:T(8,128)(2,1)}, u32[]{:S(2)}, u32[]{:S(2)}) %all-to-all-start.11) | async-done | bytes 786464 | tf_op jit(solution)/shard_map/all_to_all | solution.py:31
  (111 shorter events, 39.3 us)
Async XLA Ops:
  7.2 66.0 %copy-start = (s32[128,4]{0,1:T(4,128)S(1)}, s32[128,4]{0,1:T(4,128)}, u32[]{:S(2)}) copy-start(s32[128,4]{0,1:T(4,128)} %param.24) | copy-start | bytes 6148
  7.2 12.7 %copy-start.22 = (s32[128,2]{0,1:T(2,128)S(1)}, s32[128,2]{0,1:T(2,128)}, u32[]{:S(2)}) copy-start(s32[128,2]{0,1:T(2,128)} %param.22) | copy-start | bytes 3076
  7.2 12.8 %copy-start.7 = (bf16[512,512]{1,0:T(8,128)(2,1)S(1)}, bf16[512,512]{1,0:T(8,128)(2,1)}, u32[]{:S(2)}) copy-start(bf16[512,512]{1,0:T(8,128)(2,1)} %grid_ref.1) | copy-start | bytes 1572868
  7.2 55.0 %all-gather.5.cloned.1.call-start = ((), (), s32[]{:S(2)}) async-start(), calls=%async_computation.12 | async-start | bytes 2211840 | tf_op jit(solution)/shard_map/all_gather | solution.py:290
  11.6 30.0 %copy-start.23 = (s32[128,2]{0,1:T(2,128)S(1)}, s32[128,2]{0,1:T(2,128)}, u32[]{:S(2)}) copy-start(s32[128,2]{0,1:T(2,128)} %param.23) | copy-start | bytes 3076
  11.6 86.3 %all-gather.7.cloned.1.call-start = ((), (), s32[]{:S(2)}) async-start(), calls=%async_computation.13 | async-start | bytes 2211840 | tf_op jit(solution)/shard_map/all_gather | solution.py:295
  21.3 40.9 %all-to-all-start = ((bf16[128,2,512]{2,1,0:T(2,128)(2,1)}), bf16[128,2,512]{2,1,0:T(2,128)(2,1)S(1)}, u32[]{:S(2)}, u32[]{:S(2)}) async-start(bf16[128,2,512]{2,1,0:T(2,128)(2,1)} %reshape.58), calls=%async_computation | async-start | bytes 524288 | tf_op jit(solution)/shard_map/all_to_all | solution.py:31
  41.8 27.2 %copy-start.5 = (s32[128,2]{1,0:T(8,128)}, s32[128,2]{1,0:T(8,128)S(1)}, u32[]{:S(2)}) copy-start(s32[128,2]{1,0:T(8,128)S(1)} %copy.40.dst_ref) | copy-start | bytes 3076
  63.1 1.5 copy-start.1
  69.0 30.8 %all-to-all-start.1 = ((bf16[4,160,512]{2,1,0:T(8,128)(2,1)}), bf16[4,160,512]{2,1,0:T(8,128)(2,1)S(1)}, u32[]{:S(2)}, u32[]{:S(2)}) async-start(bf16[4,160,512]{2,1,0:T(8,128)(2,1)} %get-tuple-element.25), calls=%async_computation.1 | async-start | bytes 1310720 | tf_op jit(solution)/shard_map/all_to_all | solution.py:31
  97.9 29.8 %copy-start.3 = (bf16[1728,512]{1,0:T(8,128)(2,1)S(1)}, bf16[1728,512]{1,0:T(8,128)(2,1)}, u32[]{:S(2)}) copy-start(bf16[1728,512]{1,0:T(8,128)(2,1)} %all-gather.7.cloned.1.call-done) | copy-start | bytes 5308420
  101.9 25.7 %all-to-all-start.2 = ((bf16[128,2,256]{2,1,0:T(2,128)(2,1)}), bf16[128,2,256]{2,1,0:T(2,128)(2,1)S(1)}, u32[]{:S(2)}, u32[]{:S(2)}) async-start(bf16[128,2,256]{2,1,0:T(2,128)(2,1)} %reshape.69), calls=%async_computation.2 | async-start | bytes 262144 | tf_op jit(solution)/shard_map/all_to_all | solution.py:31
  134.0 25.1 %copy-start.12 = (bf16[512,512]{1,0:T(8,128)(2,1)}, bf16[512,512]{1,0:T(8,128)(2,1)S(1)}, u32[]{:S(2)}) copy-start(bf16[512,512]{1,0:T(8,128)(2,1)S(1)} %get-tuple-element.34.proc_term_ref) | copy-start | bytes 1572868
  134.0 28.9 %copy-start.15 = (f32[160,512]{1,0:T(8,128)S(1)}, f32[160,512]{1,0:T(8,128)}, u32[]{:S(2)}) copy-start(f32[160,512]{1,0:T(8,128)} %copy-done.14) | copy-start | bytes 983044
  159.1 16.2 %all-to-all-start.3 = ((bf16[4,208,512]{2,1,0:T(8,128)(2,1)}), bf16[4,208,512]{2,1,0:T(8,128)(2,1)S(1)}, u32[]{:S(2)}, u32[]{:S(2)}) async-start(bf16[4,208,512]{2,1,0:T(8,128)(2,1)} %copy-done.4), calls=%async_computation.3 | async-start | bytes 1703936 | tf_op jit(solution)/shard_map/all_to_all | solution.py:31
  162.8 24.3 %copy-start.6 = (s32[128,2]{1,0:T(8,128)S(1)}, s32[128,2]{1,0:T(8,128)}, u32[]{:S(2)}) copy-start(s32[128,2]{1,0:T(8,128)} %copy-done.5) | copy-start | bytes 3076
  162.8 24.3 %copy-start.9 = (f32[256,512]{1,0:T(8,128)S(1)}, f32[256,512]{1,0:T(8,128)}, u32[]{:S(2)}) copy-start(f32[256,512]{1,0:T(8,128)} %copy-done.8) | copy-start | bytes 1572868
  187.1 1.0 copy-start.11
  188.1 1.0 copy-start.13
  259.1 8.5 %all-to-all-start.6 = ((bf16[4,48,512]{2,1,0:T(8,128)(2,1)}), bf16[4,48,512]{2,1,0:T(8,128)(2,1)S(1)}, u32[]{:S(2)}, u32[]{:S(2)}) async-start(bf16[4,48,512]{2,1,0:T(8,128)(2,1)} %get-tuple-element.36), calls=%async_computation.6 | async-start | bytes 393216 | tf_op jit(solution)/shard_map/all_to_all | solution.py:31
  267.7 16.9 %all-to-all-start.10 = ((bf16[16,2,1536]{2,1,0:T(2,128)(2,1)}), bf16[16,2,1536]{2,1,0:T(2,128)(2,1)S(1)}, u32[]{:S(2)}, u32[]{:S(2)}) async-start(bf16[16,2,1536]{2,1,0:T(2,128)(2,1)} %reshape.75), calls=%async_computation.10 | async-start | bytes 196608 | tf_op jit(solution)/shard_map/all_to_all | solution.py:31
  285.2 29.9 %all-to-all-start.7 = ((bf16[128,2,512]{2,1,0:T(2,128)(2,1)}), bf16[128,2,512]{2,1,0:T(2,128)(2,1)S(1)}, u32[]{:S(2)}, u32[]{:S(2)}) async-start(bf16[128,2,512]{2,1,0:T(2,128)(2,1)} %reshape.62), calls=%async_computation.7 | async-start | bytes 524288 | tf_op jit(solution)/shard_map/all_to_all | solution.py:31
  294.6 29.2 %copy-start.2 = (bf16[1728,512]{1,0:T(8,128)(2,1)S(1)}, bf16[1728,512]{1,0:T(8,128)(2,1)}, u32[]{:S(2)}) copy-start(bf16[1728,512]{1,0:T(8,128)(2,1)} %all-gather.5.cloned.1.call-done) | copy-start | bytes 5308420
  317.0 18.3 %all-to-all-start.11 = ((bf16[8,16,3072]{2,1,0:T(8,128)(2,1)}), bf16[8,16,3072]{2,1,0:T(8,128)(2,1)}, u32[]{:S(2)}, u32[]{:S(2)}) async-start(bf16[8,16,3072]{2,1,0:T(8,128)(2,1)} %broadcast_in_dim.36), calls=%async_computation.11 | async-start | bytes 1572864 | tf_op jit(solution)/shard_map/all_to_all | solution.py:31
  (10 other events, 7.6 us)
Sparse Core Ops, SparseCore 0:
  11.8 41.1 all-gather.4
  55.0 42.8 all-gather.6

commit v2 on v1

v2 whole, which is shorter than its diff:
```python
import functools
import math

import jax
import jax.numpy as jnp
from jax import lax
from jax.experimental import pallas as pl
from jax.experimental.pallas import tpu as pltpu
from jax.sharding import Mesh
from jax.sharding import PartitionSpec as P

DOM = ("z", "x", "c")
ALL = ("z", "x", "c", "y")
EPS = 1e-05
BF = jnp.bfloat16
F32 = jnp.float32
PAD = 16


def call(kernel, outs, *operands, me=None, scratch=()):
    specs = [pl.BlockSpec()] * len(operands)
    if me is not None:
        operands = (me, *operands)
        specs = [pl.BlockSpec(memory_space=pltpu.SMEM), *specs]
    return pl.pallas_call(
        kernel,
        out_shape=tuple(jax.ShapeDtypeStruct(s, d) for s, d in outs),
        in_specs=specs,
        out_specs=tuple(pl.BlockSpec() for _ in outs),
        scratch_shapes=list(scratch),
        compiler_params=pltpu.CompilerParams(vmem_limit_bytes=60 * 1024 * 1024),
    )(*operands)


def onward(blocks):
    n = len(blocks)
    return [blocks[0]] + [
        lax.ppermute(blocks[k], "y", [(i, (i + k) % n) for i in range(n)]) for k in range(1, n)
    ]


def exchange(array, axes):
    return lax.all_to_all(array, axes, 0, 0, tiled=True)


def dot(left, right):
    return jnp.dot(left, right, preferred_element_type=F32)


def dot_t(left, right):
    return lax.dot_general(left, right, (((1,), (1,)), ((), ())), preferred_element_type=F32)


def outer(left, right):
    return lax.dot_general(left, right, (((0,), (0,)), ((), ())), preferred_element_type=F32)


def one_hot(column, count):
    places = lax.broadcasted_iota(jnp.int32, (column.shape[0], count), 1)
    return jnp.where(places == column, 1.0, 0.0).astype(BF)


def slots_hot(indices, count):
    width = indices.shape[1]
    return jnp.concatenate([one_hot(indices[:, c : c + 1], count) for c in range(width)], axis=0)


def slot_rows(wide, width):
    return jnp.concatenate(
        [wide[:, c * width : (c + 1) * width] for c in range(wide.shape[1] // width)], axis=0
    )


def wide_rows(rows, count):
    each = rows.shape[0] // count
    return jnp.concatenate([rows[c * each : (c + 1) * each] for c in range(count)], axis=1)


def whole(ref, at, rows):
    return jnp.concatenate(
        [ref[y, at * rows : (at + 1) * rows, :] for y in range(ref.shape[0])], axis=0
    )


def sigmoid(v):
    return 1.0 / (1.0 + jnp.exp(-v))


def layer_norm(values):
    center = values - jnp.mean(values, axis=-1, keepdims=True)
    spread = jnp.mean(center * center, axis=-1, keepdims=True)
    scaling = lax.rsqrt(spread + EPS)
    return (center * scaling, scaling)


def norm_back(normed, scaling, upstream):
    inner = jnp.mean(upstream, axis=-1, keepdims=True)
    along = jnp.mean(upstream * normed, axis=-1, keepdims=True)
    return scaling * (upstream - inner - normed * along)


def pack_kernel(
    send_ref, grid_ref, src_ref, dst_ref, wg_ref, wm_ref, we_ref, ws_ref, wd_ref, wp_ref, mesh_ref, cot_ref,
    out_ref, enc_ref, proc_ref, line_ref,
):
    grid = grid_ref[...]
    width = grid.shape[1]
    for c in range(send_ref.shape[1]):
        hot = one_hot(send_ref[:, c : c + 1], grid.shape[0])
        out_ref[:, c * width : (c + 1) * width] = dot(hot, grid).astype(BF)
    edges = src_ref.shape[1]
    spare = line_ref.shape[0]
    line_ref[...] = jnp.zeros_like(line_ref)
    place = lax.broadcasted_iota(jnp.int32, (spare, edges), 0)
    source = jnp.broadcast_to(src_ref[...], (spare, edges))
    target = jnp.broadcast_to(dst_ref[...], (spare, edges))
    values = jnp.where(place == 0, source >> 4, jnp.where(place == 1, source & 15, target))
    line_ref[:, :edges] = jnp.where(place < 3, values, 0).astype(F32)
    rows = wg_ref.shape[0]
    for ref, arrays, tail in (
        (enc_ref, (wg_ref, wm_ref, we_ref), mesh_ref),
        (proc_ref, (ws_ref, wd_ref, wp_ref), cot_ref),
    ):
        for k, array in enumerate(arrays):
            ref[k * rows : (k + 1) * rows, :] = array[...]
        both = jnp.concatenate([tail[...].astype(F32), line_ref[...]], axis=0)
        ref[3 * rows :, :] = both.astype(BF)


def node_rows(gath_ref, at, own):
    return jnp.concatenate(
        [gath_ref[y, at:, :].astype(F32)[:own] for y in range(gath_ref.shape[0])], axis=0
    )


def own_column(ref, me):
    table = ref[...]
    column = lax.broadcasted_iota(jnp.int32, table.shape, 1)
    return jnp.sum(jnp.where(column == me, table, 0), axis=1, keepdims=True)


def total_of(refs):
    total = refs[0].astype(F32)
    for block in refs[1:]:
        total = total + block.astype(F32)
    return total


def encode_kernel(rows, own, recv_ref, dst_ref, gath_ref, sum_ref, pre_ref, norm_ref, scale_ref):
    width = gath_ref.shape[2]
    mesh_part = node_rows(gath_ref, 3 * rows, own).astype(BF)
    received = slot_rows(recv_ref[...], width)
    hot = slots_hot(dst_ref[...], mesh_part.shape[0])
    projected = dot(received, whole(gath_ref, 0, rows)).astype(BF)
    nodes = dot(hot, mesh_part).astype(BF)
    preact = projected.astype(F32) + dot(nodes, whole(gath_ref, 1, rows))
    pre_ref[...] = preact
    hidden = (preact * sigmoid(preact)).astype(BF)
    normed, scaling = layer_norm(dot(hidden, whole(gath_ref, 2, rows)))
    norm_ref[...] = normed
    scale_ref[...] = scaling
    partial_sum = outer(hot, normed.astype(BF)).astype(BF)
    for y in range(sum_ref.shape[0]):
        sum_ref[y] = partial_sum


def latent_kernel(rows, own, me_ref, sums_ref, gath_ref, send_ref, latent_ref, halo_ref):
    total = total_of([sums_ref[y] for y in range(sums_ref.shape[0])])
    latent = (node_rows(gath_ref, 3 * rows, own) + total).astype(BF)
    latent_ref[...] = latent
    hot = one_hot(own_column(send_ref, me_ref[0]), latent.shape[0])
    halo_ref[...] = dot(hot, latent).astype(BF)


def deal(me, refs, term_ref, rows, node_ref, own):
    count = len(refs)
    width = refs[0].shape[1]
    terms = term_ref.shape[1] // width
    spare = refs[0].shape[0] - terms * rows - own
    for k, ref in enumerate(refs):
        to = lax.rem(me + k, count)
        at = pl.ds(pl.multiple_of(to * rows, rows), rows)
        for t in range(terms):
            ref[t * rows : (t + 1) * rows, :] = term_ref[at, t * width : (t + 1) * width]
        block = node_ref[pl.ds(pl.multiple_of(to * own, 8), own), :]
        block = jnp.concatenate([block, jnp.zeros((spare, width), F32)], axis=0)
        ref[terms * rows :, :] = block.astype(BF)


def process_kernel(
    rows, own, me_ref, latent_ref, halo_ref, edge_ref, gath_ref,
    back_ref, local_ref, dst_ref, b0_ref, b1_ref, b2_ref, b3_ref, term_ref, node_ref,
):
    latent = latent_ref[...]
    table = jnp.concatenate([latent, halo_ref[...]], axis=0)
    nodes, width = latent.shape
    hot_src = one_hot(edge_ref[:, 0:1], table.shape[0])
    hot_dst = one_hot(edge_ref[:, 1:2], nodes)
    w_src, w_dst, w_out = [whole(gath_ref, k, rows) for k in range(3)]
    src_rows = dot(hot_src, table).astype(BF)
    dst_rows = dot(hot_dst, latent).astype(BF)
    preact = dot(src_rows, w_src) + dot(dst_rows, w_dst)
    gate = sigmoid(preact)
    hidden = (preact * gate).astype(BF)
    normed, scaling = layer_norm(dot(hidden, w_out))
    node_ref[...] = outer(hot_dst, normed.astype(BF))
    upstream = dot(hot_dst, node_rows(gath_ref, 3 * rows, own).astype(BF))
    mid = norm_back(normed, scaling, upstream).astype(BF)
    grad = (dot_t(mid, w_out) * (gate * (1.0 + preact * (1.0 - gate)))).astype(BF)
    at_dst = outer(hot_dst, grad).astype(BF)
    dst_ref[...] = at_dst
    at_src = outer(hot_src, grad)
    local_ref[...] = at_src[:nodes]
    back_ref[...] = at_src[nodes:].astype(BF)
    term_ref[:, :width] = outer(latent, at_dst).astype(BF)
    term_ref[:, width:] = outer(hidden, mid).astype(BF)
    deal(me_ref[0], (b0_ref, b1_ref, b2_ref, b3_ref), term_ref, rows, node_ref, own)


def owner_kernel(rows, me_ref, back_ref, send_ref, local_ref, dst_ref, gath_ref, out_ref, src_ref):
    hot = one_hot(own_column(send_ref, me_ref[0]), local_ref.shape[0])
    at_src = (local_ref[...] + outer(hot, back_ref[...])).astype(BF)
    src_ref[...] = at_src
    total = dot_t(at_src, whole(gath_ref, 0, rows)) + dot_t(dst_ref[...], whole(gath_ref, 1, rows))
    total = total.astype(BF)
    for y in range(out_ref.shape[0]):
        out_ref[y] = total


def backward_kernel(
    rows, own, me_ref, node_in_ref, proc_ref, latent_ref, src_ref, enc_ref, recv_ref, dst_ref,
    pre_ref, norm_ref, scale_ref,
    node_ref, slot_ref, b0_ref, b1_ref, b2_ref, b3_ref, term_ref, share_ref,
):
    nodes, width = latent_ref.shape
    node_grad = node_rows(proc_ref, 3 * rows, own) + total_of(
        [node_in_ref[y] for y in range(node_in_ref.shape[0])]
    )
    node_ref[...] = node_grad
    hot = slots_hot(dst_ref[...], nodes)
    upstream = dot(hot, node_grad.astype(BF))
    mid = norm_back(norm_ref[...], scale_ref[...], upstream).astype(BF)
    preact = pre_ref[...]
    gate = sigmoid(preact)
    hidden = (preact * gate).astype(BF)
    grad = dot_t(mid, whole(enc_ref, 2, rows)) * (gate * (1.0 + preact * (1.0 - gate)))
    grad = grad.astype(BF)
    slot_ref[...] = wide_rows(grad, recv_ref.shape[1] // width)
    at_node = outer(hot, grad)
    share_ref[...] = at_node
    terms = (
        outer(slot_rows(recv_ref[...], width), grad),
        outer(node_rows(enc_ref, 3 * rows, own).astype(BF), at_node.astype(BF)),
        outer(hidden, mid),
        outer(latent_ref[...], src_ref[...]),
    )
    for k, term in enumerate(terms):
        term_ref[:, k * width : (k + 1) * width] = term.astype(BF)
    deal(me_ref[0], (b0_ref, b1_ref, b2_ref, b3_ref), term_ref, rows, share_ref, own)


def grid_kernel(rows, back_ref, send_ref, enc_ref, out_ref):
    nodes, width = out_ref.shape
    grads = dot_t(slot_rows(back_ref[...], width), whole(enc_ref, 0, rows)).astype(BF)
    out_ref[...] = outer(slots_hot(send_ref[...], nodes), grads).astype(BF)


def out_kernel(rows, me_ref, latent_ref, b0_ref, b1_ref, b2_ref, b3_ref, out_ref, sum_ref):
    total = total_of([b0_ref[...], b1_ref[...], b2_ref[...], b3_ref[...]])
    sum_ref[...] = total[: 2 * rows].astype(BF)
    own, nodes = out_ref.shape[0], latent_ref.shape[0]
    mine = lax.broadcasted_iota(jnp.int32, (own, 1), 0) + me_ref[0] * own
    latent = dot(one_hot(mine, nodes), latent_ref[...])
    out_ref[...] = (latent + total[2 * rows : 2 * rows + own]).astype(BF)


def mesh_kernel(
    rows, me_ref, sum_ref, node_ref, enc_ref, b0_ref, b1_ref, b2_ref, b3_ref, mesh_ref, pay_ref
):
    total = total_of([b0_ref[...], b1_ref[...], b2_ref[...], b3_ref[...]])
    own, width = mesh_ref.shape
    for k in range(4):
        pay_ref[:, k * width : (k + 1) * width] = total[k * rows : (k + 1) * rows].astype(BF)
    pay_ref[:, 4 * width : 5 * width] = sum_ref[:rows, :]
    pay_ref[:, 5 * width :] = sum_ref[rows:, :]
    back = dot_t(total[4 * rows :].astype(BF), whole(enc_ref, 1, rows))[:own]
    node = node_ref[pl.ds(pl.multiple_of(me_ref[0] * own, 8), own), :]
    mesh_ref[...] = (node + back).astype(BF)


def sum_kernel(in_ref, out_ref):
    out_ref[...] = total_of([in_ref[k] for k in range(in_ref.shape[0])]).astype(out_ref.dtype)


def split_kernel(factor, in_ref, *out_refs):
    count, thin, _ = in_ref.shape
    width = out_refs[0].shape[1]
    for r in range(count):
        for k, ref in enumerate(out_refs):
            block = in_ref[r, :, k * width : (k + 1) * width]
            ref[r * thin : (r + 1) * thin, :] = block.astype(F32) * factor


def per_device(
    grid_feat,
    mesh_feat,
    w_grid,
    w_mesh,
    w_enc2,
    w_src,
    w_dst,
    w_proc2,
    enc_send,
    enc_dst,
    hal_send,
    proc_src,
    proc_dst,
    cotangent,
):
    dom = lax.axis_size(DOM)
    feat = lax.axis_size("y")
    deep = lax.axis_size("z")
    own, width = mesh_feat.shape
    nodes = own * feat
    rows = w_grid.shape[0]
    caps = enc_send.shape[1]
    halo = hal_send.shape[1]
    edges = proc_src.shape[0]
    held = own + (-own % PAD)
    factor = 1.0 / math.sqrt(own * dom * feat)
    index = lax.axis_index("y")
    me = index.reshape(1)
    if halo != feat or held - own < 8 or edges > width:
        raise ValueError("sizes")
    bind = functools.partial

    packed = ((3 * rows + held, width), BF)
    outgoing, enc_pack, proc_pack = call(
        pack_kernel,
        [((dom, caps * width), BF), packed, packed],
        enc_send,
        grid_feat,
        proc_src.reshape(1, edges),
        proc_dst.reshape(1, edges),
        w_grid,
        w_mesh,
        w_enc2,
        w_src,
        w_dst,
        w_proc2,
        mesh_feat,
        cotangent,
        scratch=[pltpu.VMEM((held - own, width), F32)],
    )
    received = exchange(outgoing.reshape(dom, caps, width), DOM).reshape(dom, caps * width)
    enc_gath = lax.all_gather(enc_pack, "y", axis=0)
    proc_gath = lax.all_gather(proc_pack, "y", axis=0)

    slots = dom * caps
    partial_sum, preact, normed, scaling = call(
        bind(encode_kernel, rows, own),
        [((feat, nodes, width), BF), ((slots, width), F32), ((slots, width), F32), ((slots, 1), F32)],
        received,
        enc_dst,
        enc_gath,
    )
    sums = exchange(partial_sum, "y")
    latent, halo_out = call(
        bind(latent_kernel, rows, own),
        [((nodes, width), BF), ((dom, width), BF)],
        sums,
        enc_gath,
        hal_send,
        me=me,
    )
    halo_rows = exchange(halo_out, DOM)

    lines = enc_gath[:, 3 * rows + own : 3 * rows + own + 3, :edges].astype(jnp.int32)
    source = lines[:, 0] * 16 + lines[:, 1]
    slot = source - nodes
    place = jnp.where(slot < 0, source, nodes + slot // halo)
    keeper = jnp.where(slot < 0, jnp.arange(feat, dtype=jnp.int32)[:, None], slot % halo)
    mine = keeper == index
    edge_index = jnp.stack(
        [jnp.where(mine, place, -1).reshape(-1), jnp.where(mine, lines[:, 2], -1).reshape(-1)], axis=1
    )
    blocks = [((2 * rows + held, width), BF)] * 4
    halo_back, at_local, at_dst, *first = call(
        bind(process_kernel, rows, own),
        [((dom, width), BF), ((nodes, width), F32), ((nodes, width), BF)] + blocks,
        latent,
        halo_rows,
        edge_index,
        proc_gath,
        me=me,
        scratch=[pltpu.VMEM((width, 2 * width), BF), pltpu.VMEM((nodes, width), F32)],
    )
    returned = exchange(halo_back, DOM)
    returned, *first = lax.optimization_barrier((returned, *onward(first)))
    node_part, at_src = call(
        bind(owner_kernel, rows),
        [((feat, nodes, width), BF), ((nodes, width), BF)],
        returned,
        hal_send,
        at_local,
        at_dst,
        proc_gath,
        me=me,
    )
    node_in = exchange(node_part, "y")

    blocks = [((4 * rows + held, width), BF)] * 4
    node_grad, slot_out, *second = call(
        bind(backward_kernel, rows, own),
        [((nodes, width), F32), ((dom, caps * width), BF)] + blocks,
        node_in,
        proc_gath,
        latent,
        at_src,
        enc_gath,
        received,
        enc_dst,
        preact,
        normed,
        scaling,
        me=me,
        scratch=[pltpu.VMEM((width, 4 * width), BF), pltpu.VMEM((nodes, width), F32)],
    )
    slot_back = exchange(slot_out.reshape(dom, caps, width), DOM).reshape(dom, caps * width)
    slot_back, *second = lax.optimization_barrier((slot_back, *onward(second)))
    out_rows, first_sum = call(
        bind(out_kernel, rows), [((own, width), BF), ((2 * rows, width), BF)], latent, *first, me=me
    )
    g_mesh, level = call(
        bind(mesh_kernel, rows),
        [((own, width), BF), ((rows, 6 * width), BF)],
        first_sum,
        node_grad,
        enc_gath,
        *second,
        me=me,
    )
    near = lax.axis_size(("x", "c"))
    thin = rows // near
    level = exchange(level.reshape(near, thin, 6 * width), ("x", "c"))
    (level,) = call(sum_kernel, [((thin, 6 * width), BF)], level)
    level = exchange(level.reshape(deep, thin // deep, 6 * width), "z")
    mine_sum = level.astype(F32).sum(axis=0).astype(BF)
    level = exchange(jnp.broadcast_to(mine_sum[None], (deep, *mine_sum.shape)), "z")
    level = level.reshape(thin, 6 * width)
    totals = exchange(jnp.broadcast_to(level[None], (near, *level.shape)), ("x", "c"))
    totals = call(bind(split_kernel, factor), [((rows, width), F32)] * 6, totals)
    (g_grid,) = call(
        bind(grid_kernel, rows), [(grid_feat.shape, BF)], slot_back, enc_send, enc_gath
    )
    return (out_rows, g_grid, g_mesh) + tuple(totals)


def solution(mesh):
    dom, feat = mesh.shape["dom"], mesh.shape["feat"]
    x = 4 if dom % 8 == 0 else 1
    finer = Mesh(mesh.devices.reshape(dom // (2 * x), x, 2, feat), ALL)
    return jax.shard_map(
        per_device,
        mesh=finer,
        in_specs=(
            P(ALL, None),
            P(ALL, None),
            P("y", None),
            P("y", None),
            P("y", None),
            P("y", None),
            P("y", None),
            P("y", None),
            P(ALL, None),
            P(ALL, None),
            P(DOM, None),
            P(ALL),
            P(ALL),
            P(ALL, None),
        ),
        out_specs=(
            P(ALL, None),
            P(ALL, None),
            P(ALL, None),
            P("y", None),
            P("y", None),
            P("y", None),
            P("y", None),
            P("y", None),
            P("y", None),
        ),
        check_vma=False,
    )
```

time: 346 us -> 322 us (0.931)
  waiting for transfers between devices: 114 us -> 85 us
  starting transfers between devices: 61.7 us -> 87.3 us
  blocking collectives: 96.7 us -> 72.4 us
  Pallas kernels: 15.4 us -> 38.6 us
  local copies, waits for them, and re-layouts: 34.1 us -> 16.7 us
    all_gather x2, waiting for transfers between devices: 24.7 us -> 0.01 us  [the longest x1 0.01 us: per_device(): enc_gath = lax.all_gather(enc_pack, 'y', axis=0)]
    all_to_all x4, blocking collectives: 96.7 us -> 72.4 us  [exchange(): return lax.all_to_all(array, axes, 0, 0, tiled=True)]
    pallas_call x9 -> x11, Pallas kernels: 15.4 us -> 38.6 us  [call(): pl.pallas_call(kernel, out_shape=tuple((jax.ShapeDtypeStruct(s, d) for s,...]
    all_to_all x8 -> x6, waiting for transfers between devices: 89.5 us -> 69.4 us  [exchange(): return lax.all_to_all(array, axes, 0, 0, tiled=True)]
    ppermute x0 -> x6, starting transfers between devices: none -> 17.3 us  [onward(): lax.ppermute(blocks[k], 'y', [(i, (i + k) % n) for i in range(n)])]
    ppermute x0 -> x6, waiting for transfers between devices: none -> 14.9 us  [onward(): lax.ppermute(blocks[k], 'y', [(i, (i + k) % n) for i in range(n)])]
    unnamed x69 -> x36, local copies, waits for them, and re-layouts: 18.7 us -> 10.2 us
    all_to_all x8 -> x6, starting transfers between devices: 61.6 us -> 69.9 us  [exchange(): return lax.all_to_all(array, axes, 0, 0, tiled=True)]
  transfers between devices with their start and end apart: 10 -> 14, of which waited for: 8 -> 10; matrix products, arithmetic and copies ran while one was open for 5% -> 3% of each run, Pallas kernels for 1% -> 4%
where the time goes in v2:
time: 322 us; the launch traced here: 321 us
  starting transfers between devices  87.3 us (27%)
  waiting for transfers between devices  85 us (26%)
  blocking collectives  72.4 us (22%)
  Pallas kernels  38.6 us (12%)
  local copies, waits for them, and re-layouts  16.7 us (5%)
  between operations  14.3 us (4%)
  other arithmetic  6.76 us (2%)
    all_to_all x4, blocking collectives, exchange(): return lax.all_to_all(array, axes, 0, 0, tiled=True)  72.4 us
    all_to_all x6, starting transfers between devices, exchange(): return lax.all_to_all(array, axes, 0, 0, tiled=True)  69.9 us
    all_to_all x6, waiting for transfers between devices, exchange(): return lax.all_to_all(array, axes, 0, 0, tiled=True)  69.4 us
    pallas_call x11, Pallas kernels, call(): pl.pallas_call(kernel, out_shape=tuple((jax.ShapeDtypeStruct(s, d) for s,...  38.6 us
    ppermute x6, starting transfers between devices, onward(): lax.ppermute(blocks[k], 'y', [(i, (i + k) % n) for i in range(n)])  17.3 us
    ppermute x6, waiting for transfers between devices, onward(): lax.ppermute(blocks[k], 'y', [(i, (i + k) % n) for i in range(n)])  14.9 us
    unnamed x36, local copies, waits for them, and re-layouts  10.2 us
  transfers between devices with their start and end apart: 14, of which 10 were waited for; matrix products, arithmetic and copies ran while one was open for 3% of the time, Pallas kernels for 4%

profile of v2, /device:TPU:1, one launch (start us, length us, event | category | flops | bytes accessed | tf_op | source)
XLA Modules:
  0.0 320.9 jit_solution(3042887105585689703)
XLA Ops:
  13.9 20.4 %all-to-all-start = ((bf16[128,2,512]{2,1,0:T(2,128)(2,1)}), bf16[128,2,512]{2,1,0:T(2,128)(2,1)S(1)}, u32[]{:S(2)}, u32[]{:S(2)}) async-start(bf16[128,2,512]{2,1,0:T(2,128)(2,1)} %reshape.196), calls=%async_computation | async-start | bytes 524288 | tf_op jit(solution)/shard_map/all_to_all | solution.py:43
  35.0 19.7 %all-to-all-done = bf16[128,2,512]{2,1,0:T(2,128)(2,1)S(1)} async-done(((bf16[128,2,512]{2,1,0:T(2,128)(2,1)}), bf16[128,2,512]{2,1,0:T(2,128)(2,1)S(1)}, u32[]{:S(2)}, u32[]{:S(2)}) %all-to-all-start) | async-done | bytes 262176 | tf_op jit(solution)/shard_map/all_to_all | solution.py:43
  55.5 3.7 %shard_map.206 = (bf16[4,160,512]{2,1,0:T(8,128)(2,1)}, f32[256,512]{1,0:T(8,128)}, f32[256,512]{1,0:T(8,128)}, f32[256,1]{1,0:T(8,128)}) custom-call(bf16[128,1024]{1,0:T(8,128)(2,1)} %bitcast.31, s32[128,2]{1,0:T(8,128)} %copy.53.dst_ref, bf16[4,432,512]{2,1,0:T(8,128)(2,1)} %bitcast.22), custom_call_target="tpu_custom_call" | custom-call | tf_op jit(solution)/shard_map/pallas_call | solution.py:25
  59.2 4.2 %all-to-all-start.1 = ((bf16[4,160,512]{2,1,0:T(8,128)(2,1)}), bf16[4,160,512]{2,1,0:T(8,128)(2,1)S(1)}, u32[]{:S(2)}, u32[]{:S(2)}) async-start(bf16[4,160,512]{2,1,0:T(8,128)(2,1)} %get-tuple-element.55), calls=%async_computation.1 | async-start | bytes 1310720 | tf_op jit(solution)/shard_map/all_to_all | solution.py:43
  65.2 8.4 %all-to-all-done.1.sums_ref = bf16[4,160,512]{2,1,0:T(8,128)(2,1)S(1)} async-done(((bf16[4,160,512]{2,1,0:T(8,128)(2,1)}), bf16[4,160,512]{2,1,0:T(8,128)(2,1)S(1)}, u32[]{:S(2)}, u32[]{:S(2)}) %all-to-all-start.1) | async-done | bytes 655392 | tf_op jit(solution)/shard_map/all_to_all | solution.py:43
  79.7 14.1 %all-to-all-start.2 = ((bf16[128,2,256]{2,1,0:T(2,128)(2,1)}), bf16[128,2,256]{2,1,0:T(2,128)(2,1)S(1)}, u32[]{:S(2)}, u32[]{:S(2)}) async-start(bf16[128,2,256]{2,1,0:T(2,128)(2,1)} %reshape.206), calls=%async_computation.2 | async-start | bytes 262144 | tf_op jit(solution)/shard_map/all_to_all | solution.py:43
  94.8 15.1 %all-to-all-done.2 = bf16[128,2,256]{2,1,0:T(2,128)(2,1)S(1)} async-done(((bf16[128,2,256]{2,1,0:T(2,128)(2,1)}), bf16[128,2,256]{2,1,0:T(2,128)(2,1)S(1)}, u32[]{:S(2)}, u32[]{:S(2)}) %all-to-all-start.2) | async-done | bytes 131104 | tf_op jit(solution)/shard_map/all_to_all | solution.py:43
  110.6 7.0 %shard_map.208 = (bf16[128,512]{1,0:T(8,128)(2,1)}, f32[160,512]{1,0:T(8,128)}, bf16[160,512]{1,0:T(8,128)(2,1)}, bf16[304,512]{1,0:T(8,128)(2,1)}, bf16[304,512...) custom-call(s32[1]{0:T(128)} %bitcast.me_ref, bf16[160,512]{1,0:T(8,128)(2,1)} %get-tuple-element.56.latent_ref, ...), custom_call_target="tpu_custom_call" | custom-call | tf_op jit(solution)/shard_map/pallas_call | solution.py:25
  119.9 7.2 %all-to-all-start.3 = ((bf16[128,2,256]{2,1,0:T(2,128)(2,1)}), bf16[128,2,256]{2,1,0:T(2,128)(2,1)S(1)}, u32[]{:S(2)}, u32[]{:S(2)}) async-start(bf16[128,2,256]{2,1,0:T(2,128)(2,1)} %reshape.208), calls=%async_computation.3 | async-start | bytes 262144 | tf_op jit(solution)/shard_map/all_to_all | solution.py:43
  129.3 3.7 %collective-permute-start.1 = (bf16[304,512]{1,0:T(8,128)(2,1)}, bf16[304,512]{1,0:T(8,128)(2,1)S(1)}, u32[]{:S(2)}, u32[]{:S(2)}) collective-permute-start(bf16[304,512]{1,0:T(8,128)(2,1)} %get-tuple-element.62), channel_id=1, source_target_pairs={{0,2},{1,3},{2,0},{3,1},{4,6},{5,7},{6,4},{7,5},{8,10},{9,11},{10,... | collective-permute-start | bytes 933896 | tf_op jit(solution)/shard_map/ppermute | solution.py:38
  135.7 7.4 %all-to-all-done.3 = bf16[128,2,256]{2,1,0:T(2,128)(2,1)S(1)} async-done(((bf16[128,2,256]{2,1,0:T(2,128)(2,1)}), bf16[128,2,256]{2,1,0:T(2,128)(2,1)S(1)}, u32[]{:S(2)}, u32[]{:S(2)}) %all-to-all-start.3) | async-done | bytes 131104 | tf_op jit(solution)/shard_map/all_to_all | solution.py:43
  151.3 14.6 %all_to_all.63.node_in_ref = bf16[4,160,512]{2,1,0:T(8,128)(2,1)} all-to-all(bf16[4,160,512]{2,1,0:T(8,128)(2,1)} %get-tuple-element.72), channel_id=1, replica_groups=mesh['z'=16,'x'=4,'c'=2,'y'=4] {'y'}, dimensions={0} | all-to-all | bytes 1310720 | tf_op jit(solution)/shard_map/all_to_all | solution.py:43
  165.9 5.9 %shard_map.211 = (f32[160,512]{1,0:T(8,128)}, bf16[128,1024]{1,0:T(8,128)(2,1)}, bf16[560,512]{1,0:T(8,128)(2,1)}, bf16[560,512]{1,0:T(8,128)(2,1)}, bf16[560,512]{1,0:T(8,128)(2,1)}, /*index=5*/bf16[560,512]{1,0:T(8,128)(2,1)}) custom-call(s32[1]{0:T(128)} %bitcast.me_ref, bf16[4,160,512]{2,1,0:T(8,128)(2,1)} %all_to_all.63.node_in_ref, ...), custom_call_target="tpu_custom_call" | custom-call | tf_op jit(solution)/shard_map/pallas_call | solution.py:25
  173.6 17.6 %all-to-all-start.5 = ((bf16[128,2,512]{2,1,0:T(2,128)(2,1)}), bf16[128,2,512]{2,1,0:T(2,128)(2,1)S(1)}, u32[]{:S(2)}, u32[]{:S(2)}) async-start(bf16[128,2,512]{2,1,0:T(2,128)(2,1)} %reshape.198), calls=%async_computation.5 | async-start | bytes 524288 | tf_op jit(solution)/shard_map/all_to_all | solution.py:43
  193.7 3.5 %collective-permute-start.4 = (bf16[560,512]{1,0:T(8,128)(2,1)}, bf16[560,512]{1,0:T(8,128)(2,1)S(1)}, u32[]{:S(2)}, u32[]{:S(2)}) collective-permute-start(bf16[560,512]{1,0:T(8,128)(2,1)} %get-tuple-element.80), channel_id=1, source_target_pairs={{0,2},{1,3},{2,0},{3,1},{4,6},{5,7},{6,4},{7,5},{8,10},{9,11},{10,... | collective-permute-start | bytes 1720328 | tf_op jit(solution)/shard_map/ppermute | solution.py:38
  202.2 9.5 %all-to-all-done.5 = bf16[128,2,512]{2,1,0:T(2,128)(2,1)S(1)} async-done(((bf16[128,2,512]{2,1,0:T(2,128)(2,1)}), bf16[128,2,512]{2,1,0:T(2,128)(2,1)S(1)}, u32[]{:S(2)}, u32[]{:S(2)}) %all-to-all-start.5) | async-done | bytes 262176 | tf_op jit(solution)/shard_map/all_to_all | solution.py:43
  212.5 7.4 %collective-permute-done.4.b2_ref = bf16[560,512]{1,0:T(8,128)(2,1)S(1)} collective-permute-done((bf16[560,512]{1,0:T(8,128)(2,1)}, bf16[560,512]{1,0:T(8,128)(2,1)S(1)}, u32[]{:S(2)}, u32[]{:S(2)}) %collective-permute-start.4) | collective-permute-done | bytes 573472 | tf_op jit(solution)/shard_map/ppermute | solution.py:38
  219.9 3.4 %collective-permute-done.5.b3_ref = bf16[560,512]{1,0:T(8,128)(2,1)S(1)} collective-permute-done((bf16[560,512]{1,0:T(8,128)(2,1)}, bf16[560,512]{1,0:T(8,128)(2,1)S(1)}, u32[]{:S(2)}, u32[]{:S(2)}) %collective-permute-start.5) | collective-permute-done | bytes 573472 | tf_op jit(solution)/shard_map/ppermute | solution.py:38
  224.2 3.9 %shard_map.213 = (bf16[40,512]{1,0:T(8,128)(2,1)}, bf16[128,3072]{1,0:T(8,128)(2,1)}) custom-call(s32[1]{0:T(128)} %bitcast.me_ref, bf16[256,512]{1,0:T(8,128)(2,1)} %get-tuple-element.83.sum_ref, f32[160,512]{1,0:T(8,128)} %get-tuple-element.84.node_ref, bf16[4,432,512]{2,1,0:T(8,128)(2,1)} %bitcast.26, bf16[560,512]{1,0:T(8,128)(2,1)} %get-tuple-element.85.b0_ref, ...), custom_call_target="tpu_custom_call" | custom-call | tf_op jit(solution)/shard_map/pallas_call | solution.py:25
  228.1 18.2 %all_to_all.64.in_ref = bf16[8,16,3072]{2,1,0:T(8,128)(2,1)} all-to-all(bf16[8,16,3072]{2,1,0:T(8,128)(2,1)} %bitcast.36), channel_id=1, replica_groups=mesh['z'=16,'x'=4,'c'=2,'y'=4] {'x','c'}, dimensions={0} | all-to-all | bytes 1572864 | tf_op jit(solution)/shard_map/all_to_all | solution.py:43
  249.8 23.3 %all_to_all.65 = bf16[16,2,1536]{2,1,0:T(2,128)(2,1)S(1)} all-to-all(bf16[16,2,1536]{2,1,0:T(2,128)(2,1)S(1)} %reshape.210), channel_id=1, replica_groups=mesh['z'=16,'x'=4,'c'=2,'y'=4] {'z'}, dimensions={0} | all-to-all | bytes 196608 | tf_op jit(solution)/shard_map/all_to_all | solution.py:43
  274.7 16.3 %all_to_all.66 = bf16[16,2,1536]{2,1,0:T(2,128)(2,1)S(1)} all-to-all(bf16[16,2,1536]{2,1,0:T(2,128)(2,1)S(1)} %reshape.212), channel_id=1, replica_groups=mesh['z'=16,'x'=4,'c'=2,'y'=4] {'z'}, dimensions={0} | all-to-all | bytes 196608 | tf_op jit(solution)/shard_map/all_to_all | solution.py:43
  292.0 6.5 %all-to-all-start.9 = ((bf16[8,16,3072]{2,1,0:T(8,128)(2,1)}), bf16[8,16,3072]{2,1,0:T(8,128)(2,1)S(1)}, u32[]{:S(2)}, u32[]{:S(2)}) async-start(bf16[8,16,3072]{2,1,0:T(8,128)(2,1)} %broadcast_in_dim.31), calls=%async_computation.9 | async-start | bytes 1572864 | tf_op jit(solution)/shard_map/all_to_all | solution.py:43
  301.5 9.3 %all-to-all-done.9.in_ref = bf16[8,16,3072]{2,1,0:T(8,128)(2,1)S(1)} async-done(((bf16[8,16,3072]{2,1,0:T(8,128)(2,1)}), bf16[8,16,3072]{2,1,0:T(8,128)(2,1)S(1)}, u32[]{:S(2)}, u32[]{:S(2)}) %all-to-all-start.9) | async-done | bytes 786464 | tf_op jit(solution)/shard_map/all_to_all | solution.py:43
  (77 shorter events, 56.4 us)
Async XLA Ops:
  7.2 27.1 %copy-start.9 = (s32[128,2]{0,1:T(2,128)S(1)}, s32[128,2]{0,1:T(2,128)}, u32[]{:S(2)}) copy-start(s32[128,2]{0,1:T(2,128)} %param.23) | copy-start | bytes 3076
  7.2 48.3 %all-gather.5.cloned.1.call-start = ((), (), s32[]{:S(2)}) async-start(), calls=%async_computation.10 | async-start | bytes 2211840 | tf_op jit(solution)/shard_map/all_gather | solution.py:356
  11.3 99.4 %all-gather.7.cloned.1.call-start = ((), (), s32[]{:S(2)}) async-start(), calls=%async_computation.11 | async-start | bytes 2211840 | tf_op jit(solution)/shard_map/all_gather | solution.py:357
  13.9 40.9 %all-to-all-start = ((bf16[128,2,512]{2,1,0:T(2,128)(2,1)}), bf16[128,2,512]{2,1,0:T(2,128)(2,1)S(1)}, u32[]{:S(2)}, u32[]{:S(2)}) async-start(bf16[128,2,512]{2,1,0:T(2,128)(2,1)} %reshape.196), calls=%async_computation | async-start | bytes 524288 | tf_op jit(solution)/shard_map/all_to_all | solution.py:43
  55.5 8.0 %copy-start.8 = (s32[128,4]{0,1:T(4,128)S(1)}, s32[128,4]{0,1:T(4,128)}, u32[]{:S(2)}) copy-start(s32[128,4]{0,1:T(4,128)} %param.24) | copy-start | bytes 6148
  59.2 14.3 %all-to-all-start.1 = ((bf16[4,160,512]{2,1,0:T(8,128)(2,1)}), bf16[4,160,512]{2,1,0:T(8,128)(2,1)S(1)}, u32[]{:S(2)}, u32[]{:S(2)}) async-start(bf16[4,160,512]{2,1,0:T(8,128)(2,1)} %get-tuple-element.55), calls=%async_computation.1 | async-start | bytes 1310720 | tf_op jit(solution)/shard_map/all_to_all | solution.py:43
  73.5 0.8 copy-start.1
  79.7 30.1 %all-to-all-start.2 = ((bf16[128,2,256]{2,1,0:T(2,128)(2,1)}), bf16[128,2,256]{2,1,0:T(2,128)(2,1)S(1)}, u32[]{:S(2)}, u32[]{:S(2)}) async-start(bf16[128,2,256]{2,1,0:T(2,128)(2,1)} %reshape.206), calls=%async_computation.2 | async-start | bytes 262144 | tf_op jit(solution)/shard_map/all_to_all | solution.py:43
  119.9 23.2 %all-to-all-start.3 = ((bf16[128,2,256]{2,1,0:T(2,128)(2,1)}), bf16[128,2,256]{2,1,0:T(2,128)(2,1)S(1)}, u32[]{:S(2)}, u32[]{:S(2)}) async-start(bf16[128,2,256]{2,1,0:T(2,128)(2,1)} %reshape.208), calls=%async_computation.3 | async-start | bytes 262144 | tf_op jit(solution)/shard_map/all_to_all | solution.py:43
  127.0 16.8 %collective-permute-start = (bf16[304,512]{1,0:T(8,128)(2,1)}, bf16[304,512]{1,0:T(8,128)(2,1)S(1)}, u32[]{:S(2)}, u32[]{:S(2)}) collective-permute-start(bf16[304,512]{1,0:T(8,128)(2,1)} %get-tuple-element.61), channel_id=1, source_target_pairs={{0,1},{1,2},{2,3},{3,0},{4,5},{5,6},{6,7},{7,4},{8,9},{9,10},{10,1... | collective-permute-start | bytes 933896 | tf_op jit(solution)/shard_map/ppermute | solution.py:38
  129.3 15.2 %collective-permute-start.1 = (bf16[304,512]{1,0:T(8,128)(2,1)}, bf16[304,512]{1,0:T(8,128)(2,1)S(1)}, u32[]{:S(2)}, u32[]{:S(2)}) collective-permute-start(bf16[304,512]{1,0:T(8,128)(2,1)} %get-tuple-element.62), channel_id=1, source_target_pairs={{0,2},{1,3},{2,0},{3,1},{4,6},{5,7},{6,4},{7,5},{8,10},{9,11},{10,... | collective-permute-start | bytes 933896 | tf_op jit(solution)/shard_map/ppermute | solution.py:38
  133.0 14.9 %collective-permute-start.2 = (bf16[304,512]{1,0:T(8,128)(2,1)}, bf16[304,512]{1,0:T(8,128)(2,1)S(1)}, u32[]{:S(2)}, u32[]{:S(2)}) collective-permute-start(bf16[304,512]{1,0:T(8,128)(2,1)} %get-tuple-element.63), channel_id=1, source_target_pairs={{0,3},{1,0},{2,1},{3,2},{4,7},{5,4},{6,5},{7,6},{8,11},{9,8},{10,9... | collective-permute-start | bytes 933896 | tf_op jit(solution)/shard_map/ppermute | solution.py:38
  143.9 22.0 %copy-start.5 = (bf16[304,512]{1,0:T(8,128)(2,1)}, bf16[304,512]{1,0:T(8,128)(2,1)S(1)}, u32[]{:S(2)}) copy-start(bf16[304,512]{1,0:T(8,128)(2,1)S(1)} %collective-permute-done.b1_ref) | copy-start | bytes 933892
  144.4 21.4 %copy-start.6 = (bf16[304,512]{1,0:T(8,128)(2,1)}, bf16[304,512]{1,0:T(8,128)(2,1)S(1)}, u32[]{:S(2)}) copy-start(bf16[304,512]{1,0:T(8,128)(2,1)S(1)} %collective-permute-done.1.b2_ref) | copy-start | bytes 933892
  147.9 18.0 %copy-start.7 = (bf16[304,512]{1,0:T(8,128)(2,1)}, bf16[304,512]{1,0:T(8,128)(2,1)S(1)}, u32[]{:S(2)}) copy-start(bf16[304,512]{1,0:T(8,128)(2,1)S(1)} %collective-permute-done.2.b3_ref) | copy-start | bytes 933892
  173.6 38.1 %all-to-all-start.5 = ((bf16[128,2,512]{2,1,0:T(2,128)(2,1)}), bf16[128,2,512]{2,1,0:T(2,128)(2,1)S(1)}, u32[]{:S(2)}, u32[]{:S(2)}) async-start(bf16[128,2,512]{2,1,0:T(2,128)(2,1)} %reshape.198), calls=%async_computation.5 | async-start | bytes 524288 | tf_op jit(solution)/shard_map/all_to_all | solution.py:43
  191.3 21.2 %collective-permute-start.3 = (bf16[560,512]{1,0:T(8,128)(2,1)}, bf16[560,512]{1,0:T(8,128)(2,1)S(1)}, u32[]{:S(2)}, u32[]{:S(2)}) collective-permute-start(bf16[560,512]{1,0:T(8,128)(2,1)} %get-tuple-element.79), channel_id=1, source_target_pairs={{0,1},{1,2},{2,3},{3,0},{4,5},{5,6},{6,7},{7,4},{8,9},{9,10},{10,1... | collective-permute-start | bytes 1720328 | tf_op jit(solution)/shard_map/ppermute | solution.py:38
  193.7 26.2 %collective-permute-start.4 = (bf16[560,512]{1,0:T(8,128)(2,1)}, bf16[560,512]{1,0:T(8,128)(2,1)S(1)}, u32[]{:S(2)}, u32[]{:S(2)}) collective-permute-start(bf16[560,512]{1,0:T(8,128)(2,1)} %get-tuple-element.80), channel_id=1, source_target_pairs={{0,2},{1,3},{2,0},{3,1},{4,6},{5,7},{6,4},{7,5},{8,10},{9,11},{10,... | collective-permute-start | bytes 1720328 | tf_op jit(solution)/shard_map/ppermute | solution.py:38
  197.2 26.2 %collective-permute-start.5 = (bf16[560,512]{1,0:T(8,128)(2,1)}, bf16[560,512]{1,0:T(8,128)(2,1)S(1)}, u32[]{:S(2)}, u32[]{:S(2)}) collective-permute-start(bf16[560,512]{1,0:T(8,128)(2,1)} %get-tuple-element.81), channel_id=1, source_target_pairs={{0,3},{1,0},{2,1},{3,2},{4,7},{5,4},{6,5},{7,6},{8,11},{9,8},{10,9... | collective-permute-start | bytes 1720328 | tf_op jit(solution)/shard_map/ppermute | solution.py:38
  212.5 10.9 %copy-start.2 = (bf16[560,512]{1,0:T(8,128)(2,1)}, bf16[560,512]{1,0:T(8,128)(2,1)S(1)}, u32[]{:S(2)}) copy-start(bf16[560,512]{1,0:T(8,128)(2,1)S(1)} %collective-permute-done.3.b1_ref) | copy-start | bytes 1720324
  219.9 3.4 %copy-start.3 = (bf16[560,512]{1,0:T(8,128)(2,1)}, bf16[560,512]{1,0:T(8,128)(2,1)S(1)}, u32[]{:S(2)}) copy-start(bf16[560,512]{1,0:T(8,128)(2,1)S(1)} %collective-permute-done.4.b2_ref) | copy-start | bytes 1720324
  223.4 0.8 copy-start.4
  292.0 18.8 %all-to-all-start.9 = ((bf16[8,16,3072]{2,1,0:T(8,128)(2,1)}), bf16[8,16,3072]{2,1,0:T(8,128)(2,1)S(1)}, u32[]{:S(2)}, u32[]{:S(2)}) async-start(bf16[8,16,3072]{2,1,0:T(8,128)(2,1)} %broadcast_in_dim.31), calls=%async_computation.9 | async-start | bytes 1572864 | tf_op jit(solution)/shard_map/all_to_all | solution.py:43
  310.8 0.9 copy-start
Sparse Core Ops, SparseCore 0:
  11.4 41.1 all-gather.4
  54.7 35.8 all-gather.6

commit v3 on v2

--- a/solution.py
+++ b/solution.py
@@ -39,6 +39,13 @@
     ]
 
 
+def two_rounds(block):
+    n = lax.axis_size("y")
+    other = lax.ppermute(block, "y", [(i, i ^ 1) for i in range(n)])
+    (both,) = call(add_kernel, [(block.shape, block.dtype)], block, other)
+    return both, lax.ppermute(both, "y", [(i, i ^ 2) for i in range(n)])
+
+
 def exchange(array, axes):
     return lax.all_to_all(array, axes, 0, 0, tiled=True)
 
@@ -55,14 +62,15 @@
     return lax.dot_general(left, right, (((0,), (0,)), ((), ())), preferred_element_type=F32)
 
 
-def one_hot(column, count):
-    places = lax.broadcasted_iota(jnp.int32, (column.shape[0], count), 1)
-    return jnp.where(places == column, 1.0, 0.0).astype(BF)
+def one_hot(row, count):
+    places = lax.broadcasted_iota(jnp.int32, (count, row.shape[1]), 0)
+    return jnp.where(places == row, 1.0, 0.0).astype(BF)
 
 
 def slots_hot(indices, count):
-    width = indices.shape[1]
-    return jnp.concatenate([one_hot(indices[:, c : c + 1], count) for c in range(width)], axis=0)
+    return jnp.concatenate(
+        [one_hot(indices[c : c + 1, :], count) for c in range(indices.shape[0])], axis=1
+    )
 
 
 def slot_rows(wide, width):
@@ -105,9 +113,9 @@
 ):
     grid = grid_ref[...]
     width = grid.shape[1]
-    for c in range(send_ref.shape[1]):
-        hot = one_hot(send_ref[:, c : c + 1], grid.shape[0])
-        out_ref[:, c * width : (c + 1) * width] = dot(hot, grid).astype(BF)
+    for c in range(send_ref.shape[0]):
+        hot = one_hot(send_ref[c : c + 1, :], grid.shape[0])
+        out_ref[:, c * width : (c + 1) * width] = outer(hot, grid).astype(BF)
     edges = src_ref.shape[1]
     spare = line_ref.shape[0]
     line_ref[...] = jnp.zeros_like(line_ref)
@@ -133,10 +141,10 @@
     )
 
 
-def own_column(ref, me):
+def own_row(ref, me):
     table = ref[...]
-    column = lax.broadcasted_iota(jnp.int32, table.shape, 1)
-    return jnp.sum(jnp.where(column == me, table, 0), axis=1, keepdims=True)
+    place = lax.broadcasted_iota(jnp.int32, table.shape, 0)
+    return jnp.sum(jnp.where(place == me, table, 0), axis=0, keepdims=True)
 
 
 def total_of(refs):
@@ -152,24 +160,26 @@
     received = slot_rows(recv_ref[...], width)
     hot = slots_hot(dst_ref[...], mesh_part.shape[0])
     projected = dot(received, whole(gath_ref, 0, rows)).astype(BF)
-    nodes = dot(hot, mesh_part).astype(BF)
+    nodes = outer(hot, mesh_part).astype(BF)
     preact = projected.astype(F32) + dot(nodes, whole(gath_ref, 1, rows))
     pre_ref[...] = preact
     hidden = (preact * sigmoid(preact)).astype(BF)
     normed, scaling = layer_norm(dot(hidden, whole(gath_ref, 2, rows)))
     norm_ref[...] = normed
     scale_ref[...] = scaling
-    partial_sum = outer(hot, normed.astype(BF)).astype(BF)
-    for y in range(sum_ref.shape[0]):
-        sum_ref[y] = partial_sum
-
-
-def latent_kernel(rows, own, me_ref, sums_ref, gath_ref, send_ref, latent_ref, halo_ref):
-    total = total_of([sums_ref[y] for y in range(sums_ref.shape[0])])
+    sum_ref[...] = dot(hot, normed.astype(BF)).astype(BF)
+
+
+def add_kernel(left_ref, right_ref, out_ref):
+    out_ref[...] = total_of([left_ref[...], right_ref[...]]).astype(out_ref.dtype)
+
+
+def latent_kernel(rows, own, me_ref, near_ref, far_ref, gath_ref, send_ref, latent_ref, halo_ref):
+    total = total_of([near_ref[...], far_ref[...]])
     latent = (node_rows(gath_ref, 3 * rows, own) + total).astype(BF)
     latent_ref[...] = latent
-    hot = one_hot(own_column(send_ref, me_ref[0]), latent.shape[0])
-    halo_ref[...] = dot(hot, latent).astype(BF)
+    hot = one_hot(own_row(send_ref, me_ref[0]), latent.shape[0])
+    halo_ref[...] = outer(hot, latent).astype(BF)
 
 
 def deal(me, refs, term_ref, rows, node_ref, own):
@@ -188,57 +198,61 @@
 
 
 def process_kernel(
-    rows, own, me_ref, latent_ref, halo_ref, edge_ref, gath_ref,
-    back_ref, local_ref, dst_ref, b0_ref, b1_ref, b2_ref, b3_ref, term_ref, node_ref,
+    rows, own, latent_ref, halo_ref, source_ref, target_ref, gath_ref,
+    back_ref, local_ref, dst_ref, node_ref, hidden_ref, mid_ref,
 ):
     latent = latent_ref[...]
     table = jnp.concatenate([latent, halo_ref[...]], axis=0)
-    nodes, width = latent.shape
-    hot_src = one_hot(edge_ref[:, 0:1], table.shape[0])
-    hot_dst = one_hot(edge_ref[:, 1:2], nodes)
+    nodes = latent.shape[0]
+    hot_src = one_hot(source_ref[...], table.shape[0])
+    hot_dst = one_hot(target_ref[...], nodes)
     w_src, w_dst, w_out = [whole(gath_ref, k, rows) for k in range(3)]
-    src_rows = dot(hot_src, table).astype(BF)
-    dst_rows = dot(hot_dst, latent).astype(BF)
+    src_rows = outer(hot_src, table).astype(BF)
+    dst_rows = outer(hot_dst, latent).astype(BF)
     preact = dot(src_rows, w_src) + dot(dst_rows, w_dst)
     gate = sigmoid(preact)
     hidden = (preact * gate).astype(BF)
+    hidden_ref[...] = hidden
     normed, scaling = layer_norm(dot(hidden, w_out))
-    node_ref[...] = outer(hot_dst, normed.astype(BF))
-    upstream = dot(hot_dst, node_rows(gath_ref, 3 * rows, own).astype(BF))
+    node_ref[...] = dot(hot_dst, normed.astype(BF))
+    upstream = outer(hot_dst, node_rows(gath_ref, 3 * rows, own).astype(BF))
     mid = norm_back(normed, scaling, upstream).astype(BF)
+    mid_ref[...] = mid
     grad = (dot_t(mid, w_out) * (gate * (1.0 + preact * (1.0 - gate)))).astype(BF)
-    at_dst = outer(hot_dst, grad).astype(BF)
-    dst_ref[...] = at_dst
-    at_src = outer(hot_src, grad)
+    dst_ref[...] = dot(hot_dst, grad).astype(BF)
+    at_src = dot(hot_src, grad)
     local_ref[...] = at_src[:nodes]
     back_ref[...] = at_src[nodes:].astype(BF)
-    term_ref[:, :width] = outer(latent, at_dst).astype(BF)
-    term_ref[:, width:] = outer(hidden, mid).astype(BF)
+
+
+def process_terms_kernel(
+    rows, own, me_ref, latent_ref, dst_ref, hidden_ref, mid_ref, node_ref,
+    b0_ref, b1_ref, b2_ref, b3_ref, term_ref,
+):
+    width = latent_ref.shape[1]
+    term_ref[:, :width] = outer(latent_ref[...], dst_ref[...]).astype(BF)
+    term_ref[:, width:] = outer(hidden_ref[...], mid_ref[...]).astype(BF)
     deal(me_ref[0], (b0_ref, b1_ref, b2_ref, b3_ref), term_ref, rows, node_ref, own)
 
 
 def owner_kernel(rows, me_ref, back_ref, send_ref, local_ref, dst_ref, gath_ref, out_ref, src_ref):
-    hot = one_hot(own_column(send_ref, me_ref[0]), local_ref.shape[0])
-    at_src = (local_ref[...] + outer(hot, back_ref[...])).astype(BF)
+    hot = one_hot(own_row(send_ref, me_ref[0]), local_ref.shape[0])
+    at_src = (local_ref[...] + dot(hot, back_ref[...])).astype(BF)
     src_ref[...] = at_src
     total = dot_t(at_src, whole(gath_ref, 0, rows)) + dot_t(dst_ref[...], whole(gath_ref, 1, rows))
-    total = total.astype(BF)
-    for y in range(out_ref.shape[0]):
-        out_ref[y] = total
+    out_ref[...] = total.astype(BF)
 
 
 def backward_kernel(
-    rows, own, me_ref, node_in_ref, proc_ref, latent_ref, src_ref, enc_ref, recv_ref, dst_ref,
+    rows, own, me_ref, near_ref, far_ref, proc_ref, latent_ref, src_ref, enc_ref, recv_ref, dst_ref,
     pre_ref, norm_ref, scale_ref,
     node_ref, slot_ref, b0_ref, b1_ref, b2_ref, b3_ref, term_ref, share_ref,
 ):
     nodes, width = latent_ref.shape
-    node_grad = node_rows(proc_ref, 3 * rows, own) + total_of(
-        [node_in_ref[y] for y in range(node_in_ref.shape[0])]
-    )
+    node_grad = node_rows(proc_ref, 3 * rows, own) + total_of([near_ref[...], far_ref[...]])
     node_ref[...] = node_grad
     hot = slots_hot(dst_ref[...], nodes)
-    upstream = dot(hot, node_grad.astype(BF))
+    upstream = outer(hot, node_grad.astype(BF))
     mid = norm_back(norm_ref[...], scale_ref[...], upstream).astype(BF)
     preact = pre_ref[...]
     gate = sigmoid(preact)
@@ -246,7 +260,7 @@
     grad = dot_t(mid, whole(enc_ref, 2, rows)) * (gate * (1.0 + preact * (1.0 - gate)))
     grad = grad.astype(BF)
     slot_ref[...] = wide_rows(grad, recv_ref.shape[1] // width)
-    at_node = outer(hot, grad)
+    at_node = dot(hot, grad)
     share_ref[...] = at_node
     terms = (
         outer(slot_rows(recv_ref[...], width), grad),
@@ -262,34 +276,37 @@
 def grid_kernel(rows, back_ref, send_ref, enc_ref, out_ref):
     nodes, width = out_ref.shape
     grads = dot_t(slot_rows(back_ref[...], width), whole(enc_ref, 0, rows)).astype(BF)
-    out_ref[...] = outer(slots_hot(send_ref[...], nodes), grads).astype(BF)
+    out_ref[...] = dot(slots_hot(send_ref[...], nodes), grads).astype(BF)
 
 
 def out_kernel(rows, me_ref, latent_ref, b0_ref, b1_ref, b2_ref, b3_ref, out_ref, sum_ref):
     total = total_of([b0_ref[...], b1_ref[...], b2_ref[...], b3_ref[...]])
     sum_ref[...] = total[: 2 * rows].astype(BF)
     own, nodes = out_ref.shape[0], latent_ref.shape[0]
-    mine = lax.broadcasted_iota(jnp.int32, (own, 1), 0) + me_ref[0] * own
-    latent = dot(one_hot(mine, nodes), latent_ref[...])
+    mine = lax.broadcasted_iota(jnp.int32, (1, own), 1) + me_ref[0] * own
+    latent = outer(one_hot(mine, nodes), latent_ref[...])
     out_ref[...] = (latent + total[2 * rows : 2 * rows + own]).astype(BF)
 
 
-def mesh_kernel(
-    rows, me_ref, sum_ref, node_ref, enc_ref, b0_ref, b1_ref, b2_ref, b3_ref, mesh_ref, pay_ref
-):
-    total = total_of([b0_ref[...], b1_ref[...], b2_ref[...], b3_ref[...]])
-    own, width = mesh_ref.shape
-    for k in range(4):
-        pay_ref[:, k * width : (k + 1) * width] = total[k * rows : (k + 1) * rows].astype(BF)
-    pay_ref[:, 4 * width : 5 * width] = sum_ref[:rows, :]
-    pay_ref[:, 5 * width :] = sum_ref[rows:, :]
-    back = dot_t(total[4 * rows :].astype(BF), whole(enc_ref, 1, rows))[:own]
+def level_kernel(rows, me_ref, sum_ref, b0_ref, b1_ref, b2_ref, b3_ref, keep_ref, give_ref):
+    width = sum_ref.shape[1]
+    half = rows // 2
+    for ref, core in ((keep_ref, me_ref[1]), (give_ref, 1 - me_ref[1])):
+        for k in range(4):
+            at = pl.ds(pl.multiple_of(k * rows + core * half, half), half)
+            block = total_of([b0_ref[at, :], b1_ref[at, :], b2_ref[at, :], b3_ref[at, :]])
+            ref[:, k * width : (k + 1) * width] = block.astype(BF)
+        for k in range(2):
+            at = pl.ds(pl.multiple_of(k * rows + core * half, half), half)
+            ref[:, (4 + k) * width : (5 + k) * width] = sum_ref[at, :]
+
+
+def mesh_kernel(rows, me_ref, node_ref, enc_ref, b0_ref, b1_ref, b2_ref, b3_ref, mesh_ref):
+    own = mesh_ref.shape[0]
+    total = total_of([b[4 * rows :, :] for b in (b0_ref, b1_ref, b2_ref, b3_ref)])
+    back = dot_t(total.astype(BF), whole(enc_ref, 1, rows))[:own]
     node = node_ref[pl.ds(pl.multiple_of(me_ref[0] * own, 8), own), :]
     mesh_ref[...] = (node + back).astype(BF)
-
-
-def sum_kernel(in_ref, out_ref):
-    out_ref[...] = total_of([in_ref[k] for k in range(in_ref.shape[0])]).astype(out_ref.dtype)
 
 
 def split_kernel(factor, in_ref, *out_refs):
@@ -317,19 +334,21 @@
     proc_dst,
     cotangent,
 ):
+    enc_send, enc_dst, hal_send = enc_send.T, enc_dst.T, hal_send.T
     dom = lax.axis_size(DOM)
     feat = lax.axis_size("y")
     deep = lax.axis_size("z")
     own, width = mesh_feat.shape
     nodes = own * feat
     rows = w_grid.shape[0]
-    caps = enc_send.shape[1]
-    halo = hal_send.shape[1]
+    caps = enc_send.shape[0]
+    pair = (dom, 2, width // 2)
+    halo = hal_send.shape[0]
     edges = proc_src.shape[0]
     held = own + (-own % PAD)
     factor = 1.0 / math.sqrt(own * dom * feat)
     index = lax.axis_index("y")
-    me = index.reshape(1)
+    me = jnp.stack([index, lax.axis_index("c")])
     if halo != feat or held - own < 8 or edges > width:
         raise ValueError("sizes")
     bind = functools.partial
@@ -357,23 +376,23 @@
     proc_gath = lax.all_gather(proc_pack, "y", axis=0)
 
     slots = dom * caps
+    one_sum = ((nodes, width), BF)
     partial_sum, preact, normed, scaling = call(
         bind(encode_kernel, rows, own),
-        [((feat, nodes, width), BF), ((slots, width), F32), ((slots, width), F32), ((slots, 1), F32)],
+        [one_sum, ((slots, width), F32), ((slots, width), F32), ((slots, 1), F32)],
         received,
         enc_dst,
         enc_gath,
     )
-    sums = exchange(partial_sum, "y")
     latent, halo_out = call(
         bind(latent_kernel, rows, own),
-        [((nodes, width), BF), ((dom, width), BF)],
-        sums,
+        [one_sum, ((dom, width), BF)],
+        *two_rounds(partial_sum),
         enc_gath,
         hal_send,
         me=me,
     )
-    halo_rows = exchange(halo_out, DOM)
+    halo_rows = exchange(halo_out.reshape(pair), DOM).reshape(dom, width)
 
     lines = enc_gath[:, 3 * rows + own : 3 * rows + own + 3, :edges].astype(jnp.int32)
     source = lines[:, 0] * 16 + lines[:, 1]
@@ -381,39 +400,51 @@
     place = jnp.where(slot < 0, source, nodes + slot // halo)
     keeper = jnp.where(slot < 0, jnp.arange(feat, dtype=jnp.int32)[:, None], slot % halo)
     mine = keeper == index
-    edge_index = jnp.stack(
-        [jnp.where(mine, place, -1).reshape(-1), jnp.where(mine, lines[:, 2], -1).reshape(-1)], axis=1
-    )
-    blocks = [((2 * rows + held, width), BF)] * 4
-    halo_back, at_local, at_dst, *first = call(
+    halo_back, at_local, at_dst, messages, hidden, mid = call(
         bind(process_kernel, rows, own),
-        [((dom, width), BF), ((nodes, width), F32), ((nodes, width), BF)] + blocks,
+        [
+            ((dom, width), BF),
+            ((nodes, width), F32),
+            one_sum,
+            ((nodes, width), F32),
+            ((feat * edges, width), BF),
+            ((feat * edges, width), BF),
+        ],
         latent,
         halo_rows,
-        edge_index,
+        jnp.where(mine, place, -1).reshape(1, feat * edges),
+        jnp.where(mine, lines[:, 2], -1).reshape(1, feat * edges),
         proc_gath,
+    )
+    returned = exchange(halo_back.reshape(pair), DOM)
+    first = call(
+        bind(process_terms_kernel, rows, own),
+        [((2 * rows + held, width), BF)] * 4,
+        latent,
+        at_dst,
+        hidden,
+        mid,
+        messages,
         me=me,
-        scratch=[pltpu.VMEM((width, 2 * width), BF), pltpu.VMEM((nodes, width), F32)],
-    )
-    returned = exchange(halo_back, DOM)
-    returned, *first = lax.optimization_barrier((returned, *onward(first)))
+        scratch=[pltpu.VMEM((width, 2 * width), BF)],
+    )
+    first = onward(first)
+    returned, *first = lax.optimization_barrier((returned, *first))
     node_part, at_src = call(
         bind(owner_kernel, rows),
-        [((feat, nodes, width), BF), ((nodes, width), BF)],
-        returned,
+        [one_sum, one_sum],
+        returned.reshape(dom, width),
         hal_send,
         at_local,
         at_dst,
         proc_gath,
         me=me,
     )
-    node_in = exchange(node_part, "y")
-
-    blocks = [((4 * rows + held, width), BF)] * 4
+
     node_grad, slot_out, *second = call(
         bind(backward_kernel, rows, own),
-        [((nodes, width), F32), ((dom, caps * width), BF)] + blocks,
-        node_in,
+        [((nodes, width), F32), ((dom, caps * width), BF)] + [((4 * rows + held, width), BF)] * 4,
+        *two_rounds(node_part),
         proc_gath,
         latent,
         at_src,
@@ -426,32 +457,32 @@
         me=me,
         scratch=[pltpu.VMEM((width, 4 * width), BF), pltpu.VMEM((nodes, width), F32)],
     )
-    slot_back = exchange(slot_out.reshape(dom, caps, width), DOM).reshape(dom, caps * width)
-    slot_back, *second = lax.optimization_barrier((slot_back, *onward(second)))
+    slot_back = exchange(slot_out.reshape(dom, caps, width), DOM)
+    second = onward(second)
     out_rows, first_sum = call(
         bind(out_kernel, rows), [((own, width), BF), ((2 * rows, width), BF)], latent, *first, me=me
     )
-    g_mesh, level = call(
-        bind(mesh_kernel, rows),
-        [((own, width), BF), ((rows, 6 * width), BF)],
-        first_sum,
-        node_grad,
+    half = ((rows // 2, 6 * width), BF)
+    keep, give = call(bind(level_kernel, rows), [half, half], first_sum, *second, me=me)
+    given = lax.ppermute(give, "c", [(0, 1), (1, 0)])
+    slot_back, given = lax.optimization_barrier((slot_back, given))
+    (level,) = call(add_kernel, [half], keep, given)
+    level = exchange(level.reshape(rows // 2, 2, 3 * width), ("x", "z"))
+    level = level.astype(F32).sum(axis=0).astype(BF)
+    level = exchange(jnp.broadcast_to(level[None], (deep, *level.shape)), "z")
+    level = level.reshape(deep, 6 * width)
+    near = lax.axis_size(("x", "c"))
+    totals = exchange(jnp.broadcast_to(level[None], (near, *level.shape)), ("c", "x"))
+    totals = call(bind(split_kernel, factor), [((rows, width), F32)] * 6, totals)
+    (g_mesh,) = call(
+        bind(mesh_kernel, rows), [((own, width), BF)], node_grad, enc_gath, *second, me=me
+    )
+    (g_grid,) = call(
+        bind(grid_kernel, rows),
+        [(grid_feat.shape, BF)],
+        slot_back.reshape(dom, caps * width),
+        enc_send,
         enc_gath,
-        *second,
-        me=me,
-    )
-    near = lax.axis_size(("x", "c"))
-    thin = rows // near
-    level = exchange(level.reshape(near, thin, 6 * width), ("x", "c"))
-    (level,) = call(sum_kernel, [((thin, 6 * width), BF)], level)
-    level = exchange(level.reshape(deep, thin // deep, 6 * width), "z")
-    mine_sum = level.astype(F32).sum(axis=0).astype(BF)
-    level = exchange(jnp.broadcast_to(mine_sum[None], (deep, *mine_sum.shape)), "z")
-    level = level.reshape(thin, 6 * width)
-    totals = exchange(jnp.broadcast_to(level[None], (near, *level.shape)), ("x", "c"))
-    totals = call(bind(split_kernel, factor), [((rows, width), F32)] * 6, totals)
-    (g_grid,) = call(
-        bind(grid_kernel, rows), [(grid_feat.shape, BF)], slot_back, enc_send, enc_gath
     )
     return (out_rows, g_grid, g_mesh) + tuple(totals)
 

time: 322 us -> 334 us (1.037)
  blocking collectives: 72.4 us -> 97.7 us
  waiting for transfers between devices: 85 us -> 68.6 us
  Pallas kernels: 38.6 us -> 45.5 us
  other arithmetic: 6.76 us -> 2.96 us
    all_to_all x6 -> x4, waiting for transfers between devices: 69.4 us -> 20 us  [exchange(): return lax.all_to_all(array, axes, 0, 0, tiled=True)]
    all_to_all x4 -> x3, blocking collectives: 72.4 us -> 97.7 us  [exchange(): return lax.all_to_all(array, axes, 0, 0, tiled=True)]
    all_to_all x6 -> x4, starting transfers between devices: 69.9 us -> 46.7 us  [exchange(): return lax.all_to_all(array, axes, 0, 0, tiled=True)]
    ppermute x0 -> x5, starting transfers between devices: none -> 19.8 us  [the longest x2 8.99 us: two_rounds(): return (both, lax.ppermute(both, 'y', [(i, i ^ 2) for i in range(n)]))]
    ppermute x0 -> x5, waiting for transfers between devices: none -> 17.3 us  [the longest x2 8.49 us: two_rounds(): return (both, lax.ppermute(both, 'y', [(i, i ^ 2) for i in range(n)]))]
    ppermute x6, waiting for transfers between devices: 14.9 us -> 30.6 us  [onward(): lax.ppermute(blocks[k], 'y', [(i, (i + k) % n) for i in range(n)])]
    pallas_call x11 -> x15, Pallas kernels: 38.6 us -> 45.5 us  [call(): pl.pallas_call(kernel, out_shape=tuple((jax.ShapeDtypeStruct(s, d) for s,...]
    reshape x1 -> x4, local copies, waits for them, and re-layouts: 1.85 us -> 6.33 us  [the longest x1 1.85 us: per_device(): slot_back = exchange(slot_out.reshape(dom, caps, width), DOM)]
  transfers between devices with their start and end apart: 14 -> 17, of which waited for: 10 -> 13; matrix products, arithmetic and copies ran while one was open for 3% -> 2% of each run, Pallas kernels for 4% -> 7%
where the time goes in v3:
time: 334 us; the launch traced here: 332 us
  blocking collectives  97.7 us (29%)
  starting transfers between devices  86.5 us (26%)
  waiting for transfers between devices  68.6 us (21%)
  Pallas kernels  45.5 us (14%)
  local copies, waits for them, and re-layouts  16.8 us (5%)
  between operations  14.2 us (4%)
    all_to_all x3, blocking collectives, exchange(): return lax.all_to_all(array, axes, 0, 0, tiled=True)  97.7 us
    all_to_all x4, starting transfers between devices, exchange(): return lax.all_to_all(array, axes, 0, 0, tiled=True)  46.7 us
    pallas_call x15, Pallas kernels, call(): pl.pallas_call(kernel, out_shape=tuple((jax.ShapeDtypeStruct(s, d) for s,...  45.5 us
    ppermute x6, waiting for transfers between devices, onward(): lax.ppermute(blocks[k], 'y', [(i, (i + k) % n) for i in range(n)])  30.6 us
    all_to_all x4, waiting for transfers between devices, exchange(): return lax.all_to_all(array, axes, 0, 0, tiled=True)  20 us
    ppermute x6, starting transfers between devices, onward(): lax.ppermute(blocks[k], 'y', [(i, (i + k) % n) for i in range(n)])  19.9 us
    ppermute x2, starting transfers between devices, two_rounds(): return (both, lax.ppermute(both, 'y', [(i, i ^ 2) for i in range(n)]))  8.99 us
    ppermute x2, waiting for transfers between devices, two_rounds(): return (both, lax.ppermute(both, 'y', [(i, i ^ 2) for i in range(n)]))  8.49 us
  transfers between devices with their start and end apart: 17, of which 13 were waited for; matrix products, arithmetic and copies ran while one was open for 2% of the time, Pallas kernels for 7%

profile of v3, /device:TPU:1, one launch (start us, length us, event | category | flops | bytes accessed | tf_op | source)
XLA Modules:
  0.0 332.3 jit_solution(11863246567177704382)
XLA Ops:
  11.7 40.7 %all_to_all.35 = bf16[128,2,512]{2,1,0:T(2,128)(2,1)S(1)} all-to-all(bf16[128,2,512]{2,1,0:T(2,128)(2,1)S(1)} %reshape.195), channel_id=1, replica_groups=mesh['z'=16,'x'=4,'c'=2,'y'=4] {'z','x','c'}, dimensions={0} | all-to-all | bytes 524288 | tf_op jit(solution)/shard_map/all_to_all | solution.py:50
  53.2 3.5 %shard_map.206 = (bf16[160,512]{1,0:T(8,128)(2,1)}, f32[256,512]{1,0:T(8,128)}, f32[256,512]{1,0:T(8,128)}, f32[256,1]{1,0:T(8,128)}) custom-call(bf16[128,1024]{1,0:T(8,128)(2,1)} %bitcast.28, s32[2,128]{1,0:T(2,128)} %bitcast.41, bf16[4,432,512]{2,1,0:T(8,128)(2,1)} %bitcast.19), custom_call_target="tpu_custom_call" | custom-call | tf_op jit(solution)/shard_map/pallas_call | solution.py:25
  66.4 4.8 %collective-permute-start.1 = (bf16[160,512]{1,0:T(8,128)(2,1)}, bf16[160,512]{1,0:T(8,128)(2,1)S(1)}, u32[]{:S(2)}, u32[]{:S(2)}) collective-permute-start(bf16[160,512]{1,0:T(8,128)(2,1)} %shard_map.207.near_ref), channel_id=1, source_target_pairs={{0,2},{1,3},{2,0},{3,1},{4,6},{5,7},{6,4},{7,5},{8,10},{9,11},{10,... | collective-permute-start | bytes 491528 | tf_op jit(solution)/shard_map/ppermute | solution.py:46
  71.9 4.9 %collective-permute-done.1.far_ref = bf16[160,512]{1,0:T(8,128)(2,1)S(1)} collective-permute-done((bf16[160,512]{1,0:T(8,128)(2,1)}, bf16[160,512]{1,0:T(8,128)(2,1)S(1)}, u32[]{:S(2)}, u32[]{:S(2)}) %collective-permute-start.1) | collective-permute-done | bytes 163872 | tf_op jit(solution)/shard_map/ppermute | solution.py:46
  81.7 14.5 %all-to-all-start.1 = ((bf16[128,2,256]{2,1,0:T(2,128)(2,1)}), bf16[128,2,256]{2,1,0:T(2,128)(2,1)S(1)}, u32[]{:S(2)}, u32[]{:S(2)}) async-start(bf16[128,2,256]{2,1,0:T(2,128)(2,1)} %reshape.197), calls=%async_computation.1 | async-start | bytes 262144 | tf_op jit(solution)/shard_map/all_to_all | solution.py:50
  97.6 14.6 %all-to-all-done.1 = bf16[128,2,256]{2,1,0:T(2,128)(2,1)S(1)} async-done(((bf16[128,2,256]{2,1,0:T(2,128)(2,1)}), bf16[128,2,256]{2,1,0:T(2,128)(2,1)S(1)}, u32[]{:S(2)}, u32[]{:S(2)}) %all-to-all-start.1) | async-done | bytes 131104 | tf_op jit(solution)/shard_map/all_to_all | solution.py:50
  112.9 6.0 %shard_map.209 = (bf16[128,512]{1,0:T(8,128)(2,1)}, f32[160,512]{1,0:T(8,128)}, bf16[160,512]{1,0:T(8,128)(2,1)}, f32[160,512]{1,0:T(8,128)}, bf16[640,512]{1,0:T(8,128)(2,1)}, /*index=5*/bf16[640,512]{1,0:T(8,128)(2,1)}) custom-call(bf16[160,512]{1,0:T(8,128)(2,1)} %get-tuple-element.56.latent_ref, bf16[128,512]{1,0:T(8,128)(2,1)} %bitcast.33, ...), custom_call_target="tpu_custom_call" | custom-call | tf_op jit(solution)/shard_map/pallas_call | solution.py:25
  120.4 7.2 %all-to-all-start.2 = ((bf16[128,2,256]{2,1,0:T(2,128)(2,1)}), bf16[128,2,256]{2,1,0:T(2,128)(2,1)S(1)}, u32[]{:S(2)}, u32[]{:S(2)}) async-start(bf16[128,2,256]{2,1,0:T(2,128)(2,1)} %reshape.199), calls=%async_computation.2 | async-start | bytes 262144 | tf_op jit(solution)/shard_map/all_to_all | solution.py:50
  133.0 3.8 %collective-permute-start.3 = (bf16[304,512]{1,0:T(8,128)(2,1)}, bf16[304,512]{1,0:T(8,128)(2,1)S(1)}, u32[]{:S(2)}, u32[]{:S(2)}) collective-permute-start(bf16[304,512]{1,0:T(8,128)(2,1)} %get-tuple-element.66), channel_id=1, source_target_pairs={{0,2},{1,3},{2,0},{3,1},{4,6},{5,7},{6,4},{7,5},{8,10},{9,11},{10,... | collective-permute-start | bytes 933896 | tf_op jit(solution)/shard_map/ppermute | solution.py:38
  136.8 4.1 %collective-permute-start.4 = (bf16[304,512]{1,0:T(8,128)(2,1)}, bf16[304,512]{1,0:T(8,128)(2,1)S(1)}, u32[]{:S(2)}, u32[]{:S(2)}) collective-permute-start(bf16[304,512]{1,0:T(8,128)(2,1)} %get-tuple-element.67), channel_id=1, source_target_pairs={{0,3},{1,0},{2,1},{3,2},{4,7},{5,4},{6,5},{7,6},{8,11},{9,8},{10,9... | collective-permute-start | bytes 933896 | tf_op jit(solution)/shard_map/ppermute | solution.py:38
  142.6 6.0 %collective-permute-done.3.b2_ref = bf16[304,512]{1,0:T(8,128)(2,1)S(1)} collective-permute-done((bf16[304,512]{1,0:T(8,128)(2,1)}, bf16[304,512]{1,0:T(8,128)(2,1)S(1)}, u32[]{:S(2)}, u32[]{:S(2)}) %collective-permute-start.3) | collective-permute-done | bytes 311328 | tf_op jit(solution)/shard_map/ppermute | solution.py:38
  155.5 4.2 %collective-permute-start.5 = (bf16[160,512]{1,0:T(8,128)(2,1)}, bf16[160,512]{1,0:T(8,128)(2,1)S(1)}, u32[]{:S(2)}, u32[]{:S(2)}) collective-permute-start(bf16[160,512]{1,0:T(8,128)(2,1)} %get-tuple-element.75.left_ref), channel_id=1, source_target_pairs={{0,1},{1,0},{2,3},{3,2},{4,5},{5,4},{6,7},{7,6},{8,9},{9,8},{10,11... | collective-permute-start | bytes 491528 | tf_op jit(solution)/shard_map/ppermute | solution.py:44
  159.8 3.9 %collective-permute-done.5.right_ref = bf16[160,512]{1,0:T(8,128)(2,1)S(1)} collective-permute-done((bf16[160,512]{1,0:T(8,128)(2,1)}, bf16[160,512]{1,0:T(8,128)(2,1)S(1)}, u32[]{:S(2)}, u32[]{:S(2)}) %collective-permute-start.5) | collective-permute-done | bytes 163872 | tf_op jit(solution)/shard_map/ppermute | solution.py:44
  166.1 4.2 %collective-permute-start.6 = (bf16[160,512]{1,0:T(8,128)(2,1)}, bf16[160,512]{1,0:T(8,128)(2,1)S(1)}, u32[]{:S(2)}, u32[]{:S(2)}) collective-permute-start(bf16[160,512]{1,0:T(8,128)(2,1)} %shard_map.213.near_ref), channel_id=1, source_target_pairs={{0,2},{1,3},{2,0},{3,1},{4,6},{5,7},{6,4},{7,5},{8,10},{9,11},{10,... | collective-permute-start | bytes 491528 | tf_op jit(solution)/shard_map/ppermute | solution.py:46
  170.2 3.6 %collective-permute-done.6.far_ref = bf16[160,512]{1,0:T(8,128)(2,1)S(1)} collective-permute-done((bf16[160,512]{1,0:T(8,128)(2,1)}, bf16[160,512]{1,0:T(8,128)(2,1)S(1)}, u32[]{:S(2)}, u32[]{:S(2)}) %collective-permute-start.6) | collective-permute-done | bytes 163872 | tf_op jit(solution)/shard_map/ppermute | solution.py:46
  174.5 5.7 %shard_map.214 = (f32[160,512]{1,0:T(8,128)}, bf16[128,1024]{1,0:T(8,128)(2,1)}, bf16[560,512]{1,0:T(8,128)(2,1)}, bf16[560,512]{1,0:T(8,128)(2,1)}, bf16[560,512]{1,0:T(8,128)(2,1)}, /*index=5*/bf16[560,512]{1,0:T(8,128)(2,1)}) custom-call(s32[2]{0:T(128)} %pad_add_fusion.me_ref, bf16[160,512]{1,0:T(8,128)(2,1)} %shard_map.213.near_ref, ...), custom_call_target="tpu_custom_call" | custom-call | tf_op jit(solution)/shard_map/pallas_call | solution.py:25
  182.0 18.3 %all-to-all-start.3 = ((bf16[128,2,512]{2,1,0:T(2,128)(2,1)}), bf16[128,2,512]{2,1,0:T(2,128)(2,1)S(1)}, u32[]{:S(2)}, u32[]{:S(2)}) async-start(bf16[128,2,512]{2,1,0:T(2,128)(2,1)} %reshape.201), calls=%async_computation.3 | async-start | bytes 524288 | tf_op jit(solution)/shard_map/all_to_all | solution.py:50
  203.7 4.1 %collective-permute-start.8 = (bf16[560,512]{1,0:T(8,128)(2,1)}, bf16[560,512]{1,0:T(8,128)(2,1)S(1)}, u32[]{:S(2)}, u32[]{:S(2)}) collective-permute-start(bf16[560,512]{1,0:T(8,128)(2,1)} %get-tuple-element.84), channel_id=1, source_target_pairs={{0,2},{1,3},{2,0},{3,1},{4,6},{5,7},{6,4},{7,5},{8,10},{9,11},{10,... | collective-permute-start | bytes 1720328 | tf_op jit(solution)/shard_map/ppermute | solution.py:38
  212.6 4.6 %collective-permute-done.7.b1_ref = bf16[560,512]{1,0:T(8,128)(2,1)S(1)} collective-permute-done((bf16[560,512]{1,0:T(8,128)(2,1)}, bf16[560,512]{1,0:T(8,128)(2,1)S(1)}, u32[]{:S(2)}, u32[]{:S(2)}) %collective-permute-start.7) | collective-permute-done | bytes 573472 | tf_op jit(solution)/shard_map/ppermute | solution.py:38
  217.3 13.2 %collective-permute-done.8.b2_ref = bf16[560,512]{1,0:T(8,128)(2,1)S(1)} collective-permute-done((bf16[560,512]{1,0:T(8,128)(2,1)}, bf16[560,512]{1,0:T(8,128)(2,1)S(1)}, u32[]{:S(2)}, u32[]{:S(2)}) %collective-permute-start.8) | collective-permute-done | bytes 573472 | tf_op jit(solution)/shard_map/ppermute | solution.py:38
  244.9 39.7 %all_to_all.36 = bf16[64,2,1536]{2,1,0:T(2,128)(2,1)S(1)} all-to-all(bf16[64,2,1536]{2,1,0:T(2,128)(2,1)S(1)} %reshape.203), channel_id=1, replica_groups=mesh['z'=16,'x'=4,'c'=2,'y'=4] {'x','z'}, dimensions={0} | all-to-all | bytes 786432 | tf_op jit(solution)/shard_map/all_to_all | solution.py:50
  285.0 17.3 %all_to_all.37 = bf16[16,2,1536]{2,1,0:T(2,128)(2,1)S(1)} all-to-all(bf16[16,2,1536]{2,1,0:T(2,128)(2,1)S(1)} %broadcast_in_dim.29), channel_id=1, replica_groups=mesh['z'=16,'x'=4,'c'=2,'y'=4] {'z'}, dimensions={0} | all-to-all | bytes 196608 | tf_op jit(solution)/shard_map/all_to_all | solution.py:50
  303.2 6.8 %all-to-all-start.6 = ((bf16[8,16,3072]{2,1,0:T(8,128)(2,1)}), bf16[8,16,3072]{2,1,0:T(8,128)(2,1)S(1)}, u32[]{:S(2)}, u32[]{:S(2)}) async-start(bf16[8,16,3072]{2,1,0:T(8,128)(2,1)} %broadcast_in_dim.31), calls=%async_computation.6 | async-start | bytes 1572864 | tf_op jit(solution)/shard_map/all_to_all | solution.py:50
  316.9 5.4 %all-to-all-done.6.in_ref = bf16[8,16,3072]{2,1,0:T(8,128)(2,1)S(1)} async-done(((bf16[8,16,3072]{2,1,0:T(8,128)(2,1)}), bf16[8,16,3072]{2,1,0:T(8,128)(2,1)S(1)}, u32[]{:S(2)}, u32[]{:S(2)}) %all-to-all-start.6) | async-done | bytes 786464 | tf_op jit(solution)/shard_map/all_to_all | solution.py:50
  (76 shorter events, 77.0 us)
Async XLA Ops:
  7.2 46.0 %all-gather.5.cloned.1.call-start = ((), (), s32[]{:S(2)}) async-start(), calls=%async_computation.7 | async-start | bytes 2211840 | tf_op jit(solution)/shard_map/all_gather | solution.py:375
  9.8 103.0 %all-gather.7.cloned.1.call-start = ((), (), s32[]{:S(2)}) async-start(), calls=%async_computation.8 | async-start | bytes 2211840 | tf_op jit(solution)/shard_map/all_gather | solution.py:376
  56.7 7.3 %collective-permute-start = (bf16[160,512]{1,0:T(8,128)(2,1)}, bf16[160,512]{1,0:T(8,128)(2,1)S(1)}, u32[]{:S(2)}, u32[]{:S(2)}) collective-permute-start(bf16[160,512]{1,0:T(8,128)(2,1)} %get-tuple-element.55.left_ref), channel_id=1, source_target_pairs={{0,1},{1,0},{2,3},{3,2},{4,5},{5,4},{6,7},{7,6},{8,9},{9,8},{10,11... | collective-permute-start | bytes 491528 | tf_op jit(solution)/shard_map/ppermute | solution.py:44
  66.4 10.5 %collective-permute-start.1 = (bf16[160,512]{1,0:T(8,128)(2,1)}, bf16[160,512]{1,0:T(8,128)(2,1)S(1)}, u32[]{:S(2)}, u32[]{:S(2)}) collective-permute-start(bf16[160,512]{1,0:T(8,128)(2,1)} %shard_map.207.near_ref), channel_id=1, source_target_pairs={{0,2},{1,3},{2,0},{3,1},{4,6},{5,7},{6,4},{7,5},{8,10},{9,11},{10,... | collective-permute-start | bytes 491528 | tf_op jit(solution)/shard_map/ppermute | solution.py:46
  81.7 30.5 %all-to-all-start.1 = ((bf16[128,2,256]{2,1,0:T(2,128)(2,1)}), bf16[128,2,256]{2,1,0:T(2,128)(2,1)S(1)}, u32[]{:S(2)}, u32[]{:S(2)}) async-start(bf16[128,2,256]{2,1,0:T(2,128)(2,1)} %reshape.197), calls=%async_computation.1 | async-start | bytes 262144 | tf_op jit(solution)/shard_map/all_to_all | solution.py:50
  120.4 31.4 %all-to-all-start.2 = ((bf16[128,2,256]{2,1,0:T(2,128)(2,1)}), bf16[128,2,256]{2,1,0:T(2,128)(2,1)S(1)}, u32[]{:S(2)}, u32[]{:S(2)}) async-start(bf16[128,2,256]{2,1,0:T(2,128)(2,1)} %reshape.199), calls=%async_computation.2 | async-start | bytes 262144 | tf_op jit(solution)/shard_map/all_to_all | solution.py:50
  131.0 11.6 %collective-permute-start.2 = (bf16[304,512]{1,0:T(8,128)(2,1)}, bf16[304,512]{1,0:T(8,128)(2,1)S(1)}, u32[]{:S(2)}, u32[]{:S(2)}) collective-permute-start(bf16[304,512]{1,0:T(8,128)(2,1)} %get-tuple-element.65), channel_id=1, source_target_pairs={{0,1},{1,2},{2,3},{3,0},{4,5},{5,6},{6,7},{7,4},{8,9},{9,10},{10,1... | collective-permute-start | bytes 933896 | tf_op jit(solution)/shard_map/ppermute | solution.py:38
  133.0 15.6 %collective-permute-start.3 = (bf16[304,512]{1,0:T(8,128)(2,1)}, bf16[304,512]{1,0:T(8,128)(2,1)S(1)}, u32[]{:S(2)}, u32[]{:S(2)}) collective-permute-start(bf16[304,512]{1,0:T(8,128)(2,1)} %get-tuple-element.66), channel_id=1, source_target_pairs={{0,2},{1,3},{2,0},{3,1},{4,6},{5,7},{6,4},{7,5},{8,10},{9,11},{10,... | collective-permute-start | bytes 933896 | tf_op jit(solution)/shard_map/ppermute | solution.py:38
  136.8 15.0 %collective-permute-start.4 = (bf16[304,512]{1,0:T(8,128)(2,1)}, bf16[304,512]{1,0:T(8,128)(2,1)S(1)}, u32[]{:S(2)}, u32[]{:S(2)}) collective-permute-start(bf16[304,512]{1,0:T(8,128)(2,1)} %get-tuple-element.67), channel_id=1, source_target_pairs={{0,3},{1,0},{2,1},{3,2},{4,7},{5,4},{6,5},{7,6},{8,11},{9,8},{10,9... | collective-permute-start | bytes 933896 | tf_op jit(solution)/shard_map/ppermute | solution.py:38
  142.6 37.6 %copy-start.5 = (bf16[304,512]{1,0:T(8,128)(2,1)}, bf16[304,512]{1,0:T(8,128)(2,1)S(1)}, u32[]{:S(2)}) copy-start(bf16[304,512]{1,0:T(8,128)(2,1)S(1)} %collective-permute-done.2.b1_ref) | copy-start | bytes 933892
  148.6 31.5 %copy-start.6 = (bf16[304,512]{1,0:T(8,128)(2,1)}, bf16[304,512]{1,0:T(8,128)(2,1)S(1)}, u32[]{:S(2)}) copy-start(bf16[304,512]{1,0:T(8,128)(2,1)S(1)} %collective-permute-done.3.b2_ref) | copy-start | bytes 933892
  151.8 28.4 %copy-start.7 = (bf16[304,512]{1,0:T(8,128)(2,1)}, bf16[304,512]{1,0:T(8,128)(2,1)S(1)}, u32[]{:S(2)}) copy-start(bf16[304,512]{1,0:T(8,128)(2,1)S(1)} %collective-permute-done.4.b3_ref) | copy-start | bytes 933892
  155.5 8.2 %collective-permute-start.5 = (bf16[160,512]{1,0:T(8,128)(2,1)}, bf16[160,512]{1,0:T(8,128)(2,1)S(1)}, u32[]{:S(2)}, u32[]{:S(2)}) collective-permute-start(bf16[160,512]{1,0:T(8,128)(2,1)} %get-tuple-element.75.left_ref), channel_id=1, source_target_pairs={{0,1},{1,0},{2,3},{3,2},{4,5},{5,4},{6,7},{7,6},{8,9},{9,8},{10,11... | collective-permute-start | bytes 491528 | tf_op jit(solution)/shard_map/ppermute | solution.py:44
  166.1 7.8 %collective-permute-start.6 = (bf16[160,512]{1,0:T(8,128)(2,1)}, bf16[160,512]{1,0:T(8,128)(2,1)S(1)}, u32[]{:S(2)}, u32[]{:S(2)}) collective-permute-start(bf16[160,512]{1,0:T(8,128)(2,1)} %shard_map.213.near_ref), channel_id=1, source_target_pairs={{0,2},{1,3},{2,0},{3,1},{4,6},{5,7},{6,4},{7,5},{8,10},{9,11},{10,... | collective-permute-start | bytes 491528 | tf_op jit(solution)/shard_map/ppermute | solution.py:46
  182.0 58.8 %all-to-all-start.3 = ((bf16[128,2,512]{2,1,0:T(2,128)(2,1)}), bf16[128,2,512]{2,1,0:T(2,128)(2,1)S(1)}, u32[]{:S(2)}, u32[]{:S(2)}) async-start(bf16[128,2,512]{2,1,0:T(2,128)(2,1)} %reshape.201), calls=%async_computation.3 | async-start | bytes 524288 | tf_op jit(solution)/shard_map/all_to_all | solution.py:50
  200.3 16.9 %collective-permute-start.7 = (bf16[560,512]{1,0:T(8,128)(2,1)}, bf16[560,512]{1,0:T(8,128)(2,1)S(1)}, u32[]{:S(2)}, u32[]{:S(2)}) collective-permute-start(bf16[560,512]{1,0:T(8,128)(2,1)} %get-tuple-element.83), channel_id=1, source_target_pairs={{0,1},{1,2},{2,3},{3,0},{4,5},{5,6},{6,7},{7,4},{8,9},{9,10},{10,1... | collective-permute-start | bytes 1720328 | tf_op jit(solution)/shard_map/ppermute | solution.py:38
  203.7 26.8 %collective-permute-start.8 = (bf16[560,512]{1,0:T(8,128)(2,1)}, bf16[560,512]{1,0:T(8,128)(2,1)S(1)}, u32[]{:S(2)}, u32[]{:S(2)}) collective-permute-start(bf16[560,512]{1,0:T(8,128)(2,1)} %get-tuple-element.84), channel_id=1, source_target_pairs={{0,2},{1,3},{2,0},{3,1},{4,6},{5,7},{6,4},{7,5},{8,10},{9,11},{10,... | collective-permute-start | bytes 1720328 | tf_op jit(solution)/shard_map/ppermute | solution.py:38
  207.8 24.6 %collective-permute-start.9 = (bf16[560,512]{1,0:T(8,128)(2,1)}, bf16[560,512]{1,0:T(8,128)(2,1)S(1)}, u32[]{:S(2)}, u32[]{:S(2)}) collective-permute-start(bf16[560,512]{1,0:T(8,128)(2,1)} %get-tuple-element.85), channel_id=1, source_target_pairs={{0,3},{1,0},{2,1},{3,2},{4,7},{5,4},{6,5},{7,6},{8,11},{9,8},{10,9... | collective-permute-start | bytes 1720328 | tf_op jit(solution)/shard_map/ppermute | solution.py:38
  217.3 15.2 %copy-start.1 = (bf16[560,512]{1,0:T(8,128)(2,1)}, bf16[560,512]{1,0:T(8,128)(2,1)S(1)}, u32[]{:S(2)}) copy-start(bf16[560,512]{1,0:T(8,128)(2,1)S(1)} %collective-permute-done.7.b1_ref) | copy-start | bytes 1720324
  230.5 2.0 copy-start.2
  232.4 0.8 copy-start.3
  235.9 4.9 %collective-permute-start.10 = (bf16[64,3072]{1,0:T(8,128)(2,1)}, bf16[64,3072]{1,0:T(8,128)(2,1)S(1)}, u32[]{:S(2)}, u32[]{:S(2)}) collective-permute-start(bf16[64,3072]{1,0:T(8,128)(2,1)} %get-tuple-element.86), channel_id=1, source_target_pairs={{0,4},{4,0},{1,5},{5,1},{2,6},{6,2},{3,7},{7,3},{8,12},{12,8},{9,1... | collective-permute-start | bytes 1179656 | tf_op jit(solution)/shard_map/ppermute | solution.py:467
  303.2 19.0 %all-to-all-start.6 = ((bf16[8,16,3072]{2,1,0:T(8,128)(2,1)}), bf16[8,16,3072]{2,1,0:T(8,128)(2,1)S(1)}, u32[]{:S(2)}, u32[]{:S(2)}) async-start(bf16[8,16,3072]{2,1,0:T(8,128)(2,1)} %broadcast_in_dim.31), calls=%async_computation.6 | async-start | bytes 1572864 | tf_op jit(solution)/shard_map/all_to_all | solution.py:50
  322.2 0.9 copy-start
  (5 other events, 3.4 us)
Sparse Core Ops, SparseCore 0:
  10.7 41.1 all-gather.4
  54.0 36.5 all-gather.6

commit v4 on v3

--- a/solution.py
+++ b/solution.py
@@ -32,18 +32,14 @@
     )(*operands)
 
 
-def onward(blocks):
-    n = len(blocks)
+def onward(keep, give, tail):
+    n = lax.axis_size("y")
+    given = lax.ppermute(give, "c", [(0, 1), (1, 0)])
+    size = (keep.shape[0] + tail.shape[0]) // n
+    blocks = call(merge_kernel, [((size, keep.shape[1]), BF)] * n, keep, given, tail)
     return [blocks[0]] + [
         lax.ppermute(blocks[k], "y", [(i, (i + k) % n) for i in range(n)]) for k in range(1, n)
     ]
-
-
-def two_rounds(block):
-    n = lax.axis_size("y")
-    other = lax.ppermute(block, "y", [(i, i ^ 1) for i in range(n)])
-    (both,) = call(add_kernel, [(block.shape, block.dtype)], block, other)
-    return both, lax.ppermute(both, "y", [(i, i ^ 2) for i in range(n)])
 
 
 def exchange(array, axes):
@@ -167,34 +163,45 @@
     normed, scaling = layer_norm(dot(hidden, whole(gath_ref, 2, rows)))
     norm_ref[...] = normed
     scale_ref[...] = scaling
-    sum_ref[...] = dot(hot, normed.astype(BF)).astype(BF)
-
-
-def add_kernel(left_ref, right_ref, out_ref):
-    out_ref[...] = total_of([left_ref[...], right_ref[...]]).astype(out_ref.dtype)
-
-
-def latent_kernel(rows, own, me_ref, near_ref, far_ref, gath_ref, send_ref, latent_ref, halo_ref):
-    total = total_of([near_ref[...], far_ref[...]])
+    partial_sum = dot(hot, normed.astype(BF)).astype(BF)
+    for y in range(sum_ref.shape[0]):
+        sum_ref[y] = partial_sum
+
+
+def latent_kernel(rows, own, me_ref, sums_ref, gath_ref, send_ref, latent_ref, halo_ref):
+    total = total_of([sums_ref[y] for y in range(sums_ref.shape[0])])
     latent = (node_rows(gath_ref, 3 * rows, own) + total).astype(BF)
     latent_ref[...] = latent
     hot = one_hot(own_row(send_ref, me_ref[0]), latent.shape[0])
     halo_ref[...] = outer(hot, latent).astype(BF)
 
 
-def deal(me, refs, term_ref, rows, node_ref, own):
-    count = len(refs)
-    width = refs[0].shape[1]
+def deal(me_ref, keep_ref, give_ref, tail_ref, term_ref, rows, node_ref, own):
+    width = keep_ref.shape[1]
     terms = term_ref.shape[1] // width
-    spare = refs[0].shape[0] - terms * rows - own
-    for k, ref in enumerate(refs):
+    count = term_ref.shape[0] // rows
+    half = rows // 2
+    held = tail_ref.shape[0] // count
+    me, core = me_ref[0], me_ref[1]
+    for k in range(count):
         to = lax.rem(me + k, count)
-        at = pl.ds(pl.multiple_of(to * rows, rows), rows)
-        for t in range(terms):
-            ref[t * rows : (t + 1) * rows, :] = term_ref[at, t * width : (t + 1) * width]
+        for ref, side in ((keep_ref, core), (give_ref, 1 - core)):
+            at = pl.ds(pl.multiple_of(to * rows + side * half, half), half)
+            for t in range(terms):
+                place = (k * terms + t) * half
+                ref[place : place + half, :] = term_ref[at, t * width : (t + 1) * width]
         block = node_ref[pl.ds(pl.multiple_of(to * own, 8), own), :]
-        block = jnp.concatenate([block, jnp.zeros((spare, width), F32)], axis=0)
-        ref[terms * rows :, :] = block.astype(BF)
+        block = jnp.concatenate([block, jnp.zeros((held - own, width), F32)], axis=0)
+        tail_ref[k * held : (k + 1) * held, :] = block.astype(BF)
+
+
+def merge_kernel(keep_ref, given_ref, tail_ref, *out_refs):
+    count = len(out_refs)
+    size, held = keep_ref.shape[0] // count, tail_ref.shape[0] // count
+    for k, ref in enumerate(out_refs):
+        at = slice(k * size, (k + 1) * size)
+        ref[:size, :] = total_of([keep_ref[at, :], given_ref[at, :]]).astype(BF)
+        ref[size:, :] = tail_ref[k * held : (k + 1) * held, :]
 
 
 def process_kernel(
@@ -227,12 +234,12 @@
 
 def process_terms_kernel(
     rows, own, me_ref, latent_ref, dst_ref, hidden_ref, mid_ref, node_ref,
-    b0_ref, b1_ref, b2_ref, b3_ref, term_ref,
+    keep_ref, give_ref, tail_ref, term_ref,
 ):
     width = latent_ref.shape[1]
     term_ref[:, :width] = outer(latent_ref[...], dst_ref[...]).astype(BF)
     term_ref[:, width:] = outer(hidden_ref[...], mid_ref[...]).astype(BF)
-    deal(me_ref[0], (b0_ref, b1_ref, b2_ref, b3_ref), term_ref, rows, node_ref, own)
+    deal(me_ref, keep_ref, give_ref, tail_ref, term_ref, rows, node_ref, own)
 
 
 def owner_kernel(rows, me_ref, back_ref, send_ref, local_ref, dst_ref, gath_ref, out_ref, src_ref):
@@ -240,16 +247,20 @@
     at_src = (local_ref[...] + dot(hot, back_ref[...])).astype(BF)
     src_ref[...] = at_src
     total = dot_t(at_src, whole(gath_ref, 0, rows)) + dot_t(dst_ref[...], whole(gath_ref, 1, rows))
-    out_ref[...] = total.astype(BF)
+    total = total.astype(BF)
+    for y in range(out_ref.shape[0]):
+        out_ref[y] = total
 
 
 def backward_kernel(
-    rows, own, me_ref, near_ref, far_ref, proc_ref, latent_ref, src_ref, enc_ref, recv_ref, dst_ref,
+    rows, own, me_ref, sums_ref, proc_ref, latent_ref, src_ref, enc_ref, recv_ref, dst_ref,
     pre_ref, norm_ref, scale_ref,
-    node_ref, slot_ref, b0_ref, b1_ref, b2_ref, b3_ref, term_ref, share_ref,
+    node_ref, slot_ref, keep_ref, give_ref, tail_ref, term_ref, share_ref,
 ):
     nodes, width = latent_ref.shape
-    node_grad = node_rows(proc_ref, 3 * rows, own) + total_of([near_ref[...], far_ref[...]])
+    node_grad = node_rows(proc_ref, 3 * rows, own) + total_of(
+        [sums_ref[y] for y in range(sums_ref.shape[0])]
+    )
     node_ref[...] = node_grad
     hot = slots_hot(dst_ref[...], nodes)
     upstream = outer(hot, node_grad.astype(BF))
@@ -270,7 +281,7 @@
     )
     for k, term in enumerate(terms):
         term_ref[:, k * width : (k + 1) * width] = term.astype(BF)
-    deal(me_ref[0], (b0_ref, b1_ref, b2_ref, b3_ref), term_ref, rows, share_ref, own)
+    deal(me_ref, keep_ref, give_ref, tail_ref, term_ref, rows, share_ref, own)
 
 
 def grid_kernel(rows, back_ref, send_ref, enc_ref, out_ref):
@@ -279,34 +290,37 @@
     out_ref[...] = dot(slots_hot(send_ref[...], nodes), grads).astype(BF)
 
 
-def out_kernel(rows, me_ref, latent_ref, b0_ref, b1_ref, b2_ref, b3_ref, out_ref, sum_ref):
+def out_kernel(me_ref, latent_ref, b0_ref, b1_ref, b2_ref, b3_ref, out_ref, sum_ref):
     total = total_of([b0_ref[...], b1_ref[...], b2_ref[...], b3_ref[...]])
-    sum_ref[...] = total[: 2 * rows].astype(BF)
+    size = sum_ref.shape[0]
+    sum_ref[...] = total[:size].astype(BF)
     own, nodes = out_ref.shape[0], latent_ref.shape[0]
     mine = lax.broadcasted_iota(jnp.int32, (1, own), 1) + me_ref[0] * own
     latent = outer(one_hot(mine, nodes), latent_ref[...])
-    out_ref[...] = (latent + total[2 * rows : 2 * rows + own]).astype(BF)
-
-
-def level_kernel(rows, me_ref, sum_ref, b0_ref, b1_ref, b2_ref, b3_ref, keep_ref, give_ref):
+    out_ref[...] = (latent + total[size : size + own]).astype(BF)
+
+
+def level_kernel(sum_ref, b0_ref, b1_ref, b2_ref, b3_ref, out_ref):
     width = sum_ref.shape[1]
-    half = rows // 2
-    for ref, core in ((keep_ref, me_ref[1]), (give_ref, 1 - me_ref[1])):
-        for k in range(4):
-            at = pl.ds(pl.multiple_of(k * rows + core * half, half), half)
-            block = total_of([b0_ref[at, :], b1_ref[at, :], b2_ref[at, :], b3_ref[at, :]])
-            ref[:, k * width : (k + 1) * width] = block.astype(BF)
-        for k in range(2):
-            at = pl.ds(pl.multiple_of(k * rows + core * half, half), half)
-            ref[:, (4 + k) * width : (5 + k) * width] = sum_ref[at, :]
+    half = out_ref.shape[0]
+    for k in range(4):
+        at = slice(k * half, (k + 1) * half)
+        block = total_of([b0_ref[at, :], b1_ref[at, :], b2_ref[at, :], b3_ref[at, :]])
+        out_ref[:, k * width : (k + 1) * width] = block.astype(BF)
+    for k in range(2):
+        out_ref[:, (4 + k) * width : (5 + k) * width] = sum_ref[k * half : (k + 1) * half, :]
 
 
 def mesh_kernel(rows, me_ref, node_ref, enc_ref, b0_ref, b1_ref, b2_ref, b3_ref, mesh_ref):
     own = mesh_ref.shape[0]
-    total = total_of([b[4 * rows :, :] for b in (b0_ref, b1_ref, b2_ref, b3_ref)])
+    total = total_of([b[2 * rows :, :] for b in (b0_ref, b1_ref, b2_ref, b3_ref)])
     back = dot_t(total.astype(BF), whole(enc_ref, 1, rows))[:own]
     node = node_ref[pl.ds(pl.multiple_of(me_ref[0] * own, 8), own), :]
     mesh_ref[...] = (node + back).astype(BF)
+
+
+def sum_kernel(in_ref, out_ref):
+    out_ref[...] = total_of([in_ref[k] for k in range(in_ref.shape[0])]).astype(out_ref.dtype)
 
 
 def split_kernel(factor, in_ref, *out_refs):
@@ -376,10 +390,10 @@
     proc_gath = lax.all_gather(proc_pack, "y", axis=0)
 
     slots = dom * caps
-    one_sum = ((nodes, width), BF)
+    one_sum, all_sums = ((nodes, width), BF), ((feat, nodes, width), BF)
     partial_sum, preact, normed, scaling = call(
         bind(encode_kernel, rows, own),
-        [one_sum, ((slots, width), F32), ((slots, width), F32), ((slots, 1), F32)],
+        [all_sums, ((slots, width), F32), ((slots, width), F32), ((slots, 1), F32)],
         received,
         enc_dst,
         enc_gath,
@@ -387,7 +401,7 @@
     latent, halo_out = call(
         bind(latent_kernel, rows, own),
         [one_sum, ((dom, width), BF)],
-        *two_rounds(partial_sum),
+        exchange(partial_sum, "y"),
         enc_gath,
         hal_send,
         me=me,
@@ -419,7 +433,7 @@
     returned = exchange(halo_back.reshape(pair), DOM)
     first = call(
         bind(process_terms_kernel, rows, own),
-        [((2 * rows + held, width), BF)] * 4,
+        [((4 * rows, width), BF), ((4 * rows, width), BF), ((feat * held, width), BF)],
         latent,
         at_dst,
         hidden,
@@ -428,11 +442,10 @@
         me=me,
         scratch=[pltpu.VMEM((width, 2 * width), BF)],
     )
-    first = onward(first)
-    returned, *first = lax.optimization_barrier((returned, *first))
+    first = onward(*first)
     node_part, at_src = call(
         bind(owner_kernel, rows),
-        [one_sum, one_sum],
+        [all_sums, one_sum],
         returned.reshape(dom, width),
         hal_send,
         at_local,
@@ -441,10 +454,19 @@
         me=me,
     )
 
+    node_in = exchange(node_part, "y")
+    node_in, *first = lax.optimization_barrier((node_in, *first))
+
     node_grad, slot_out, *second = call(
         bind(backward_kernel, rows, own),
-        [((nodes, width), F32), ((dom, caps * width), BF)] + [((4 * rows + held, width), BF)] * 4,
-        *two_rounds(node_part),
+        [
+            ((nodes, width), F32),
+            ((dom, caps * width), BF),
+            ((8 * rows, width), BF),
+            ((8 * rows, width), BF),
+            ((feat * held, width), BF),
+        ],
+        node_in,
         proc_gath,
         latent,
         at_src,
@@ -458,16 +480,17 @@
         scratch=[pltpu.VMEM((width, 4 * width), BF), pltpu.VMEM((nodes, width), F32)],
     )
     slot_back = exchange(slot_out.reshape(dom, caps, width), DOM)
-    second = onward(second)
+    second = onward(*second)
     out_rows, first_sum = call(
-        bind(out_kernel, rows), [((own, width), BF), ((2 * rows, width), BF)], latent, *first, me=me
-    )
-    half = ((rows // 2, 6 * width), BF)
-    keep, give = call(bind(level_kernel, rows), [half, half], first_sum, *second, me=me)
-    given = lax.ppermute(give, "c", [(0, 1), (1, 0)])
-    slot_back, given = lax.optimization_barrier((slot_back, given))
-    (level,) = call(add_kernel, [half], keep, given)
-    level = exchange(level.reshape(rows // 2, 2, 3 * width), ("x", "z"))
+        out_kernel, [((own, width), BF), ((rows, width), BF)], latent, *first, me=me
+    )
+    (level,) = call(level_kernel, [((rows // 2, 6 * width), BF)], first_sum, *second)
+    slot_back, level = lax.optimization_barrier((slot_back, level))
+    across = lax.axis_size("x")
+    thin = rows // (2 * across)
+    level = exchange(level.reshape(across, thin, 6 * width), "x")
+    (level,) = call(sum_kernel, [((thin, 6 * width), BF)], level)
+    level = exchange(level.reshape(deep, 2, 3 * width), "z")
     level = level.astype(F32).sum(axis=0).astype(BF)
     level = exchange(jnp.broadcast_to(level[None], (deep, *level.shape)), "z")
     level = level.reshape(deep, 6 * width)

time: 334 us -> 297 us (0.89)
  waiting for transfers between devices: 68.6 us -> 51.9 us
  starting transfers between devices: 86.5 us -> 73.7 us
  blocking collectives: 97.7 us -> 90 us
    all_to_all x4 -> x6, waiting for transfers between devices: 20 us -> 38.9 us  [exchange(): return lax.all_to_all(array, axes, 0, 0, tiled=True)]
    ppermute x6, waiting for transfers between devices: 30.6 us -> 12.3 us  [onward(): lax.ppermute(blocks[k], 'y', [(i, (i + k) % n) for i in range(n)])]
    ppermute x5 -> x2, waiting for transfers between devices: 17.3 us -> 0.01 us  [onward(): given = lax.ppermute(give, 'c', [(0, 1), (1, 0)])]
    ppermute x5 -> x2, starting transfers between devices: 19.8 us -> 6.02 us  [onward(): given = lax.ppermute(give, 'c', [(0, 1), (1, 0)])]
    all_to_all x3 -> x4, blocking collectives: 97.7 us -> 90 us  [exchange(): return lax.all_to_all(array, axes, 0, 0, tiled=True)]
    all_to_all x4 -> x6, starting transfers between devices: 46.7 us -> 46.3 us  [exchange(): return lax.all_to_all(array, axes, 0, 0, tiled=True)]
    unnamed x29 -> x27, local copies, waits for them, and re-layouts: 8.05 us -> 7.95 us
  transfers between devices with their start and end apart: 17 -> 16, of which waited for: 13 -> 8; matrix products, arithmetic and copies ran while one was open for 2% -> 3% of each run, Pallas kernels for 7% -> 9%
where the time goes in v4:
time: 297 us; the launch traced here: 295 us
  blocking collectives  90 us (30%)
  starting transfers between devices  73.7 us (25%)
  waiting for transfers between devices  51.9 us (17%)
  Pallas kernels  45.9 us (15%)
  local copies, waits for them, and re-layouts  16.4 us (6%)
  between operations  14.3 us (5%)
    all_to_all x4, blocking collectives, exchange(): return lax.all_to_all(array, axes, 0, 0, tiled=True)  90 us
    all_to_all x6, starting transfers between devices, exchange(): return lax.all_to_all(array, axes, 0, 0, tiled=True)  46.3 us
    pallas_call x15, Pallas kernels, call(): pl.pallas_call(kernel, out_shape=tuple((jax.ShapeDtypeStruct(s, d) for s,...  45.9 us
    all_to_all x6, waiting for transfers between devices, exchange(): return lax.all_to_all(array, axes, 0, 0, tiled=True)  38.9 us
    ppermute x6, starting transfers between devices, onward(): lax.ppermute(blocks[k], 'y', [(i, (i + k) % n) for i in range(n)])  21.3 us
    ppermute x6, waiting for transfers between devices, onward(): lax.ppermute(blocks[k], 'y', [(i, (i + k) % n) for i in range(n)])  12.3 us
    unnamed x27, local copies, waits for them, and re-layouts  7.95 us
    ppermute x2, starting transfers between devices, onward(): given = lax.ppermute(give, 'c', [(0, 1), (1, 0)])  6.02 us
  transfers between devices with their start and end apart: 16, of which 8 were waited for; matrix products, arithmetic and copies ran while one was open for 3% of the time, Pallas kernels for 9%

profile of v4, /device:TPU:1, one launch (start us, length us, event | category | flops | bytes accessed | tf_op | source)
XLA Modules:
  0.0 294.9 jit_solution(13810750906475507619)
XLA Ops:
  11.7 40.7 %all_to_all.50 = bf16[128,2,512]{2,1,0:T(2,128)(2,1)S(1)} all-to-all(bf16[128,2,512]{2,1,0:T(2,128)(2,1)S(1)} %reshape.198), channel_id=1, replica_groups=mesh['z'=16,'x'=4,'c'=2,'y'=4] {'z','x','c'}, dimensions={0} | all-to-all | bytes 524288 | tf_op jit(solution)/shard_map/all_to_all | solution.py:46
  53.2 3.7 %shard_map.206 = (bf16[4,160,512]{2,1,0:T(8,128)(2,1)}, f32[256,512]{1,0:T(8,128)}, f32[256,512]{1,0:T(8,128)}, f32[256,1]{1,0:T(8,128)}) custom-call(bf16[128,1024]{1,0:T(8,128)(2,1)} %bitcast.29, s32[2,128]{1,0:T(2,128)} %bitcast.45, bf16[4,432,512]{2,1,0:T(8,128)(2,1)} %bitcast.20), custom_call_target="tpu_custom_call" | custom-call | tf_op jit(solution)/shard_map/pallas_call | solution.py:25
  56.9 4.2 %all-to-all-start.1 = ((bf16[4,160,512]{2,1,0:T(8,128)(2,1)}), bf16[4,160,512]{2,1,0:T(8,128)(2,1)S(1)}, u32[]{:S(2)}, u32[]{:S(2)}) async-start(bf16[4,160,512]{2,1,0:T(8,128)(2,1)} %get-tuple-element.59), calls=%async_computation.1 | async-start | bytes 1310720 | tf_op jit(solution)/shard_map/all_to_all | solution.py:46
  62.5 8.7 %all-to-all-done.1.sums_ref = bf16[4,160,512]{2,1,0:T(8,128)(2,1)S(1)} async-done(((bf16[4,160,512]{2,1,0:T(8,128)(2,1)}), bf16[4,160,512]{2,1,0:T(8,128)(2,1)S(1)}, u32[]{:S(2)}, u32[]{:S(2)}) %all-to-all-start.1) | async-done | bytes 655392 | tf_op jit(solution)/shard_map/all_to_all | solution.py:46
  76.3 15.6 %all-to-all-start.2 = ((bf16[128,2,256]{2,1,0:T(2,128)(2,1)}), bf16[128,2,256]{2,1,0:T(2,128)(2,1)S(1)}, u32[]{:S(2)}, u32[]{:S(2)}) async-start(bf16[128,2,256]{2,1,0:T(2,128)(2,1)} %reshape.200), calls=%async_computation.2 | async-start | bytes 262144 | tf_op jit(solution)/shard_map/all_to_all | solution.py:46
  93.3 14.6 %all-to-all-done.2 = bf16[128,2,256]{2,1,0:T(2,128)(2,1)S(1)} async-done(((bf16[128,2,256]{2,1,0:T(2,128)(2,1)}), bf16[128,2,256]{2,1,0:T(2,128)(2,1)S(1)}, u32[]{:S(2)}, u32[]{:S(2)}) %all-to-all-start.2) | async-done | bytes 131104 | tf_op jit(solution)/shard_map/all_to_all | solution.py:46
  108.6 6.0 %shard_map.208 = (bf16[128,512]{1,0:T(8,128)(2,1)}, f32[160,512]{1,0:T(8,128)}, bf16[160,512]{1,0:T(8,128)(2,1)}, f32[160,512]{1,0:T(8,128)}, bf16[640,512]{1,0:T(8,128)(2,1)}, /*index=5*/bf16[640,512]{1,0:T(8,128)(2,1)}) custom-call(bf16[160,512]{1,0:T(8,128)(2,1)} %get-tuple-element.60.latent_ref, bf16[128,512]{1,0:T(8,128)(2,1)} %bitcast.35, ...), custom_call_target="tpu_custom_call" | custom-call | tf_op jit(solution)/shard_map/pallas_call | solution.py:25
  116.2 7.2 %all-to-all-start.3 = ((bf16[128,2,256]{2,1,0:T(2,128)(2,1)}), bf16[128,2,256]{2,1,0:T(2,128)(2,1)S(1)}, u32[]{:S(2)}, u32[]{:S(2)}) async-start(bf16[128,2,256]{2,1,0:T(2,128)(2,1)} %reshape.202), calls=%async_computation.3 | async-start | bytes 262144 | tf_op jit(solution)/shard_map/all_to_all | solution.py:46
  123.4 3.4 %shard_map.210 = (bf16[512,512]{1,0:T(8,128)(2,1)}, bf16[512,512]{1,0:T(8,128)(2,1)}, bf16[192,512]{1,0:T(8,128)(2,1)}) custom-call(s32[2]{0:T(128)} %pad_add_fusion.me_ref, bf16[160,512]{1,0:T(8,128)(2,1)} %get-tuple-element.60.latent_ref, bf16[160,512]{1,0:T(8,128)(2,1)} %get-tuple-element.65.dst_ref, bf16[640,512]{1,0:T(8,128)(2,1)} %get-tuple-element.67.hidden_ref, ...), custom_call_target="tpu_custom_call" | custom-call | tf_op jit(solution)/shard_map/pallas_call | solution.py:25
  129.5 9.9 %all-to-all-done.3 = bf16[128,2,256]{2,1,0:T(2,128)(2,1)S(1)} async-done(((bf16[128,2,256]{2,1,0:T(2,128)(2,1)}), bf16[128,2,256]{2,1,0:T(2,128)(2,1)S(1)}, u32[]{:S(2)}, u32[]{:S(2)}) %all-to-all-start.3) | async-done | bytes 131104 | tf_op jit(solution)/shard_map/all_to_all | solution.py:46
  143.2 3.7 %all-to-all-start.4 = ((bf16[4,160,512]{2,1,0:T(8,128)(2,1)}), bf16[4,160,512]{2,1,0:T(8,128)(2,1)S(1)}, u32[]{:S(2)}, u32[]{:S(2)}) async-start(bf16[4,160,512]{2,1,0:T(8,128)(2,1)} %get-tuple-element.66), calls=%async_computation.4 | async-start | bytes 1310720 | tf_op jit(solution)/shard_map/all_to_all | solution.py:46
  149.8 3.3 %collective-permute-start.1 = (bf16[176,512]{1,0:T(8,128)(2,1)}, bf16[176,512]{1,0:T(8,128)(2,1)S(1)}, u32[]{:S(2)}, u32[]{:S(2)}) collective-permute-start(bf16[176,512]{1,0:T(8,128)(2,1)} %get-tuple-element.74), channel_id=1, source_target_pairs={{0,1},{1,2},{2,3},{3,0},{4,5},{5,6},{6,7},{7,4},{8,9},{9,10},{10,1... | collective-permute-start | bytes 540680 | tf_op jit(solution)/shard_map/ppermute | solution.py:41
  153.2 4.3 %collective-permute-start.2 = (bf16[176,512]{1,0:T(8,128)(2,1)}, bf16[176,512]{1,0:T(8,128)(2,1)S(1)}, u32[]{:S(2)}, u32[]{:S(2)}) collective-permute-start(bf16[176,512]{1,0:T(8,128)(2,1)} %get-tuple-element.75), channel_id=1, source_target_pairs={{0,2},{1,3},{2,0},{3,1},{4,6},{5,7},{6,4},{7,5},{8,10},{9,11},{10,... | collective-permute-start | bytes 540680 | tf_op jit(solution)/shard_map/ppermute | solution.py:41
  166.1 5.6 %shard_map.213 = (f32[160,512]{1,0:T(8,128)}, bf16[128,1024]{1,0:T(8,128)(2,1)}, bf16[1024,512]{1,0:T(8,128)(2,1)}, bf16[1024,512]{1,0:T(8,128)(2,1)}, bf16[192,512]{1,0:T(8,128)(2,1)}) custom-call(s32[2]{0:T(128)} %pad_add_fusion.me_ref, bf16[4,160,512]{2,1,0:T(8,128)(2,1)} %copy-done.2, bf16[4,432,512]{2,1,0:T(8,128)(2,1)} %bitcast.28, ...), custom_call_target="tpu_custom_call" | custom-call | tf_op jit(solution)/shard_map/pallas_call | solution.py:25
  176.8 6.8 %all-to-all-start.5 = ((bf16[128,2,512]{2,1,0:T(2,128)(2,1)}), bf16[128,2,512]{2,1,0:T(2,128)(2,1)S(1)}, u32[]{:S(2)}, u32[]{:S(2)}) async-start(bf16[128,2,512]{2,1,0:T(2,128)(2,1)} %reshape.204), calls=%async_computation.5 | async-start | bytes 524288 | tf_op jit(solution)/shard_map/all_to_all | solution.py:46
  187.2 4.1 %collective-permute-start.5 = (bf16[304,512]{1,0:T(8,128)(2,1)}, bf16[304,512]{1,0:T(8,128)(2,1)S(1)}, u32[]{:S(2)}, u32[]{:S(2)}) collective-permute-start(bf16[304,512]{1,0:T(8,128)(2,1)} %get-tuple-element.93), channel_id=1, source_target_pairs={{0,1},{1,2},{2,3},{3,0},{4,5},{5,6},{6,7},{7,4},{8,9},{9,10},{10,1... | collective-permute-start | bytes 933896 | tf_op jit(solution)/shard_map/ppermute | solution.py:41
  191.4 3.2 %collective-permute-start.6 = (bf16[304,512]{1,0:T(8,128)(2,1)}, bf16[304,512]{1,0:T(8,128)(2,1)S(1)}, u32[]{:S(2)}, u32[]{:S(2)}) collective-permute-start(bf16[304,512]{1,0:T(8,128)(2,1)} %get-tuple-element.94), channel_id=1, source_target_pairs={{0,2},{1,3},{2,0},{3,1},{4,6},{5,7},{6,4},{7,5},{8,10},{9,11},{10,... | collective-permute-start | bytes 933896 | tf_op jit(solution)/shard_map/ppermute | solution.py:41
  194.6 3.2 %collective-permute-start.7 = (bf16[304,512]{1,0:T(8,128)(2,1)}, bf16[304,512]{1,0:T(8,128)(2,1)S(1)}, u32[]{:S(2)}, u32[]{:S(2)}) collective-permute-start(bf16[304,512]{1,0:T(8,128)(2,1)} %get-tuple-element.95), channel_id=1, source_target_pairs={{0,3},{1,0},{2,1},{3,2},{4,7},{5,4},{6,5},{7,6},{8,11},{9,8},{10,9... | collective-permute-start | bytes 933896 | tf_op jit(solution)/shard_map/ppermute | solution.py:41
  200.0 6.0 %collective-permute-done.6.b2_ref = bf16[304,512]{1,0:T(8,128)(2,1)S(1)} collective-permute-done((bf16[304,512]{1,0:T(8,128)(2,1)}, bf16[304,512]{1,0:T(8,128)(2,1)S(1)}, u32[]{:S(2)}, u32[]{:S(2)}) %collective-permute-start.6) | collective-permute-done | bytes 311328 | tf_op jit(solution)/shard_map/ppermute | solution.py:41
  210.6 10.9 %all_to_all.51.in_ref = bf16[4,16,3072]{2,1,0:T(8,128)(2,1)} all-to-all(bf16[4,16,3072]{2,1,0:T(8,128)(2,1)} %bitcast.31), channel_id=1, replica_groups=mesh['z'=16,'x'=4,'c'=2,'y'=4] {'x'}, dimensions={0} | all-to-all | bytes 786432 | tf_op jit(solution)/shard_map/all_to_all | solution.py:46
  224.1 23.4 %all_to_all.52 = bf16[16,2,1536]{2,1,0:T(2,128)(2,1)S(1)} all-to-all(bf16[16,2,1536]{2,1,0:T(2,128)(2,1)S(1)} %reshape.207), channel_id=1, replica_groups=mesh['z'=16,'x'=4,'c'=2,'y'=4] {'z'}, dimensions={0} | all-to-all | bytes 196608 | tf_op jit(solution)/shard_map/all_to_all | solution.py:46
  247.6 15.1 %all_to_all.53 = bf16[16,2,1536]{2,1,0:T(2,128)(2,1)S(1)} all-to-all(bf16[16,2,1536]{2,1,0:T(2,128)(2,1)S(1)} %broadcast_in_dim.29), channel_id=1, replica_groups=mesh['z'=16,'x'=4,'c'=2,'y'=4] {'z'}, dimensions={0} | all-to-all | bytes 196608 | tf_op jit(solution)/shard_map/all_to_all | solution.py:46
  263.7 8.9 %all-to-all-start.9 = ((bf16[8,16,3072]{2,1,0:T(8,128)(2,1)}), bf16[8,16,3072]{2,1,0:T(8,128)(2,1)S(1)}, u32[]{:S(2)}, u32[]{:S(2)}) async-start(bf16[8,16,3072]{2,1,0:T(8,128)(2,1)} %broadcast_in_dim.31), calls=%async_computation.9 | async-start | bytes 1572864 | tf_op jit(solution)/shard_map/all_to_all | solution.py:46
  279.1 5.7 %all-to-all-done.9.in_ref = bf16[8,16,3072]{2,1,0:T(8,128)(2,1)S(1)} async-done(((bf16[8,16,3072]{2,1,0:T(8,128)(2,1)}), bf16[8,16,3072]{2,1,0:T(8,128)(2,1)S(1)}, u32[]{:S(2)}, u32[]{:S(2)}) %all-to-all-start.9) | async-done | bytes 786464 | tf_op jit(solution)/shard_map/all_to_all | solution.py:46
  (73 shorter events, 62.4 us)
Async XLA Ops:
  7.2 46.0 %all-gather.5.cloned.1.call-start = ((), (), s32[]{:S(2)}) async-start(), calls=%async_computation.10 | async-start | bytes 2211840 | tf_op jit(solution)/shard_map/all_gather | solution.py:389
  9.8 98.8 %all-gather.7.cloned.1.call-start = ((), (), s32[]{:S(2)}) async-start(), calls=%async_computation.11 | async-start | bytes 2211840 | tf_op jit(solution)/shard_map/all_gather | solution.py:390
  56.9 14.3 %all-to-all-start.1 = ((bf16[4,160,512]{2,1,0:T(8,128)(2,1)}), bf16[4,160,512]{2,1,0:T(8,128)(2,1)S(1)}, u32[]{:S(2)}, u32[]{:S(2)}) async-start(bf16[4,160,512]{2,1,0:T(8,128)(2,1)} %get-tuple-element.59), calls=%async_computation.1 | async-start | bytes 1310720 | tf_op jit(solution)/shard_map/all_to_all | solution.py:46
  76.3 31.7 %all-to-all-start.2 = ((bf16[128,2,256]{2,1,0:T(2,128)(2,1)}), bf16[128,2,256]{2,1,0:T(2,128)(2,1)S(1)}, u32[]{:S(2)}, u32[]{:S(2)}) async-start(bf16[128,2,256]{2,1,0:T(2,128)(2,1)} %reshape.200), calls=%async_computation.2 | async-start | bytes 262144 | tf_op jit(solution)/shard_map/all_to_all | solution.py:46
  116.2 23.2 %all-to-all-start.3 = ((bf16[128,2,256]{2,1,0:T(2,128)(2,1)}), bf16[128,2,256]{2,1,0:T(2,128)(2,1)S(1)}, u32[]{:S(2)}, u32[]{:S(2)}) async-start(bf16[128,2,256]{2,1,0:T(2,128)(2,1)} %reshape.202), calls=%async_computation.3 | async-start | bytes 262144 | tf_op jit(solution)/shard_map/all_to_all | solution.py:46
  126.7 20.2 %collective-permute-start = (bf16[512,512]{1,0:T(8,128)(2,1)}, bf16[512,512]{1,0:T(8,128)(2,1)S(1)}, u32[]{:S(2)}, u32[]{:S(2)}) collective-permute-start(bf16[512,512]{1,0:T(8,128)(2,1)} %get-tuple-element.71), channel_id=1, source_target_pairs={{0,4},{4,0},{1,5},{5,1},{2,6},{6,2},{3,7},{7,3},{8,12},{12,8},{9,1... | collective-permute-start | bytes 1572872 | tf_op jit(solution)/shard_map/ppermute | solution.py:37
  143.2 22.0 %all-to-all-start.4 = ((bf16[4,160,512]{2,1,0:T(8,128)(2,1)}), bf16[4,160,512]{2,1,0:T(8,128)(2,1)S(1)}, u32[]{:S(2)}, u32[]{:S(2)}) async-start(bf16[4,160,512]{2,1,0:T(8,128)(2,1)} %get-tuple-element.66), calls=%async_computation.4 | async-start | bytes 1310720 | tf_op jit(solution)/shard_map/all_to_all | solution.py:46
  149.8 13.0 %collective-permute-start.1 = (bf16[176,512]{1,0:T(8,128)(2,1)}, bf16[176,512]{1,0:T(8,128)(2,1)S(1)}, u32[]{:S(2)}, u32[]{:S(2)}) collective-permute-start(bf16[176,512]{1,0:T(8,128)(2,1)} %get-tuple-element.74), channel_id=1, source_target_pairs={{0,1},{1,2},{2,3},{3,0},{4,5},{5,6},{6,7},{7,4},{8,9},{9,10},{10,1... | collective-permute-start | bytes 540680 | tf_op jit(solution)/shard_map/ppermute | solution.py:41
  153.2 12.0 %collective-permute-start.2 = (bf16[176,512]{1,0:T(8,128)(2,1)}, bf16[176,512]{1,0:T(8,128)(2,1)S(1)}, u32[]{:S(2)}, u32[]{:S(2)}) collective-permute-start(bf16[176,512]{1,0:T(8,128)(2,1)} %get-tuple-element.75), channel_id=1, source_target_pairs={{0,2},{1,3},{2,0},{3,1},{4,6},{5,7},{6,4},{7,5},{8,10},{9,11},{10,... | collective-permute-start | bytes 540680 | tf_op jit(solution)/shard_map/ppermute | solution.py:41
  157.5 7.7 %collective-permute-start.3 = (bf16[176,512]{1,0:T(8,128)(2,1)}, bf16[176,512]{1,0:T(8,128)(2,1)S(1)}, u32[]{:S(2)}, u32[]{:S(2)}) collective-permute-start(bf16[176,512]{1,0:T(8,128)(2,1)} %get-tuple-element.76), channel_id=1, source_target_pairs={{0,3},{1,0},{2,1},{3,2},{4,7},{5,4},{6,5},{7,6},{8,11},{9,8},{10,9... | collective-permute-start | bytes 540680 | tf_op jit(solution)/shard_map/ppermute | solution.py:41
  162.8 35.1 %copy-start.8 = (bf16[176,512]{1,0:T(8,128)(2,1)}, bf16[176,512]{1,0:T(8,128)(2,1)S(1)}, u32[]{:S(2)}) copy-start(bf16[176,512]{1,0:T(8,128)(2,1)S(1)} %collective-permute-done.1.b1_ref) | copy-start | bytes 540676
  165.2 32.7 %copy-start.9 = (bf16[176,512]{1,0:T(8,128)(2,1)}, bf16[176,512]{1,0:T(8,128)(2,1)S(1)}, u32[]{:S(2)}) copy-start(bf16[176,512]{1,0:T(8,128)(2,1)S(1)} %collective-permute-done.2.b2_ref) | copy-start | bytes 540676
  165.2 32.7 %copy-start.10 = (bf16[176,512]{1,0:T(8,128)(2,1)}, bf16[176,512]{1,0:T(8,128)(2,1)S(1)}, u32[]{:S(2)}) copy-start(bf16[176,512]{1,0:T(8,128)(2,1)S(1)} %collective-permute-done.3.b3_ref) | copy-start | bytes 540676
  165.2 0.9 copy-start.2
  171.7 11.9 %collective-permute-start.4 = (bf16[1024,512]{1,0:T(8,128)(2,1)}, bf16[1024,512]{1,0:T(8,128)(2,1)S(1)}, u32[]{:S(2)}, u32[]{:S(2)}) collective-permute-start(bf16[1024,512]{1,0:T(8,128)(2,1)} %get-tuple-element.90), channel_id=1, source_target_pairs={{0,4},{4,0},{1,5},{5,1},{2,6},{6,2},{3,7},{7,3},{8,12},{12,8},{9,1... | collective-permute-start | bytes 3145736 | tf_op jit(solution)/shard_map/ppermute | solution.py:37
  176.8 33.8 %all-to-all-start.5 = ((bf16[128,2,512]{2,1,0:T(2,128)(2,1)}), bf16[128,2,512]{2,1,0:T(2,128)(2,1)S(1)}, u32[]{:S(2)}, u32[]{:S(2)}) async-start(bf16[128,2,512]{2,1,0:T(2,128)(2,1)} %reshape.204), calls=%async_computation.5 | async-start | bytes 524288 | tf_op jit(solution)/shard_map/all_to_all | solution.py:46
  183.6 1.0 copy-start.6
  187.2 12.8 %collective-permute-start.5 = (bf16[304,512]{1,0:T(8,128)(2,1)}, bf16[304,512]{1,0:T(8,128)(2,1)S(1)}, u32[]{:S(2)}, u32[]{:S(2)}) collective-permute-start(bf16[304,512]{1,0:T(8,128)(2,1)} %get-tuple-element.93), channel_id=1, source_target_pairs={{0,1},{1,2},{2,3},{3,0},{4,5},{5,6},{6,7},{7,4},{8,9},{9,10},{10,1... | collective-permute-start | bytes 933896 | tf_op jit(solution)/shard_map/ppermute | solution.py:41
  191.4 14.7 %collective-permute-start.6 = (bf16[304,512]{1,0:T(8,128)(2,1)}, bf16[304,512]{1,0:T(8,128)(2,1)S(1)}, u32[]{:S(2)}, u32[]{:S(2)}) collective-permute-start(bf16[304,512]{1,0:T(8,128)(2,1)} %get-tuple-element.94), channel_id=1, source_target_pairs={{0,2},{1,3},{2,0},{3,1},{4,6},{5,7},{6,4},{7,5},{8,10},{9,11},{10,... | collective-permute-start | bytes 933896 | tf_op jit(solution)/shard_map/ppermute | solution.py:41
  194.6 13.1 %collective-permute-start.7 = (bf16[304,512]{1,0:T(8,128)(2,1)}, bf16[304,512]{1,0:T(8,128)(2,1)S(1)}, u32[]{:S(2)}, u32[]{:S(2)}) collective-permute-start(bf16[304,512]{1,0:T(8,128)(2,1)} %get-tuple-element.95), channel_id=1, source_target_pairs={{0,3},{1,0},{2,1},{3,2},{4,7},{5,4},{6,5},{7,6},{8,11},{9,8},{10,9... | collective-permute-start | bytes 933896 | tf_op jit(solution)/shard_map/ppermute | solution.py:41
  200.0 7.7 %copy-start.3 = (bf16[304,512]{1,0:T(8,128)(2,1)}, bf16[304,512]{1,0:T(8,128)(2,1)S(1)}, u32[]{:S(2)}) copy-start(bf16[304,512]{1,0:T(8,128)(2,1)S(1)} %collective-permute-done.5.b1_ref) | copy-start | bytes 933892
  206.1 1.6 copy-start.4
  263.7 21.1 %all-to-all-start.9 = ((bf16[8,16,3072]{2,1,0:T(8,128)(2,1)}), bf16[8,16,3072]{2,1,0:T(8,128)(2,1)S(1)}, u32[]{:S(2)}, u32[]{:S(2)}) async-start(bf16[8,16,3072]{2,1,0:T(8,128)(2,1)} %broadcast_in_dim.31), calls=%async_computation.9 | async-start | bytes 1572864 | tf_op jit(solution)/shard_map/all_to_all | solution.py:46
  284.8 0.9 copy-start
  (3 other events, 2.4 us)
Sparse Core Ops, SparseCore 0:
  10.7 41.1 all-gather.4
  54.0 35.8 all-gather.6

commit v5 on v4

--- a/solution.py
+++ b/solution.py
@@ -32,14 +32,12 @@
     )(*operands)
 
 
-def onward(keep, give, tail):
+def over_feat(keep, give, tail):
     n = lax.axis_size("y")
     given = lax.ppermute(give, "c", [(0, 1), (1, 0)])
-    size = (keep.shape[0] + tail.shape[0]) // n
-    blocks = call(merge_kernel, [((size, keep.shape[1]), BF)] * n, keep, given, tail)
-    return [blocks[0]] + [
-        lax.ppermute(blocks[k], "y", [(i, (i + k) % n) for i in range(n)]) for k in range(1, n)
-    ]
+    size = (keep.shape[0] + tail.shape[0], keep.shape[1])
+    (both,) = call(functools.partial(merge_kernel, n), [(size, BF)], keep, given, tail)
+    return lax.psum_scatter(both, "y", scatter_dimension=0, tiled=True)
 
 
 def exchange(array, axes):
@@ -182,26 +180,24 @@
     count = term_ref.shape[0] // rows
     half = rows // 2
     held = tail_ref.shape[0] // count
-    me, core = me_ref[0], me_ref[1]
-    for k in range(count):
-        to = lax.rem(me + k, count)
+    core = me_ref[1]
+    for y in range(count):
         for ref, side in ((keep_ref, core), (give_ref, 1 - core)):
-            at = pl.ds(pl.multiple_of(to * rows + side * half, half), half)
+            at = pl.ds(pl.multiple_of(y * rows + side * half, half), half)
             for t in range(terms):
-                place = (k * terms + t) * half
+                place = (y * terms + t) * half
                 ref[place : place + half, :] = term_ref[at, t * width : (t + 1) * width]
-        block = node_ref[pl.ds(pl.multiple_of(to * own, 8), own), :]
+        block = node_ref[y * own : (y + 1) * own, :]
         block = jnp.concatenate([block, jnp.zeros((held - own, width), F32)], axis=0)
-        tail_ref[k * held : (k + 1) * held, :] = block.astype(BF)
-
-
-def merge_kernel(keep_ref, given_ref, tail_ref, *out_refs):
-    count = len(out_refs)
+        tail_ref[y * held : (y + 1) * held, :] = block.astype(BF)
+
+
+def merge_kernel(count, keep_ref, given_ref, tail_ref, out_ref):
     size, held = keep_ref.shape[0] // count, tail_ref.shape[0] // count
-    for k, ref in enumerate(out_refs):
-        at = slice(k * size, (k + 1) * size)
-        ref[:size, :] = total_of([keep_ref[at, :], given_ref[at, :]]).astype(BF)
-        ref[size:, :] = tail_ref[k * held : (k + 1) * held, :]
+    for y in range(count):
+        at, start = slice(y * size, (y + 1) * size), y * (size + held)
+        out_ref[start : start + size, :] = total_of([keep_ref[at, :], given_ref[at, :]]).astype(BF)
+        out_ref[start + size : start + size + held, :] = tail_ref[y * held : (y + 1) * held, :]
 
 
 def process_kernel(
@@ -290,31 +286,27 @@
     out_ref[...] = dot(slots_hot(send_ref[...], nodes), grads).astype(BF)
 
 
-def out_kernel(me_ref, latent_ref, b0_ref, b1_ref, b2_ref, b3_ref, out_ref, sum_ref):
-    total = total_of([b0_ref[...], b1_ref[...], b2_ref[...], b3_ref[...]])
-    size = sum_ref.shape[0]
-    sum_ref[...] = total[:size].astype(BF)
+def out_kernel(me_ref, latent_ref, first_ref, out_ref):
     own, nodes = out_ref.shape[0], latent_ref.shape[0]
+    held = own + (-own % PAD)
     mine = lax.broadcasted_iota(jnp.int32, (1, own), 1) + me_ref[0] * own
     latent = outer(one_hot(mine, nodes), latent_ref[...])
-    out_ref[...] = (latent + total[size : size + own]).astype(BF)
-
-
-def level_kernel(sum_ref, b0_ref, b1_ref, b2_ref, b3_ref, out_ref):
-    width = sum_ref.shape[1]
+    out_ref[...] = (latent + first_ref[first_ref.shape[0] - held :, :].astype(F32)[:own]).astype(BF)
+
+
+def level_kernel(first_ref, second_ref, out_ref):
+    width = first_ref.shape[1]
     half = out_ref.shape[0]
-    for k in range(4):
-        at = slice(k * half, (k + 1) * half)
-        block = total_of([b0_ref[at, :], b1_ref[at, :], b2_ref[at, :], b3_ref[at, :]])
-        out_ref[:, k * width : (k + 1) * width] = block.astype(BF)
-    for k in range(2):
-        out_ref[:, (4 + k) * width : (5 + k) * width] = sum_ref[k * half : (k + 1) * half, :]
-
-
-def mesh_kernel(rows, me_ref, node_ref, enc_ref, b0_ref, b1_ref, b2_ref, b3_ref, mesh_ref):
+    for k in range(6):
+        ref, t = (second_ref, k) if k < 4 else (first_ref, k - 4)
+        out_ref[:, k * width : (k + 1) * width] = ref[t * half : (t + 1) * half, :]
+
+
+def mesh_kernel(rows, me_ref, node_ref, enc_ref, second_ref, mesh_ref):
     own = mesh_ref.shape[0]
-    total = total_of([b[2 * rows :, :] for b in (b0_ref, b1_ref, b2_ref, b3_ref)])
-    back = dot_t(total.astype(BF), whole(enc_ref, 1, rows))[:own]
+    held = own + (-own % PAD)
+    total = second_ref[second_ref.shape[0] - held :, :]
+    back = dot_t(total, whole(enc_ref, 1, rows))[:own]
     node = node_ref[pl.ds(pl.multiple_of(me_ref[0] * own, 8), own), :]
     mesh_ref[...] = (node + back).astype(BF)
 
@@ -442,7 +434,7 @@
         me=me,
         scratch=[pltpu.VMEM((width, 2 * width), BF)],
     )
-    first = onward(*first)
+    first = over_feat(*first)
     node_part, at_src = call(
         bind(owner_kernel, rows),
         [all_sums, one_sum],
@@ -455,7 +447,6 @@
     )
 
     node_in = exchange(node_part, "y")
-    node_in, *first = lax.optimization_barrier((node_in, *first))
 
     node_grad, slot_out, *second = call(
         bind(backward_kernel, rows, own),
@@ -480,11 +471,8 @@
         scratch=[pltpu.VMEM((width, 4 * width), BF), pltpu.VMEM((nodes, width), F32)],
     )
     slot_back = exchange(slot_out.reshape(dom, caps, width), DOM)
-    second = onward(*second)
-    out_rows, first_sum = call(
-        out_kernel, [((own, width), BF), ((rows, width), BF)], latent, *first, me=me
-    )
-    (level,) = call(level_kernel, [((rows // 2, 6 * width), BF)], first_sum, *second)
+    second = over_feat(*second)
+    (level,) = call(level_kernel, [((rows // 2, 6 * width), BF)], first, second)
     slot_back, level = lax.optimization_barrier((slot_back, level))
     across = lax.axis_size("x")
     thin = rows // (2 * across)
@@ -497,8 +485,9 @@
     near = lax.axis_size(("x", "c"))
     totals = exchange(jnp.broadcast_to(level[None], (near, *level.shape)), ("c", "x"))
     totals = call(bind(split_kernel, factor), [((rows, width), F32)] * 6, totals)
+    (out_rows,) = call(out_kernel, [((own, width), BF)], latent, first, me=me)
     (g_mesh,) = call(
-        bind(mesh_kernel, rows), [((own, width), BF)], node_grad, enc_gath, *second, me=me
+        bind(mesh_kernel, rows), [((own, width), BF)], node_grad, enc_gath, second, me=me
     )
     (g_grid,) = call(
         bind(grid_kernel, rows),

time: 297 us -> 293 us (0.987)
  waiting for transfers between devices: 51.9 us -> 72.8 us
  starting transfers between devices: 73.7 us -> 52.9 us
    reduce_scatter x0 -> x2, waiting for transfers between devices: none -> 24.8 us  [over_feat(): return lax.psum_scatter(both, 'y', scatter_dimension=0, tiled=True)]
    ppermute x8 -> x2, starting transfers between devices: 27.3 us -> 5.91 us  [over_feat(): given = lax.ppermute(give, 'c', [(0, 1), (1, 0)])]
    ppermute x8 -> x2, waiting for transfers between devices: 12.3 us -> 2.48 us  [over_feat(): given = lax.ppermute(give, 'c', [(0, 1), (1, 0)])]
    all_to_all x6, waiting for transfers between devices: 38.9 us -> 44.8 us  [exchange(): return lax.all_to_all(array, axes, 0, 0, tiled=True)]
    unnamed x27 -> x17, local copies, waits for them, and re-layouts: 7.95 us -> 7.19 us
  transfers between devices with their start and end apart: 16 -> 12, of which waited for: 8 -> 7; matrix products, arithmetic and copies ran while one was open for 3% -> 3% of each run, Pallas kernels for 9% -> 11%
where the time goes in v5:
time: 293 us; the launch traced here: 292 us
  blocking collectives  89.9 us (31%)
  waiting for transfers between devices  72.8 us (25%)
  starting transfers between devices  52.9 us (18%)
  Pallas kernels  45.4 us (15%)
  local copies, waits for them, and re-layouts  14.6 us (5%)
  between operations  13.9 us (5%)
    all_to_all x4, blocking collectives, exchange(): return lax.all_to_all(array, axes, 0, 0, tiled=True)  89.9 us
    all_to_all x6, starting transfers between devices, exchange(): return lax.all_to_all(array, axes, 0, 0, tiled=True)  46.8 us
    pallas_call x15, Pallas kernels, call(): pl.pallas_call(kernel, out_shape=tuple((jax.ShapeDtypeStruct(s, d) for s,...  45.4 us
    all_to_all x6, waiting for transfers between devices, exchange(): return lax.all_to_all(array, axes, 0, 0, tiled=True)  44.8 us
    reduce_scatter x2, waiting for transfers between devices, over_feat(): return lax.psum_scatter(both, 'y', scatter_dimension=0, tiled=True)  24.8 us
    unnamed x17, local copies, waits for them, and re-layouts  7.19 us
    ppermute x2, starting transfers between devices, over_feat(): given = lax.ppermute(give, 'c', [(0, 1), (1, 0)])  5.91 us
  transfers between devices with their start and end apart: 12, of which 7 were waited for; matrix products, arithmetic and copies ran while one was open for 3% of the time, Pallas kernels for 11%

profile of v5, /device:TPU:1, one launch (start us, length us, event | category | flops | bytes accessed | tf_op | source)
XLA Modules:
  0.0 292.1 jit_solution(7801168204036956542)
XLA Ops:
  11.7 40.7 %all_to_all.50 = bf16[128,2,512]{2,1,0:T(2,128)(2,1)S(1)} all-to-all(bf16[128,2,512]{2,1,0:T(2,128)(2,1)S(1)} %reshape.198), channel_id=1, replica_groups=mesh['z'=16,'x'=4,'c'=2,'y'=4] {'z','x','c'}, dimensions={0} | all-to-all | bytes 524288 | tf_op jit(solution)/shard_map/all_to_all | solution.py:44
  53.2 3.7 %shard_map.206 = (bf16[4,160,512]{2,1,0:T(8,128)(2,1)}, f32[256,512]{1,0:T(8,128)}, f32[256,512]{1,0:T(8,128)}, f32[256,1]{1,0:T(8,128)}) custom-call(bf16[128,1024]{1,0:T(8,128)(2,1)} %bitcast.29, s32[2,128]{1,0:T(2,128)} %bitcast.45, bf16[4,432,512]{2,1,0:T(8,128)(2,1)} %bitcast.20), custom_call_target="tpu_custom_call" | custom-call | tf_op jit(solution)/shard_map/pallas_call | solution.py:25
  56.9 4.2 %all-to-all-start.1 = ((bf16[4,160,512]{2,1,0:T(8,128)(2,1)}), bf16[4,160,512]{2,1,0:T(8,128)(2,1)S(1)}, u32[]{:S(2)}, u32[]{:S(2)}) async-start(bf16[4,160,512]{2,1,0:T(8,128)(2,1)} %get-tuple-element.44), calls=%async_computation.1 | async-start | bytes 1310720 | tf_op jit(solution)/shard_map/all_to_all | solution.py:44
  62.5 8.7 %all-to-all-done.1.sums_ref = bf16[4,160,512]{2,1,0:T(8,128)(2,1)S(1)} async-done(((bf16[4,160,512]{2,1,0:T(8,128)(2,1)}), bf16[4,160,512]{2,1,0:T(8,128)(2,1)S(1)}, u32[]{:S(2)}, u32[]{:S(2)}) %all-to-all-start.1) | async-done | bytes 655392 | tf_op jit(solution)/shard_map/all_to_all | solution.py:44
  76.3 15.6 %all-to-all-start.2 = ((bf16[128,2,256]{2,1,0:T(2,128)(2,1)}), bf16[128,2,256]{2,1,0:T(2,128)(2,1)S(1)}, u32[]{:S(2)}, u32[]{:S(2)}) async-start(bf16[128,2,256]{2,1,0:T(2,128)(2,1)} %reshape.200), calls=%async_computation.2 | async-start | bytes 262144 | tf_op jit(solution)/shard_map/all_to_all | solution.py:44
  93.3 14.6 %all-to-all-done.2 = bf16[128,2,256]{2,1,0:T(2,128)(2,1)S(1)} async-done(((bf16[128,2,256]{2,1,0:T(2,128)(2,1)}), bf16[128,2,256]{2,1,0:T(2,128)(2,1)S(1)}, u32[]{:S(2)}, u32[]{:S(2)}) %all-to-all-start.2) | async-done | bytes 131104 | tf_op jit(solution)/shard_map/all_to_all | solution.py:44
  108.6 6.0 %shard_map.208 = (bf16[128,512]{1,0:T(8,128)(2,1)}, f32[160,512]{1,0:T(8,128)}, bf16[160,512]{1,0:T(8,128)(2,1)}, f32[160,512]{1,0:T(8,128)}, bf16[640,512]{1,0:T(8,128)(2,1)}, /*index=5*/bf16[640,512]{1,0:T(8,128)(2,1)}) custom-call(bf16[160,512]{1,0:T(8,128)(2,1)} %get-tuple-element.45.latent_ref, bf16[128,512]{1,0:T(8,128)(2,1)} %bitcast.35, ...), custom_call_target="tpu_custom_call" | custom-call | tf_op jit(solution)/shard_map/pallas_call | solution.py:25
  116.2 7.2 %all-to-all-start.3 = ((bf16[128,2,256]{2,1,0:T(2,128)(2,1)}), bf16[128,2,256]{2,1,0:T(2,128)(2,1)S(1)}, u32[]{:S(2)}, u32[]{:S(2)}) async-start(bf16[128,2,256]{2,1,0:T(2,128)(2,1)} %reshape.202), calls=%async_computation.4 | async-start | bytes 262144 | tf_op jit(solution)/shard_map/all_to_all | solution.py:44
  123.3 3.4 %shard_map.209 = (bf16[512,512]{1,0:T(8,128)(2,1)}, bf16[512,512]{1,0:T(8,128)(2,1)}, bf16[192,512]{1,0:T(8,128)(2,1)}) custom-call(s32[2]{0:T(128)} %pad_add_fusion.me_ref, bf16[160,512]{1,0:T(8,128)(2,1)} %get-tuple-element.45.latent_ref, bf16[160,512]{1,0:T(8,128)(2,1)} %get-tuple-element.48.dst_ref, bf16[640,512]{1,0:T(8,128)(2,1)} %get-tuple-element.49.hidden_ref, ...), custom_call_target="tpu_custom_call" | custom-call | tf_op jit(solution)/shard_map/pallas_call | solution.py:25
  129.5 9.9 %all-to-all-done.3 = bf16[128,2,256]{2,1,0:T(2,128)(2,1)S(1)} async-done(((bf16[128,2,256]{2,1,0:T(2,128)(2,1)}), bf16[128,2,256]{2,1,0:T(2,128)(2,1)S(1)}, u32[]{:S(2)}, u32[]{:S(2)}) %all-to-all-start.3) | async-done | bytes 131104 | tf_op jit(solution)/shard_map/all_to_all | solution.py:44
  140.0 3.1 %shard_map.212 = (bf16[4,160,512]{2,1,0:T(8,128)(2,1)}, bf16[160,512]{1,0:T(8,128)(2,1)}) custom-call(s32[2]{0:T(128)} %pad_add_fusion.me_ref, bf16[128,512]{1,0:T(8,128)(2,1)} %bitcast.36, s32[4,128]{1,0:T(4,128)} %bitcast.42, f32[160,512]{1,0:T(8,128)} %get-tuple-element.56.local_ref, bf16[160,512]{1,0:T(8,128)(2,1)} %get-tuple-element.48.dst_ref, ...), custom_call_target="tpu_custom_call" | custom-call | tf_op jit(solution)/shard_map/pallas_call | solution.py:25
  143.1 3.7 %all-to-all-start.4 = ((bf16[4,160,512]{2,1,0:T(8,128)(2,1)}), bf16[4,160,512]{2,1,0:T(8,128)(2,1)S(1)}, u32[]{:S(2)}, u32[]{:S(2)}) async-start(bf16[4,160,512]{2,1,0:T(8,128)(2,1)} %get-tuple-element.57), calls=%async_computation.5 | async-start | bytes 1310720 | tf_op jit(solution)/shard_map/all_to_all | solution.py:44
  150.0 7.4 %all-to-all-done.4.sums_ref = bf16[4,160,512]{2,1,0:T(8,128)(2,1)S(1)} async-done(((bf16[4,160,512]{2,1,0:T(8,128)(2,1)}), bf16[4,160,512]{2,1,0:T(8,128)(2,1)S(1)}, u32[]{:S(2)}, u32[]{:S(2)}) %all-to-all-start.4) | async-done | bytes 655392 | tf_op jit(solution)/shard_map/all_to_all | solution.py:44
  158.2 5.8 %shard_map.213 = (f32[160,512]{1,0:T(8,128)}, bf16[128,1024]{1,0:T(8,128)(2,1)}, bf16[1024,512]{1,0:T(8,128)(2,1)}, bf16[1024,512]{1,0:T(8,128)(2,1)}, bf16[192,512]{1,0:T(8,128)(2,1)}) custom-call(s32[2]{0:T(128)} %pad_add_fusion.me_ref, bf16[4,160,512]{2,1,0:T(8,128)(2,1)} %copy-done.2, bf16[4,432,512]{2,1,0:T(8,128)(2,1)} %bitcast.28, ...), custom_call_target="tpu_custom_call" | custom-call | tf_op jit(solution)/shard_map/pallas_call | solution.py:25
  164.0 3.1 %collective-permute-start.1 = (bf16[1024,512]{1,0:T(8,128)(2,1)}, bf16[1024,512]{1,0:T(8,128)(2,1)S(1)}, u32[]{:S(2)}, u32[]{:S(2)}) collective-permute-start(bf16[1024,512]{1,0:T(8,128)(2,1)} %get-tuple-element.64), channel_id=1, source_target_pairs={{0,4},{4,0},{1,5},{5,1},{2,6},{6,2},{3,7},{7,3},{8,12},{12,8},{9,1... | collective-permute-start | bytes 3145736 | tf_op jit(solution)/shard_map/ppermute | solution.py:37
  170.6 2.9 shard_map.214
  174.4 6.9 %all-to-all-start.5 = ((bf16[128,2,512]{2,1,0:T(2,128)(2,1)}), bf16[128,2,512]{2,1,0:T(2,128)(2,1)S(1)}, u32[]{:S(2)}, u32[]{:S(2)}) async-start(bf16[128,2,512]{2,1,0:T(2,128)(2,1)} %reshape.204), calls=%async_computation.6 | async-start | bytes 524288 | tf_op jit(solution)/shard_map/all_to_all | solution.py:44
  181.4 24.8 %reduce-scatter.5.cloned.1.call-done.second_ref = bf16[304,512]{1,0:T(8,128)(2,1)} async-done(((bf16[1216,512]{1,0:T(8,128)(2,1)}), bf16[304,512]{1,0:T(8,128)(2,1)}) %reduce-scatter.5.cloned.1.call-update) | async-done | bytes 311312 | tf_op jit(solution)/shard_map/reduce_scatter | solution.py:40
  208.0 10.4 %all_to_all.51.in_ref = bf16[4,16,3072]{2,1,0:T(8,128)(2,1)} all-to-all(bf16[4,16,3072]{2,1,0:T(8,128)(2,1)} %bitcast.31), channel_id=1, replica_groups=mesh['z'=16,'x'=4,'c'=2,'y'=4] {'x'}, dimensions={0} | all-to-all | bytes 786432 | tf_op jit(solution)/shard_map/all_to_all | solution.py:44
  221.0 23.7 %all_to_all.52 = bf16[16,2,1536]{2,1,0:T(2,128)(2,1)S(1)} all-to-all(bf16[16,2,1536]{2,1,0:T(2,128)(2,1)S(1)} %reshape.207), channel_id=1, replica_groups=mesh['z'=16,'x'=4,'c'=2,'y'=4] {'z'}, dimensions={0} | all-to-all | bytes 196608 | tf_op jit(solution)/shard_map/all_to_all | solution.py:44
  244.8 15.1 %all_to_all.53 = bf16[16,2,1536]{2,1,0:T(2,128)(2,1)S(1)} all-to-all(bf16[16,2,1536]{2,1,0:T(2,128)(2,1)S(1)} %broadcast_in_dim.29), channel_id=1, replica_groups=mesh['z'=16,'x'=4,'c'=2,'y'=4] {'z'}, dimensions={0} | all-to-all | bytes 196608 | tf_op jit(solution)/shard_map/all_to_all | solution.py:44
  260.9 9.2 %all-to-all-start.9 = ((bf16[8,16,3072]{2,1,0:T(8,128)(2,1)}), bf16[8,16,3072]{2,1,0:T(8,128)(2,1)S(1)}, u32[]{:S(2)}, u32[]{:S(2)}) async-start(bf16[8,16,3072]{2,1,0:T(8,128)(2,1)} %broadcast_in_dim.31), calls=%async_computation.11 | async-start | bytes 1572864 | tf_op jit(solution)/shard_map/all_to_all | solution.py:44
  272.7 3.0 %shard_map.216 = bf16[512,512]{1,0:T(8,128)(2,1)} custom-call(bf16[128,1024]{1,0:T(8,128)(2,1)} %bitcast.32, s32[2,128]{1,0:T(2,128)} %bitcast.44, bf16[4,432,512]{2,1,0:T(8,128)(2,1)} %bitcast.24), custom_call_target="tpu_custom_call" | custom-call | tf_op jit(solution)/shard_map/pallas_call | solution.py:25
  278.2 4.2 %all-to-all-done.9.in_ref = bf16[8,16,3072]{2,1,0:T(8,128)(2,1)S(1)} async-done(((bf16[8,16,3072]{2,1,0:T(8,128)(2,1)}), bf16[8,16,3072]{2,1,0:T(8,128)(2,1)S(1)}, u32[]{:S(2)}, u32[]{:S(2)}) %all-to-all-start.9) | async-done | bytes 786464 | tf_op jit(solution)/shard_map/all_to_all | solution.py:44
  (57 shorter events, 41.1 us)
Async XLA Ops:
  7.2 46.0 %all-gather.5.cloned.1.call-start = ((), (), s32[]{:S(2)}) async-start(), calls=%async_computation.14 | async-start | bytes 2211840 | tf_op jit(solution)/shard_map/all_gather | solution.py:381
  9.8 98.8 %all-gather.7.cloned.1.call-start = ((), (), s32[]{:S(2)}) async-start(), calls=%async_computation.15 | async-start | bytes 2211840 | tf_op jit(solution)/shard_map/all_gather | solution.py:382
  56.9 14.3 %all-to-all-start.1 = ((bf16[4,160,512]{2,1,0:T(8,128)(2,1)}), bf16[4,160,512]{2,1,0:T(8,128)(2,1)S(1)}, u32[]{:S(2)}, u32[]{:S(2)}) async-start(bf16[4,160,512]{2,1,0:T(8,128)(2,1)} %get-tuple-element.44), calls=%async_computation.1 | async-start | bytes 1310720 | tf_op jit(solution)/shard_map/all_to_all | solution.py:44
  71.2 0.8 copy-start.1
  76.3 31.7 %all-to-all-start.2 = ((bf16[128,2,256]{2,1,0:T(2,128)(2,1)}), bf16[128,2,256]{2,1,0:T(2,128)(2,1)S(1)}, u32[]{:S(2)}, u32[]{:S(2)}) async-start(bf16[128,2,256]{2,1,0:T(2,128)(2,1)} %reshape.200), calls=%async_computation.2 | async-start | bytes 262144 | tf_op jit(solution)/shard_map/all_to_all | solution.py:44
  116.2 23.2 %all-to-all-start.3 = ((bf16[128,2,256]{2,1,0:T(2,128)(2,1)}), bf16[128,2,256]{2,1,0:T(2,128)(2,1)S(1)}, u32[]{:S(2)}, u32[]{:S(2)}) async-start(bf16[128,2,256]{2,1,0:T(2,128)(2,1)} %reshape.202), calls=%async_computation.4 | async-start | bytes 262144 | tf_op jit(solution)/shard_map/all_to_all | solution.py:44
  126.7 20.2 %collective-permute-start = (bf16[512,512]{1,0:T(8,128)(2,1)}, bf16[512,512]{1,0:T(8,128)(2,1)S(1)}, u32[]{:S(2)}, u32[]{:S(2)}) collective-permute-start(bf16[512,512]{1,0:T(8,128)(2,1)} %get-tuple-element.53), channel_id=1, source_target_pairs={{0,4},{4,0},{1,5},{5,1},{2,6},{6,2},{3,7},{7,3},{8,12},{12,8},{9,1... | collective-permute-start | bytes 1572872 | tf_op jit(solution)/shard_map/ppermute | solution.py:37
  143.1 14.2 %all-to-all-start.4 = ((bf16[4,160,512]{2,1,0:T(8,128)(2,1)}), bf16[4,160,512]{2,1,0:T(8,128)(2,1)S(1)}, u32[]{:S(2)}, u32[]{:S(2)}) async-start(bf16[4,160,512]{2,1,0:T(8,128)(2,1)} %get-tuple-element.57), calls=%async_computation.5 | async-start | bytes 1310720 | tf_op jit(solution)/shard_map/all_to_all | solution.py:44
  146.8 34.6 %reduce-scatter.3.cloned.1.call-start = ((), (), s32[]{:S(2)}) async-start(), calls=%async_computation.12 | async-start | bytes 901120 | tf_op jit(solution)/shard_map/reduce_scatter | solution.py:40
  146.9 0.8 copy-start.4
  149.9 56.2 %reduce-scatter.5.cloned.1.call-start = ((), (), s32[]{:S(2)}) async-start(), calls=%async_computation.13 | async-start | bytes 1556480 | tf_op jit(solution)/shard_map/reduce_scatter | solution.py:40
  157.4 0.8 copy-start.2
  164.0 5.6 %collective-permute-start.1 = (bf16[1024,512]{1,0:T(8,128)(2,1)}, bf16[1024,512]{1,0:T(8,128)(2,1)S(1)}, u32[]{:S(2)}, u32[]{:S(2)}) collective-permute-start(bf16[1024,512]{1,0:T(8,128)(2,1)} %get-tuple-element.64), channel_id=1, source_target_pairs={{0,4},{4,0},{1,5},{5,1},{2,6},{6,2},{3,7},{7,3},{8,12},{12,8},{9,1... | collective-permute-start | bytes 3145736 | tf_op jit(solution)/shard_map/ppermute | solution.py:37
  169.6 1.0 copy-start.3
  170.6 2.9 copy-start.5
  174.4 33.6 %all-to-all-start.5 = ((bf16[128,2,512]{2,1,0:T(2,128)(2,1)}), bf16[128,2,512]{2,1,0:T(2,128)(2,1)S(1)}, u32[]{:S(2)}, u32[]{:S(2)}) async-start(bf16[128,2,512]{2,1,0:T(2,128)(2,1)} %reshape.204), calls=%async_computation.6 | async-start | bytes 524288 | tf_op jit(solution)/shard_map/all_to_all | solution.py:44
  260.9 21.4 %all-to-all-start.9 = ((bf16[8,16,3072]{2,1,0:T(8,128)(2,1)}), bf16[8,16,3072]{2,1,0:T(8,128)(2,1)S(1)}, u32[]{:S(2)}, u32[]{:S(2)}) async-start(bf16[8,16,3072]{2,1,0:T(8,128)(2,1)} %broadcast_in_dim.31), calls=%async_computation.11 | async-start | bytes 1572864 | tf_op jit(solution)/shard_map/all_to_all | solution.py:44
  282.3 0.9 copy-start
Sparse Core Ops, SparseCore 0:
  10.7 41.1 all-gather.4
  54.0 35.8 all-gather.6
  150.5 21.1 reduce-scatter.2
  174.4 31.7 reduce-scatter.4

commit v6 on v5

--- a/solution.py
+++ b/solution.py
@@ -32,12 +32,20 @@
     )(*operands)
 
 
-def over_feat(keep, give, tail):
-    n = lax.axis_size("y")
+def over_cores(keep, give, tail):
     given = lax.ppermute(give, "c", [(0, 1), (1, 0)])
     size = (keep.shape[0] + tail.shape[0], keep.shape[1])
-    (both,) = call(functools.partial(merge_kernel, n), [(size, BF)], keep, given, tail)
-    return lax.psum_scatter(both, "y", scatter_dimension=0, tiled=True)
+    kernel = functools.partial(merge_kernel, lax.axis_size("y"))
+    return call(kernel, [(size, BF)], keep, given, tail)[0]
+
+
+def onward(array, me):
+    n = lax.axis_size("y")
+    size = (array.shape[0] // n, array.shape[1])
+    blocks = call(deal_out_kernel, [(size, BF)] * n, array, me=me)
+    return [blocks[0]] + [
+        lax.ppermute(blocks[k], "y", [(i, (i + k) % n) for i in range(n)]) for k in range(1, n)
+    ]
 
 
 def exchange(array, axes):
@@ -102,7 +110,7 @@
 
 
 def pack_kernel(
-    send_ref, grid_ref, src_ref, dst_ref, wg_ref, wm_ref, we_ref, ws_ref, wd_ref, wp_ref, mesh_ref, cot_ref,
+    send_ref, grid_ref, src_ref, dst_ref, wg_ref, wm_ref, ws_ref, wd_ref, wp_ref, mesh_ref, cot_ref,
     out_ref, enc_ref, proc_ref, line_ref,
 ):
     grid = grid_ref[...]
@@ -120,13 +128,13 @@
     line_ref[:, :edges] = jnp.where(place < 3, values, 0).astype(F32)
     rows = wg_ref.shape[0]
     for ref, arrays, tail in (
-        (enc_ref, (wg_ref, wm_ref, we_ref), mesh_ref),
+        (enc_ref, (wg_ref, wm_ref), mesh_ref),
         (proc_ref, (ws_ref, wd_ref, wp_ref), cot_ref),
     ):
         for k, array in enumerate(arrays):
             ref[k * rows : (k + 1) * rows, :] = array[...]
         both = jnp.concatenate([tail[...].astype(F32), line_ref[...]], axis=0)
-        ref[3 * rows :, :] = both.astype(BF)
+        ref[len(arrays) * rows :, :] = both.astype(BF)
 
 
 def node_rows(gath_ref, at, own):
@@ -148,9 +156,9 @@
     return total
 
 
-def encode_kernel(rows, own, recv_ref, dst_ref, gath_ref, sum_ref, pre_ref, norm_ref, scale_ref):
+def encode_kernel(rows, own, recv_ref, dst_ref, gath_ref, w_ref, sum_ref, pre_ref, norm_ref, scale_ref):
     width = gath_ref.shape[2]
-    mesh_part = node_rows(gath_ref, 3 * rows, own).astype(BF)
+    mesh_part = node_rows(gath_ref, 2 * rows, own).astype(BF)
     received = slot_rows(recv_ref[...], width)
     hot = slots_hot(dst_ref[...], mesh_part.shape[0])
     projected = dot(received, whole(gath_ref, 0, rows)).astype(BF)
@@ -158,7 +166,7 @@
     preact = projected.astype(F32) + dot(nodes, whole(gath_ref, 1, rows))
     pre_ref[...] = preact
     hidden = (preact * sigmoid(preact)).astype(BF)
-    normed, scaling = layer_norm(dot(hidden, whole(gath_ref, 2, rows)))
+    normed, scaling = layer_norm(dot(hidden, w_ref[...]))
     norm_ref[...] = normed
     scale_ref[...] = scaling
     partial_sum = dot(hot, normed.astype(BF)).astype(BF)
@@ -168,7 +176,7 @@
 
 def latent_kernel(rows, own, me_ref, sums_ref, gath_ref, send_ref, latent_ref, halo_ref):
     total = total_of([sums_ref[y] for y in range(sums_ref.shape[0])])
-    latent = (node_rows(gath_ref, 3 * rows, own) + total).astype(BF)
+    latent = (node_rows(gath_ref, 2 * rows, own) + total).astype(BF)
     latent_ref[...] = latent
     hot = one_hot(own_row(send_ref, me_ref[0]), latent.shape[0])
     halo_ref[...] = outer(hot, latent).astype(BF)
@@ -249,7 +257,7 @@
 
 
 def backward_kernel(
-    rows, own, me_ref, sums_ref, proc_ref, latent_ref, src_ref, enc_ref, recv_ref, dst_ref,
+    rows, own, me_ref, sums_ref, proc_ref, latent_ref, src_ref, enc_ref, w_ref, recv_ref, dst_ref,
     pre_ref, norm_ref, scale_ref,
     node_ref, slot_ref, keep_ref, give_ref, tail_ref, term_ref, share_ref,
 ):
@@ -264,14 +272,14 @@
     preact = pre_ref[...]
     gate = sigmoid(preact)
     hidden = (preact * gate).astype(BF)
-    grad = dot_t(mid, whole(enc_ref, 2, rows)) * (gate * (1.0 + preact * (1.0 - gate)))
+    grad = dot_t(mid, w_ref[...]) * (gate * (1.0 + preact * (1.0 - gate)))
     grad = grad.astype(BF)
     slot_ref[...] = wide_rows(grad, recv_ref.shape[1] // width)
     at_node = dot(hot, grad)
     share_ref[...] = at_node
     terms = (
         outer(slot_rows(recv_ref[...], width), grad),
-        outer(node_rows(enc_ref, 3 * rows, own).astype(BF), at_node.astype(BF)),
+        outer(node_rows(enc_ref, 2 * rows, own).astype(BF), at_node.astype(BF)),
         outer(hidden, mid),
         outer(latent_ref[...], src_ref[...]),
     )
@@ -286,20 +294,32 @@
     out_ref[...] = dot(slots_hot(send_ref[...], nodes), grads).astype(BF)
 
 
-def out_kernel(me_ref, latent_ref, first_ref, out_ref):
+def out_kernel(me_ref, latent_ref, b0_ref, b1_ref, b2_ref, b3_ref, out_ref):
     own, nodes = out_ref.shape[0], latent_ref.shape[0]
-    held = own + (-own % PAD)
+    start = b0_ref.shape[0] - own - (-own % PAD)
+    total = total_of([b[start:, :] for b in (b0_ref, b1_ref, b2_ref, b3_ref)])
     mine = lax.broadcasted_iota(jnp.int32, (1, own), 1) + me_ref[0] * own
     latent = outer(one_hot(mine, nodes), latent_ref[...])
-    out_ref[...] = (latent + first_ref[first_ref.shape[0] - held :, :].astype(F32)[:own]).astype(BF)
-
-
-def level_kernel(first_ref, second_ref, out_ref):
-    width = first_ref.shape[1]
+    out_ref[...] = (latent + total[:own]).astype(BF)
+
+
+def level_kernel(second_ref, b0_ref, b1_ref, b2_ref, b3_ref, out_ref):
+    width = second_ref.shape[1]
     half = out_ref.shape[0]
-    for k in range(6):
-        ref, t = (second_ref, k) if k < 4 else (first_ref, k - 4)
-        out_ref[:, k * width : (k + 1) * width] = ref[t * half : (t + 1) * half, :]
+    for k in range(4):
+        out_ref[:, k * width : (k + 1) * width] = second_ref[k * half : (k + 1) * half, :]
+    for k in range(2):
+        at = slice(k * half, (k + 1) * half)
+        block = total_of([b[at, :] for b in (b0_ref, b1_ref, b2_ref, b3_ref)])
+        out_ref[:, (4 + k) * width : (5 + k) * width] = block.astype(BF)
+
+
+def deal_out_kernel(me_ref, in_ref, *out_refs):
+    count = len(out_refs)
+    size = out_refs[0].shape[0]
+    for k, ref in enumerate(out_refs):
+        to = lax.rem(me_ref[0] + k, count)
+        ref[...] = in_ref[pl.ds(pl.multiple_of(to * size, PAD), size), :]
 
 
 def mesh_kernel(rows, me_ref, node_ref, enc_ref, second_ref, mesh_ref):
@@ -359,17 +379,20 @@
         raise ValueError("sizes")
     bind = functools.partial
 
-    packed = ((3 * rows + held, width), BF)
+    half = rows // 2
     outgoing, enc_pack, proc_pack = call(
         pack_kernel,
-        [((dom, caps * width), BF), packed, packed],
+        [
+            ((dom, caps * width), BF),
+            ((2 * rows + held, width), BF),
+            ((3 * rows + held, width), BF),
+        ],
         enc_send,
         grid_feat,
         proc_src.reshape(1, edges),
         proc_dst.reshape(1, edges),
         w_grid,
         w_mesh,
-        w_enc2,
         w_src,
         w_dst,
         w_proc2,
@@ -379,16 +402,23 @@
     )
     received = exchange(outgoing.reshape(dom, caps, width), DOM).reshape(dom, caps * width)
     enc_gath = lax.all_gather(enc_pack, "y", axis=0)
+    full_enc2 = lax.all_gather(w_enc2, "y", axis=0, tiled=True)
     proc_gath = lax.all_gather(proc_pack, "y", axis=0)
 
     slots = dom * caps
     one_sum, all_sums = ((nodes, width), BF), ((feat, nodes, width), BF)
     partial_sum, preact, normed, scaling = call(
         bind(encode_kernel, rows, own),
-        [all_sums, ((slots, width), F32), ((slots, width), F32), ((slots, 1), F32)],
+        [
+            all_sums,
+            ((slots, width), F32),
+            ((slots, width), F32),
+            ((slots, 1), F32),
+        ],
         received,
         enc_dst,
         enc_gath,
+        full_enc2,
     )
     latent, halo_out = call(
         bind(latent_kernel, rows, own),
@@ -400,7 +430,7 @@
     )
     halo_rows = exchange(halo_out.reshape(pair), DOM).reshape(dom, width)
 
-    lines = enc_gath[:, 3 * rows + own : 3 * rows + own + 3, :edges].astype(jnp.int32)
+    lines = enc_gath[:, 2 * rows + own : 2 * rows + own + 3, :edges].astype(jnp.int32)
     source = lines[:, 0] * 16 + lines[:, 1]
     slot = source - nodes
     place = jnp.where(slot < 0, source, nodes + slot // halo)
@@ -434,7 +464,7 @@
         me=me,
         scratch=[pltpu.VMEM((width, 2 * width), BF)],
     )
-    first = over_feat(*first)
+    first = over_cores(*first)
     node_part, at_src = call(
         bind(owner_kernel, rows),
         [all_sums, one_sum],
@@ -446,7 +476,7 @@
         me=me,
     )
 
-    node_in = exchange(node_part, "y")
+    node_in, first = lax.optimization_barrier((exchange(node_part, "y"), first))
 
     node_grad, slot_out, *second = call(
         bind(backward_kernel, rows, own),
@@ -462,6 +492,7 @@
         latent,
         at_src,
         enc_gath,
+        full_enc2,
         received,
         enc_dst,
         preact,
@@ -471,8 +502,11 @@
         scratch=[pltpu.VMEM((width, 4 * width), BF), pltpu.VMEM((nodes, width), F32)],
     )
     slot_back = exchange(slot_out.reshape(dom, caps, width), DOM)
-    second = over_feat(*second)
-    (level,) = call(level_kernel, [((rows // 2, 6 * width), BF)], first, second)
+    second = over_cores(*second)
+    first, second = lax.optimization_barrier((first, second))
+    first = onward(first, me)
+    second = lax.psum_scatter(second, "y", scatter_dimension=0, tiled=True)
+    (level,) = call(level_kernel, [((half, 6 * width), BF)], second, *first)
     slot_back, level = lax.optimization_barrier((slot_back, level))
     across = lax.axis_size("x")
     thin = rows // (2 * across)
@@ -485,7 +519,7 @@
     near = lax.axis_size(("x", "c"))
     totals = exchange(jnp.broadcast_to(level[None], (near, *level.shape)), ("c", "x"))
     totals = call(bind(split_kernel, factor), [((rows, width), F32)] * 6, totals)
-    (out_rows,) = call(out_kernel, [((own, width), BF)], latent, first, me=me)
+    (out_rows,) = call(out_kernel, [((own, width), BF)], latent, *first, me=me)
     (g_mesh,) = call(
         bind(mesh_kernel, rows), [((own, width), BF)], node_grad, enc_gath, second, me=me
     )

time: 293 us -> 288 us (0.983)
  starting transfers between devices: 52.9 us -> 79.8 us
  blocking collectives: 89.9 us -> 64.4 us
  waiting for transfers between devices: 72.8 us -> 62.3 us
    all_to_all x4 -> x3, blocking collectives: 89.9 us -> 50.3 us  [exchange(): return lax.all_to_all(array, axes, 0, 0, tiled=True)]
    reduce_scatter x2 -> x1, waiting for transfers between devices: 24.8 us -> 0.02 us  [per_device(): second = lax.psum_scatter(second, 'y', scatter_dimension=0, tiled=True)]
    all_to_all x6 -> x7, starting transfers between devices: 46.8 us -> 65.2 us  [exchange(): return lax.all_to_all(array, axes, 0, 0, tiled=True)]
    all_gather x0 -> x1, blocking collectives: none -> 14.1 us  [per_device(): full_enc2 = lax.all_gather(w_enc2, 'y', axis=0, tiled=True)]
    ppermute x2 -> x5, starting transfers between devices: 5.91 us -> 14.5 us  [the longest x3 8.4 us: onward(): lax.ppermute(blocks[k], 'y', [(i, (i + k) % n) for i in range(n)])]
    ppermute x2 -> x5, waiting for transfers between devices: 2.48 us -> 10.5 us  [the longest x3 8.06 us: onward(): lax.ppermute(blocks[k], 'y', [(i, (i + k) % n) for i in range(n)])]
    all_to_all x6 -> x7, waiting for transfers between devices: 44.8 us -> 51 us  [exchange(): return lax.all_to_all(array, axes, 0, 0, tiled=True)]
    unnamed x17 -> x25, local copies, waits for them, and re-layouts: 7.19 us -> 8.83 us
  transfers between devices with their start and end apart: 12 -> 15, of which waited for: 7 -> 9; matrix products, arithmetic and copies ran while one was open for 3% -> 3% of each run, Pallas kernels for 11% -> 9%
where the time goes in v6:
time: 288 us; the launch traced here: 287 us
  starting transfers between devices  79.8 us (28%)
  blocking collectives  64.4 us (22%)
  waiting for transfers between devices  62.3 us (22%)
  Pallas kernels  47 us (16%)
  local copies, waits for them, and re-layouts  17 us (6%)
  between operations  13.9 us (5%)
    all_to_all x7, starting transfers between devices, exchange(): return lax.all_to_all(array, axes, 0, 0, tiled=True)  65.2 us
    all_to_all x7, waiting for transfers between devices, exchange(): return lax.all_to_all(array, axes, 0, 0, tiled=True)  51 us
    all_to_all x3, blocking collectives, exchange(): return lax.all_to_all(array, axes, 0, 0, tiled=True)  50.3 us
    pallas_call x16, Pallas kernels, call(): pl.pallas_call(kernel, out_shape=tuple((jax.ShapeDtypeStruct(s, d) for s,...  47 us
    all_gather x1, blocking collectives, per_device(): full_enc2 = lax.all_gather(w_enc2, 'y', axis=0, tiled=True)  14.1 us
    unnamed x25, local copies, waits for them, and re-layouts  8.83 us
    ppermute x3, starting transfers between devices, onward(): lax.ppermute(blocks[k], 'y', [(i, (i + k) % n) for i in range(n)])  8.4 us
    ppermute x3, waiting for transfers between devices, onward(): lax.ppermute(blocks[k], 'y', [(i, (i + k) % n) for i in range(n)])  8.06 us
  transfers between devices with their start and end apart: 15, of which 9 were waited for; matrix products, arithmetic and copies ran while one was open for 3% of the time, Pallas kernels for 9%

profile of v6, /device:TPU:1, one launch (start us, length us, event | category | flops | bytes accessed | tf_op | source)
XLA Modules:
  0.0 287.1 jit_solution(14101275489407779669)
XLA Ops:
  12.4 20.4 %all-to-all-start = ((bf16[128,2,512]{2,1,0:T(2,128)(2,1)}), bf16[128,2,512]{2,1,0:T(2,128)(2,1)S(1)}, u32[]{:S(2)}, u32[]{:S(2)}) async-start(bf16[128,2,512]{2,1,0:T(2,128)(2,1)} %reshape.198), calls=%async_computation | async-start | bytes 524288 | tf_op jit(solution)/shard_map/all_to_all | solution.py:52
  32.8 14.1 %all_gather.17.w_ref = bf16[512,512]{1,0:T(8,128)(2,1)} all-gather(bf16[128,512]{1,0:T(8,128)(2,1)S(1)} %copy-done.9), channel_id=1, replica_groups=mesh['z'=16,'x'=4,'c'=2,'y'=4] {'y'}, dimensions={0}, use_global_device_ids=true | all-gather | bytes 655360 | tf_op jit(solution)/shard_map/all_gather | solution.py:405
  47.0 6.3 %all-to-all-done = bf16[128,2,512]{2,1,0:T(2,128)(2,1)S(1)} async-done(((bf16[128,2,512]{2,1,0:T(2,128)(2,1)}), bf16[128,2,512]{2,1,0:T(2,128)(2,1)S(1)}, u32[]{:S(2)}, u32[]{:S(2)}) %all-to-all-start) | async-done | bytes 262176 | tf_op jit(solution)/shard_map/all_to_all | solution.py:52
  54.0 3.6 %shard_map.206 = (bf16[4,160,512]{2,1,0:T(8,128)(2,1)}, f32[256,512]{1,0:T(8,128)}, f32[256,512]{1,0:T(8,128)}, f32[256,1]{1,0:T(8,128)}) custom-call(bf16[128,1024]{1,0:T(8,128)(2,1)} %bitcast.29, s32[2,128]{1,0:T(2,128)} %bitcast.45, bf16[4,304,512]{2,1,0:T(8,128)(2,1)} %bitcast.20, bf16[512,512]{1,0:T(8,128)(2,1)} %all_gather.17.w_ref), custom_call_target="tpu_custom_call" | custom-call | tf_op jit(solution)/shard_map/pallas_call | solution.py:25
  57.6 4.2 %all-to-all-start.1 = ((bf16[4,160,512]{2,1,0:T(8,128)(2,1)}), bf16[4,160,512]{2,1,0:T(8,128)(2,1)S(1)}, u32[]{:S(2)}, u32[]{:S(2)}) async-start(bf16[4,160,512]{2,1,0:T(8,128)(2,1)} %get-tuple-element.52), calls=%async_computation.1 | async-start | bytes 1310720 | tf_op jit(solution)/shard_map/all_to_all | solution.py:52
  63.3 8.7 %all-to-all-done.1.sums_ref = bf16[4,160,512]{2,1,0:T(8,128)(2,1)S(1)} async-done(((bf16[4,160,512]{2,1,0:T(8,128)(2,1)}), bf16[4,160,512]{2,1,0:T(8,128)(2,1)S(1)}, u32[]{:S(2)}, u32[]{:S(2)}) %all-to-all-start.1) | async-done | bytes 655392 | tf_op jit(solution)/shard_map/all_to_all | solution.py:52
  76.8 14.9 %all-to-all-start.2 = ((bf16[128,2,256]{2,1,0:T(2,128)(2,1)}), bf16[128,2,256]{2,1,0:T(2,128)(2,1)S(1)}, u32[]{:S(2)}, u32[]{:S(2)}) async-start(bf16[128,2,256]{2,1,0:T(2,128)(2,1)} %reshape.200), calls=%async_computation.2 | async-start | bytes 262144 | tf_op jit(solution)/shard_map/all_to_all | solution.py:52
  93.1 14.6 %all-to-all-done.2 = bf16[128,2,256]{2,1,0:T(2,128)(2,1)S(1)} async-done(((bf16[128,2,256]{2,1,0:T(2,128)(2,1)}), bf16[128,2,256]{2,1,0:T(2,128)(2,1)S(1)}, u32[]{:S(2)}, u32[]{:S(2)}) %all-to-all-start.2) | async-done | bytes 131104 | tf_op jit(solution)/shard_map/all_to_all | solution.py:52
  108.4 6.0 %shard_map.208 = (bf16[128,512]{1,0:T(8,128)(2,1)}, f32[160,512]{1,0:T(8,128)}, bf16[160,512]{1,0:T(8,128)(2,1)}, f32[160,512]{1,0:T(8,128)}, bf16[640,512]{1,0:T(8,128)(2,1)}, /*index=5*/bf16[640,512]{1,0:T(8,128)(2,1)}) custom-call(bf16[160,512]{1,0:T(8,128)(2,1)} %get-tuple-element.53.latent_ref, bf16[128,512]{1,0:T(8,128)(2,1)} %bitcast.35, ...), custom_call_target="tpu_custom_call" | custom-call | tf_op jit(solution)/shard_map/pallas_call | solution.py:25
  116.0 7.2 %all-to-all-start.3 = ((bf16[128,2,256]{2,1,0:T(2,128)(2,1)}), bf16[128,2,256]{2,1,0:T(2,128)(2,1)S(1)}, u32[]{:S(2)}, u32[]{:S(2)}) async-start(bf16[128,2,256]{2,1,0:T(2,128)(2,1)} %reshape.202), calls=%async_computation.3 | async-start | bytes 262144 | tf_op jit(solution)/shard_map/all_to_all | solution.py:52
  123.2 3.4 %shard_map.210 = (bf16[512,512]{1,0:T(8,128)(2,1)}, bf16[512,512]{1,0:T(8,128)(2,1)}, bf16[192,512]{1,0:T(8,128)(2,1)}) custom-call(s32[2]{0:T(128)} %pad_add_fusion.me_ref, bf16[160,512]{1,0:T(8,128)(2,1)} %get-tuple-element.53.latent_ref, bf16[160,512]{1,0:T(8,128)(2,1)} %get-tuple-element.58.dst_ref, bf16[640,512]{1,0:T(8,128)(2,1)} %get-tuple-element.60.hidden_ref, ...), custom_call_target="tpu_custom_call" | custom-call | tf_op jit(solution)/shard_map/pallas_call | solution.py:25
  129.5 9.6 %all-to-all-done.3 = bf16[128,2,256]{2,1,0:T(2,128)(2,1)S(1)} async-done(((bf16[128,2,256]{2,1,0:T(2,128)(2,1)}), bf16[128,2,256]{2,1,0:T(2,128)(2,1)S(1)}, u32[]{:S(2)}, u32[]{:S(2)}) %all-to-all-start.3) | async-done | bytes 131104 | tf_op jit(solution)/shard_map/all_to_all | solution.py:52
  139.8 3.1 %shard_map.209 = (bf16[4,160,512]{2,1,0:T(8,128)(2,1)}, bf16[160,512]{1,0:T(8,128)(2,1)}) custom-call(s32[2]{0:T(128)} %pad_add_fusion.me_ref, bf16[128,512]{1,0:T(8,128)(2,1)} %bitcast.36, s32[4,128]{1,0:T(4,128)} %bitcast.42, f32[160,512]{1,0:T(8,128)} %get-tuple-element.57.local_ref, bf16[160,512]{1,0:T(8,128)(2,1)} %get-tuple-element.58.dst_ref, ...), custom_call_target="tpu_custom_call" | custom-call | tf_op jit(solution)/shard_map/pallas_call | solution.py:25
  142.9 3.5 %all-to-all-start.4 = ((bf16[4,160,512]{2,1,0:T(8,128)(2,1)}), bf16[4,160,512]{2,1,0:T(8,128)(2,1)S(1)}, u32[]{:S(2)}, u32[]{:S(2)}) async-start(bf16[4,160,512]{2,1,0:T(8,128)(2,1)} %get-tuple-element.59), calls=%async_computation.4 | async-start | bytes 1310720 | tf_op jit(solution)/shard_map/all_to_all | solution.py:52
  149.5 7.5 %all-to-all-done.4.sums_ref = bf16[4,160,512]{2,1,0:T(8,128)(2,1)S(1)} async-done(((bf16[4,160,512]{2,1,0:T(8,128)(2,1)}), bf16[4,160,512]{2,1,0:T(8,128)(2,1)S(1)}, u32[]{:S(2)}, u32[]{:S(2)}) %all-to-all-start.4) | async-done | bytes 655392 | tf_op jit(solution)/shard_map/all_to_all | solution.py:52
  157.8 5.6 %shard_map.212 = (f32[160,512]{1,0:T(8,128)}, bf16[128,1024]{1,0:T(8,128)(2,1)}, bf16[1024,512]{1,0:T(8,128)(2,1)}, bf16[1024,512]{1,0:T(8,128)(2,1)}, bf16[192,512]{1,0:T(8,128)(2,1)}) custom-call(s32[2]{0:T(128)} %pad_add_fusion.me_ref, bf16[4,160,512]{2,1,0:T(8,128)(2,1)} %copy-done.2, bf16[4,432,512]{2,1,0:T(8,128)(2,1)} %bitcast.28, ...), custom_call_target="tpu_custom_call" | custom-call | tf_op jit(solution)/shard_map/pallas_call | solution.py:25
  174.7 7.1 %all-to-all-start.5 = ((bf16[128,2,512]{2,1,0:T(2,128)(2,1)}), bf16[128,2,512]{2,1,0:T(2,128)(2,1)S(1)}, u32[]{:S(2)}, u32[]{:S(2)}) async-start(bf16[128,2,512]{2,1,0:T(2,128)(2,1)} %reshape.204), calls=%async_computation.5 | async-start | bytes 524288 | tf_op jit(solution)/shard_map/all_to_all | solution.py:52
  186.1 3.7 %collective-permute-start.3 = (bf16[176,512]{1,0:T(8,128)(2,1)}, bf16[176,512]{1,0:T(8,128)(2,1)S(1)}, u32[]{:S(2)}, u32[]{:S(2)}) collective-permute-start(bf16[176,512]{1,0:T(8,128)(2,1)} %get-tuple-element.78), channel_id=1, source_target_pairs={{0,2},{1,3},{2,0},{3,1},{4,6},{5,7},{6,4},{7,5},{8,10},{9,11},{10,... | collective-permute-start | bytes 540680 | tf_op jit(solution)/shard_map/ppermute | solution.py:47
  195.2 5.1 %collective-permute-done.3.b2_ref = bf16[176,512]{1,0:T(8,128)(2,1)S(1)} collective-permute-done((bf16[176,512]{1,0:T(8,128)(2,1)}, bf16[176,512]{1,0:T(8,128)(2,1)S(1)}, u32[]{:S(2)}, u32[]{:S(2)}) %collective-permute-start.3) | collective-permute-done | bytes 180256 | tf_op jit(solution)/shard_map/ppermute | solution.py:47
  203.2 11.6 %all_to_all.50.in_ref = bf16[4,16,3072]{2,1,0:T(8,128)(2,1)} all-to-all(bf16[4,16,3072]{2,1,0:T(8,128)(2,1)} %bitcast.31), channel_id=1, replica_groups=mesh['z'=16,'x'=4,'c'=2,'y'=4] {'x'}, dimensions={0} | all-to-all | bytes 786432 | tf_op jit(solution)/shard_map/all_to_all | solution.py:52
  217.4 23.6 %all_to_all.51 = bf16[16,2,1536]{2,1,0:T(2,128)(2,1)S(1)} all-to-all(bf16[16,2,1536]{2,1,0:T(2,128)(2,1)S(1)} %reshape.207), channel_id=1, replica_groups=mesh['z'=16,'x'=4,'c'=2,'y'=4] {'z'}, dimensions={0} | all-to-all | bytes 196608 | tf_op jit(solution)/shard_map/all_to_all | solution.py:52
  241.1 15.1 %all_to_all.52 = bf16[16,2,1536]{2,1,0:T(2,128)(2,1)S(1)} all-to-all(bf16[16,2,1536]{2,1,0:T(2,128)(2,1)S(1)} %broadcast_in_dim.29), channel_id=1, replica_groups=mesh['z'=16,'x'=4,'c'=2,'y'=4] {'z'}, dimensions={0} | all-to-all | bytes 196608 | tf_op jit(solution)/shard_map/all_to_all | solution.py:52
  257.2 7.9 %all-to-all-start.9 = ((bf16[8,16,3072]{2,1,0:T(8,128)(2,1)}), bf16[8,16,3072]{2,1,0:T(8,128)(2,1)S(1)}, u32[]{:S(2)}, u32[]{:S(2)}) async-start(bf16[8,16,3072]{2,1,0:T(8,128)(2,1)} %broadcast_in_dim.31), calls=%async_computation.10 | async-start | bytes 1572864 | tf_op jit(solution)/shard_map/all_to_all | solution.py:52
  273.0 4.3 %all-to-all-done.9.in_ref = bf16[8,16,3072]{2,1,0:T(8,128)(2,1)S(1)} async-done(((bf16[8,16,3072]{2,1,0:T(8,128)(2,1)}), bf16[8,16,3072]{2,1,0:T(8,128)(2,1)S(1)}, u32[]{:S(2)}, u32[]{:S(2)}) %all-to-all-start.9) | async-done | bytes 786464 | tf_op jit(solution)/shard_map/all_to_all | solution.py:52
  (71 shorter events, 62.1 us)
Async XLA Ops:
  7.2 46.8 %all-gather.5.cloned.1.call-start = ((), (), s32[]{:S(2)}) async-start(), calls=%async_computation.12 | async-start | bytes 1556480 | tf_op jit(solution)/shard_map/all_gather | solution.py:404
  7.2 25.6 %copy-start.9 = (bf16[128,512]{1,0:T(8,128)(2,1)S(1)}, bf16[128,512]{1,0:T(8,128)(2,1)}, u32[]{:S(2)}) copy-start(bf16[128,512]{1,0:T(8,128)(2,1)} %param.18) | copy-start | bytes 393220
  9.8 98.6 %all-gather.7.cloned.1.call-start = ((), (), s32[]{:S(2)}) async-start(), calls=%async_computation.13 | async-start | bytes 2211840 | tf_op jit(solution)/shard_map/all_gather | solution.py:406
  12.4 40.9 %all-to-all-start = ((bf16[128,2,512]{2,1,0:T(2,128)(2,1)}), bf16[128,2,512]{2,1,0:T(2,128)(2,1)S(1)}, u32[]{:S(2)}, u32[]{:S(2)}) async-start(bf16[128,2,512]{2,1,0:T(2,128)(2,1)} %reshape.198), calls=%async_computation | async-start | bytes 524288 | tf_op jit(solution)/shard_map/all_to_all | solution.py:52
  57.6 14.3 %all-to-all-start.1 = ((bf16[4,160,512]{2,1,0:T(8,128)(2,1)}), bf16[4,160,512]{2,1,0:T(8,128)(2,1)S(1)}, u32[]{:S(2)}, u32[]{:S(2)}) async-start(bf16[4,160,512]{2,1,0:T(8,128)(2,1)} %get-tuple-element.52), calls=%async_computation.1 | async-start | bytes 1310720 | tf_op jit(solution)/shard_map/all_to_all | solution.py:52
  72.0 0.8 copy-start.1
  76.8 31.0 %all-to-all-start.2 = ((bf16[128,2,256]{2,1,0:T(2,128)(2,1)}), bf16[128,2,256]{2,1,0:T(2,128)(2,1)S(1)}, u32[]{:S(2)}, u32[]{:S(2)}) async-start(bf16[128,2,256]{2,1,0:T(2,128)(2,1)} %reshape.200), calls=%async_computation.2 | async-start | bytes 262144 | tf_op jit(solution)/shard_map/all_to_all | solution.py:52
  116.0 23.1 %all-to-all-start.3 = ((bf16[128,2,256]{2,1,0:T(2,128)(2,1)}), bf16[128,2,256]{2,1,0:T(2,128)(2,1)S(1)}, u32[]{:S(2)}, u32[]{:S(2)}) async-start(bf16[128,2,256]{2,1,0:T(2,128)(2,1)} %reshape.202), calls=%async_computation.3 | async-start | bytes 262144 | tf_op jit(solution)/shard_map/all_to_all | solution.py:52
  126.5 20.0 %collective-permute-start = (bf16[512,512]{1,0:T(8,128)(2,1)}, bf16[512,512]{1,0:T(8,128)(2,1)S(1)}, u32[]{:S(2)}, u32[]{:S(2)}) collective-permute-start(bf16[512,512]{1,0:T(8,128)(2,1)} %get-tuple-element.64), channel_id=1, source_target_pairs={{0,4},{4,0},{1,5},{5,1},{2,6},{6,2},{3,7},{7,3},{8,12},{12,8},{9,1... | collective-permute-start | bytes 1572872 | tf_op jit(solution)/shard_map/ppermute | solution.py:36
  142.9 14.1 %all-to-all-start.4 = ((bf16[4,160,512]{2,1,0:T(8,128)(2,1)}), bf16[4,160,512]{2,1,0:T(8,128)(2,1)S(1)}, u32[]{:S(2)}, u32[]{:S(2)}) async-start(bf16[4,160,512]{2,1,0:T(8,128)(2,1)} %get-tuple-element.59), calls=%async_computation.4 | async-start | bytes 1310720 | tf_op jit(solution)/shard_map/all_to_all | solution.py:52
  146.4 54.0 %reduce-scatter.2.cloned.1.call-start = ((), (), s32[]{:S(2)}) async-start(), calls=%async_computation.11 | async-start | bytes 1556480 | tf_op jit(solution)/shard_map/reduce_scatter | solution.py:508
  146.5 0.8 copy-start.7
  157.0 0.8 copy-start.2
  163.4 5.6 %collective-permute-start.1 = (bf16[1024,512]{1,0:T(8,128)(2,1)}, bf16[1024,512]{1,0:T(8,128)(2,1)S(1)}, u32[]{:S(2)}, u32[]{:S(2)}) collective-permute-start(bf16[1024,512]{1,0:T(8,128)(2,1)} %get-tuple-element.73), channel_id=1, source_target_pairs={{0,4},{4,0},{1,5},{5,1},{2,6},{6,2},{3,7},{7,3},{8,12},{12,8},{9,1... | collective-permute-start | bytes 3145736 | tf_op jit(solution)/shard_map/ppermute | solution.py:36
  169.0 1.0 copy-start.3
  172.9 0.9 copy-start.8
  174.7 28.4 %all-to-all-start.5 = ((bf16[128,2,512]{2,1,0:T(2,128)(2,1)}), bf16[128,2,512]{2,1,0:T(2,128)(2,1)S(1)}, u32[]{:S(2)}, u32[]{:S(2)}) async-start(bf16[128,2,512]{2,1,0:T(2,128)(2,1)} %reshape.204), calls=%async_computation.5 | async-start | bytes 524288 | tf_op jit(solution)/shard_map/all_to_all | solution.py:52
  183.9 11.3 %collective-permute-start.2 = (bf16[176,512]{1,0:T(8,128)(2,1)}, bf16[176,512]{1,0:T(8,128)(2,1)S(1)}, u32[]{:S(2)}, u32[]{:S(2)}) collective-permute-start(bf16[176,512]{1,0:T(8,128)(2,1)} %get-tuple-element.77), channel_id=1, source_target_pairs={{0,1},{1,2},{2,3},{3,0},{4,5},{5,6},{6,7},{7,4},{8,9},{9,10},{10,1... | collective-permute-start | bytes 540680 | tf_op jit(solution)/shard_map/ppermute | solution.py:47
  186.1 14.3 %collective-permute-start.3 = (bf16[176,512]{1,0:T(8,128)(2,1)}, bf16[176,512]{1,0:T(8,128)(2,1)S(1)}, u32[]{:S(2)}, u32[]{:S(2)}) collective-permute-start(bf16[176,512]{1,0:T(8,128)(2,1)} %get-tuple-element.78), channel_id=1, source_target_pairs={{0,2},{1,3},{2,0},{3,1},{4,6},{5,7},{6,4},{7,5},{8,10},{9,11},{10,... | collective-permute-start | bytes 540680 | tf_op jit(solution)/shard_map/ppermute | solution.py:47
  189.8 10.6 %collective-permute-start.4 = (bf16[176,512]{1,0:T(8,128)(2,1)}, bf16[176,512]{1,0:T(8,128)(2,1)S(1)}, u32[]{:S(2)}, u32[]{:S(2)}) collective-permute-start(bf16[176,512]{1,0:T(8,128)(2,1)} %get-tuple-element.79), channel_id=1, source_target_pairs={{0,3},{1,0},{2,1},{3,2},{4,7},{5,4},{6,5},{7,6},{8,11},{9,8},{10,9... | collective-permute-start | bytes 540680 | tf_op jit(solution)/shard_map/ppermute | solution.py:47
  195.2 5.2 %copy-start.4 = (bf16[176,512]{1,0:T(8,128)(2,1)}, bf16[176,512]{1,0:T(8,128)(2,1)S(1)}, u32[]{:S(2)}) copy-start(bf16[176,512]{1,0:T(8,128)(2,1)S(1)} %collective-permute-done.2.b1_ref) | copy-start | bytes 540676
  200.4 0.7 copy-start.6
  257.2 20.1 %all-to-all-start.9 = ((bf16[8,16,3072]{2,1,0:T(8,128)(2,1)}), bf16[8,16,3072]{2,1,0:T(8,128)(2,1)S(1)}, u32[]{:S(2)}, u32[]{:S(2)}) async-start(bf16[8,16,3072]{2,1,0:T(8,128)(2,1)} %broadcast_in_dim.31), calls=%async_computation.10 | async-start | bytes 1572864 | tf_op jit(solution)/shard_map/all_to_all | solution.py:52
  277.3 0.9 copy-start
  (1 other events, 0.7 us)
Sparse Core Ops, SparseCore 0:
  10.7 41.0 all-gather.4
  53.9 36.3 all-gather.6
  173.0 22.7 reduce-scatter.1

commit v7 on v6

--- a/solution.py
+++ b/solution.py
@@ -37,15 +37,6 @@
     size = (keep.shape[0] + tail.shape[0], keep.shape[1])
     kernel = functools.partial(merge_kernel, lax.axis_size("y"))
     return call(kernel, [(size, BF)], keep, given, tail)[0]
-
-
-def onward(array, me):
-    n = lax.axis_size("y")
-    size = (array.shape[0] // n, array.shape[1])
-    blocks = call(deal_out_kernel, [(size, BF)] * n, array, me=me)
-    return [blocks[0]] + [
-        lax.ppermute(blocks[k], "y", [(i, (i + k) % n) for i in range(n)]) for k in range(1, n)
-    ]
 
 
 def exchange(array, axes):
@@ -236,14 +227,20 @@
     back_ref[...] = at_src[nodes:].astype(BF)
 
 
-def process_terms_kernel(
-    rows, own, me_ref, latent_ref, dst_ref, hidden_ref, mid_ref, node_ref,
-    keep_ref, give_ref, tail_ref, term_ref,
-):
+def process_terms_kernel(rows, own, latent_ref, dst_ref, hidden_ref, mid_ref, node_ref, out_ref, term_ref):
     width = latent_ref.shape[1]
     term_ref[:, :width] = outer(latent_ref[...], dst_ref[...]).astype(BF)
     term_ref[:, width:] = outer(hidden_ref[...], mid_ref[...]).astype(BF)
-    deal(me_ref, keep_ref, give_ref, tail_ref, term_ref, rows, node_ref, own)
+    count = term_ref.shape[0] // rows
+    size = out_ref.shape[0] // count
+    for y in range(count):
+        for t in range(2):
+            at = y * size + t * rows
+            block = term_ref[y * rows : (y + 1) * rows, t * width : (t + 1) * width]
+            out_ref[at : at + rows, :] = block
+        block = node_ref[y * own : (y + 1) * own, :]
+        block = jnp.concatenate([block, jnp.zeros((size - 2 * rows - own, width), F32)], axis=0)
+        out_ref[y * size + 2 * rows : (y + 1) * size, :] = block.astype(BF)
 
 
 def owner_kernel(rows, me_ref, back_ref, send_ref, local_ref, dst_ref, gath_ref, out_ref, src_ref):
@@ -294,32 +291,22 @@
     out_ref[...] = dot(slots_hot(send_ref[...], nodes), grads).astype(BF)
 
 
-def out_kernel(me_ref, latent_ref, b0_ref, b1_ref, b2_ref, b3_ref, out_ref):
+def out_kernel(rows, me_ref, latent_ref, first_ref, out_ref):
     own, nodes = out_ref.shape[0], latent_ref.shape[0]
-    start = b0_ref.shape[0] - own - (-own % PAD)
-    total = total_of([b[start:, :] for b in (b0_ref, b1_ref, b2_ref, b3_ref)])
     mine = lax.broadcasted_iota(jnp.int32, (1, own), 1) + me_ref[0] * own
     latent = outer(one_hot(mine, nodes), latent_ref[...])
-    out_ref[...] = (latent + total[:own]).astype(BF)
-
-
-def level_kernel(second_ref, b0_ref, b1_ref, b2_ref, b3_ref, out_ref):
+    out_ref[...] = (latent + first_ref[2 * rows :, :].astype(F32)[:own]).astype(BF)
+
+
+def level_kernel(me_ref, second_ref, first_ref, given_ref, out_ref):
     width = second_ref.shape[1]
     half = out_ref.shape[0]
     for k in range(4):
         out_ref[:, k * width : (k + 1) * width] = second_ref[k * half : (k + 1) * half, :]
     for k in range(2):
-        at = slice(k * half, (k + 1) * half)
-        block = total_of([b[at, :] for b in (b0_ref, b1_ref, b2_ref, b3_ref)])
+        mine = pl.ds(pl.multiple_of((2 * k + me_ref[1]) * half, half), half)
+        block = total_of([first_ref[mine, :], given_ref[k * half : (k + 1) * half, :]])
         out_ref[:, (4 + k) * width : (5 + k) * width] = block.astype(BF)
-
-
-def deal_out_kernel(me_ref, in_ref, *out_refs):
-    count = len(out_refs)
-    size = out_refs[0].shape[0]
-    for k, ref in enumerate(out_refs):
-        to = lax.rem(me_ref[0] + k, count)
-        ref[...] = in_ref[pl.ds(pl.multiple_of(to * size, PAD), size), :]
 
 
 def mesh_kernel(rows, me_ref, node_ref, enc_ref, second_ref, mesh_ref):
@@ -453,18 +440,18 @@
         proc_gath,
     )
     returned = exchange(halo_back.reshape(pair), DOM)
-    first = call(
+    (first,) = call(
         bind(process_terms_kernel, rows, own),
-        [((4 * rows, width), BF), ((4 * rows, width), BF), ((feat * held, width), BF)],
+        [((feat * (2 * rows + held), width), BF)],
         latent,
         at_dst,
         hidden,
         mid,
         messages,
-        me=me,
         scratch=[pltpu.VMEM((width, 2 * width), BF)],
     )
-    first = over_cores(*first)
+    returned, first = lax.optimization_barrier((returned, first))
+    first = lax.psum_scatter(first, "y", scatter_dimension=0, tiled=True)
     node_part, at_src = call(
         bind(owner_kernel, rows),
         [all_sums, one_sum],
@@ -476,7 +463,7 @@
         me=me,
     )
 
-    node_in, first = lax.optimization_barrier((exchange(node_part, "y"), first))
+    node_in = exchange(node_part, "y")
 
     node_grad, slot_out, *second = call(
         bind(backward_kernel, rows, own),
@@ -503,10 +490,10 @@
     )
     slot_back = exchange(slot_out.reshape(dom, caps, width), DOM)
     second = over_cores(*second)
-    first, second = lax.optimization_barrier((first, second))
-    first = onward(first, me)
     second = lax.psum_scatter(second, "y", scatter_dimension=0, tiled=True)
-    (level,) = call(level_kernel, [((half, 6 * width), BF)], second, *first)
+    give = lax.dynamic_slice_in_dim(first[: 2 * rows].reshape(2, 2, half, width), 1 - me[1], 1, 1)
+    given = lax.ppermute(give.reshape(rows, width), "c", [(0, 1), (1, 0)])
+    (level,) = call(level_kernel, [((half, 6 * width), BF)], second, first, given, me=me)
     slot_back, level = lax.optimization_barrier((slot_back, level))
     across = lax.axis_size("x")
     thin = rows // (2 * across)
@@ -519,7 +506,7 @@
     near = lax.axis_size(("x", "c"))
     totals = exchange(jnp.broadcast_to(level[None], (near, *level.shape)), ("c", "x"))
     totals = call(bind(split_kernel, factor), [((rows, width), F32)] * 6, totals)
-    (out_rows,) = call(out_kernel, [((own, width), BF)], latent, *first, me=me)
+    (out_rows,) = call(bind(out_kernel, rows), [((own, width), BF)], latent, first, me=me)
     (g_mesh,) = call(
         bind(mesh_kernel, rows), [((own, width), BF)], node_grad, enc_gath, second, me=me
     )

time: 288 us -> 289 us (level)
  blocking collectives: 64.4 us -> 80.9 us
  starting transfers between devices: 79.8 us -> 67.1 us
  Pallas kernels: 47 us -> 42.4 us
    all_to_all x3 -> x4, blocking collectives: 50.3 us -> 66.7 us  [exchange(): return lax.all_to_all(array, axes, 0, 0, tiled=True)]
    reduce_scatter x1, waiting for transfers between devices: 0.02 us -> 7.29 us  [per_device(): second = lax.psum_scatter(second, 'y', scatter_dimension=0, tiled=True)]
    ppermute x3 -> x1, waiting for transfers between devices: 8.06 us -> 0.96 us  [per_device(): given = lax.ppermute(give.reshape(rows, width), 'c', [(0, 1), (1, 0)])]
    ppermute x3 -> x1, starting transfers between devices: 8.4 us -> 2.8 us  [per_device(): given = lax.ppermute(give.reshape(rows, width), 'c', [(0, 1), (1, 0)])]
    pallas_call x16 -> x14, Pallas kernels: 47 us -> 42.4 us  [call(): pl.pallas_call(kernel, out_shape=tuple((jax.ShapeDtypeStruct(s, d) for s,...]
    all_to_all x7 -> x6, starting transfers between devices: 65.2 us -> 61.1 us  [exchange(): return lax.all_to_all(array, axes, 0, 0, tiled=True)]
    ppermute x2 -> x1, starting transfers between devices: 6.09 us -> 2.96 us  [over_cores(): given = lax.ppermute(give, 'c', [(0, 1), (1, 0)])]
    all_to_all x7 -> x6, waiting for transfers between devices: 51 us -> 53.4 us  [exchange(): return lax.all_to_all(array, axes, 0, 0, tiled=True)]
  transfers between devices with their start and end apart: 15 -> 12, of which waited for: 9 -> 9; matrix products, arithmetic and copies ran while one was open for 3% -> 4% of each run, Pallas kernels for 9% -> 10%
where the time goes in v7:
time: 289 us; the launch traced here: 287 us
  blocking collectives  80.9 us (28%)
  starting transfers between devices  67.1 us (23%)
  waiting for transfers between devices  64.9 us (22%)
  Pallas kernels  42.4 us (15%)
  local copies, waits for them, and re-layouts  15.6 us (5%)
  between operations  13.9 us (5%)
    all_to_all x4, blocking collectives, exchange(): return lax.all_to_all(array, axes, 0, 0, tiled=True)  66.7 us
    all_to_all x6, starting transfers between devices, exchange(): return lax.all_to_all(array, axes, 0, 0, tiled=True)  61.1 us
    all_to_all x6, waiting for transfers between devices, exchange(): return lax.all_to_all(array, axes, 0, 0, tiled=True)  53.4 us
    pallas_call x14, Pallas kernels, call(): pl.pallas_call(kernel, out_shape=tuple((jax.ShapeDtypeStruct(s, d) for s,...  42.4 us
    all_gather x1, blocking collectives, per_device(): full_enc2 = lax.all_gather(w_enc2, 'y', axis=0, tiled=True)  14.1 us
    reduce_scatter x1, waiting for transfers between devices, per_device(): second = lax.psum_scatter(second, 'y', scatter_dimension=0, tiled=True)  7.29 us
    unnamed x17, local copies, waits for them, and re-layouts  6.48 us
  transfers between devices with their start and end apart: 12, of which 9 were waited for; matrix products, arithmetic and copies ran while one was open for 4% of the time, Pallas kernels for 10%

profile of v7, /device:TPU:1, one launch (start us, length us, event | category | flops | bytes accessed | tf_op | source)
XLA Modules:
  0.0 287.3 jit_solution(3803653064848343749)
XLA Ops:
  12.4 20.4 %all-to-all-start = ((bf16[128,2,512]{2,1,0:T(2,128)(2,1)}), bf16[128,2,512]{2,1,0:T(2,128)(2,1)S(1)}, u32[]{:S(2)}, u32[]{:S(2)}) async-start(bf16[128,2,512]{2,1,0:T(2,128)(2,1)} %reshape.204), calls=%async_computation | async-start | bytes 524288 | tf_op jit(solution)/shard_map/all_to_all | solution.py:43
  32.8 14.1 %all_gather.17.w_ref = bf16[512,512]{1,0:T(8,128)(2,1)} all-gather(bf16[128,512]{1,0:T(8,128)(2,1)S(1)} %copy-done.4), channel_id=1, replica_groups=mesh['z'=16,'x'=4,'c'=2,'y'=4] {'y'}, dimensions={0}, use_global_device_ids=true | all-gather | bytes 655360 | tf_op jit(solution)/shard_map/all_gather | solution.py:392
  47.0 6.3 %all-to-all-done = bf16[128,2,512]{2,1,0:T(2,128)(2,1)S(1)} async-done(((bf16[128,2,512]{2,1,0:T(2,128)(2,1)}), bf16[128,2,512]{2,1,0:T(2,128)(2,1)S(1)}, u32[]{:S(2)}, u32[]{:S(2)}) %all-to-all-start) | async-done | bytes 262176 | tf_op jit(solution)/shard_map/all_to_all | solution.py:43
  54.0 3.6 %shard_map.206 = (bf16[4,160,512]{2,1,0:T(8,128)(2,1)}, f32[256,512]{1,0:T(8,128)}, f32[256,512]{1,0:T(8,128)}, f32[256,1]{1,0:T(8,128)}) custom-call(bf16[128,1024]{1,0:T(8,128)(2,1)} %bitcast.33, s32[2,128]{1,0:T(2,128)} %bitcast.51, bf16[4,304,512]{2,1,0:T(8,128)(2,1)} %bitcast.24, bf16[512,512]{1,0:T(8,128)(2,1)} %all_gather.17.w_ref), custom_call_target="tpu_custom_call" | custom-call | tf_op jit(solution)/shard_map/pallas_call | solution.py:25
  57.7 4.2 %all-to-all-start.1 = ((bf16[4,160,512]{2,1,0:T(8,128)(2,1)}), bf16[4,160,512]{2,1,0:T(8,128)(2,1)S(1)}, u32[]{:S(2)}, u32[]{:S(2)}) async-start(bf16[4,160,512]{2,1,0:T(8,128)(2,1)} %get-tuple-element.43), calls=%async_computation.1 | async-start | bytes 1310720 | tf_op jit(solution)/shard_map/all_to_all | solution.py:43
  63.2 8.7 %all-to-all-done.1.sums_ref = bf16[4,160,512]{2,1,0:T(8,128)(2,1)S(1)} async-done(((bf16[4,160,512]{2,1,0:T(8,128)(2,1)}), bf16[4,160,512]{2,1,0:T(8,128)(2,1)S(1)}, u32[]{:S(2)}, u32[]{:S(2)}) %all-to-all-start.1) | async-done | bytes 655392 | tf_op jit(solution)/shard_map/all_to_all | solution.py:43
  76.8 14.9 %all-to-all-start.2 = ((bf16[128,2,256]{2,1,0:T(2,128)(2,1)}), bf16[128,2,256]{2,1,0:T(2,128)(2,1)S(1)}, u32[]{:S(2)}, u32[]{:S(2)}) async-start(bf16[128,2,256]{2,1,0:T(2,128)(2,1)} %reshape.206), calls=%async_computation.2 | async-start | bytes 262144 | tf_op jit(solution)/shard_map/all_to_all | solution.py:43
  93.1 14.6 %all-to-all-done.2 = bf16[128,2,256]{2,1,0:T(2,128)(2,1)S(1)} async-done(((bf16[128,2,256]{2,1,0:T(2,128)(2,1)}), bf16[128,2,256]{2,1,0:T(2,128)(2,1)S(1)}, u32[]{:S(2)}, u32[]{:S(2)}) %all-to-all-start.2) | async-done | bytes 131104 | tf_op jit(solution)/shard_map/all_to_all | solution.py:43
  108.5 6.0 %shard_map.208 = (bf16[128,512]{1,0:T(8,128)(2,1)}, f32[160,512]{1,0:T(8,128)}, bf16[160,512]{1,0:T(8,128)(2,1)}, f32[160,512]{1,0:T(8,128)}, bf16[640,512]{1,0:T(8,128)(2,1)}, /*index=5*/bf16[640,512]{1,0:T(8,128)(2,1)}) custom-call(bf16[160,512]{1,0:T(8,128)(2,1)} %get-tuple-element.44.latent_ref, bf16[128,512]{1,0:T(8,128)(2,1)} %bitcast.40, ...), custom_call_target="tpu_custom_call" | custom-call | tf_op jit(solution)/shard_map/pallas_call | solution.py:25
  116.0 7.2 %all-to-all-start.3 = ((bf16[128,2,256]{2,1,0:T(2,128)(2,1)}), bf16[128,2,256]{2,1,0:T(2,128)(2,1)S(1)}, u32[]{:S(2)}, u32[]{:S(2)}) async-start(bf16[128,2,256]{2,1,0:T(2,128)(2,1)} %reshape.208), calls=%async_computation.3 | async-start | bytes 262144 | tf_op jit(solution)/shard_map/all_to_all | solution.py:43
  123.2 3.3 %shard_map.209 = bf16[1216,512]{1,0:T(8,128)(2,1)} custom-call(bf16[160,512]{1,0:T(8,128)(2,1)} %get-tuple-element.44.latent_ref, bf16[160,512]{1,0:T(8,128)(2,1)} %get-tuple-element.48.dst_ref, bf16[640,512]{1,0:T(8,128)(2,1)} %get-tuple-element.49.hidden_ref, bf16[640,512]{1,0:T(8,128)(2,1)} %get-tuple-element.50.mid_ref, ...), custom_call_target="tpu_custom_call" | custom-call | tf_op jit(solution)/shard_map/pallas_call | solution.py:25
  126.5 12.7 %all-to-all-done.3 = bf16[128,2,256]{2,1,0:T(2,128)(2,1)S(1)} async-done(((bf16[128,2,256]{2,1,0:T(2,128)(2,1)}), bf16[128,2,256]{2,1,0:T(2,128)(2,1)S(1)}, u32[]{:S(2)}, u32[]{:S(2)}) %all-to-all-start.3) | async-done | bytes 131104 | tf_op jit(solution)/shard_map/all_to_all | solution.py:43
  140.0 3.1 %shard_map.211 = (bf16[4,160,512]{2,1,0:T(8,128)(2,1)}, bf16[160,512]{1,0:T(8,128)(2,1)}) custom-call(s32[2]{0:T(128)} %pad_add_fusion.me_ref, bf16[128,512]{1,0:T(8,128)(2,1)} %bitcast.41, s32[4,128]{1,0:T(4,128)} %bitcast.48, f32[160,512]{1,0:T(8,128)} %get-tuple-element.54.local_ref, bf16[160,512]{1,0:T(8,128)(2,1)} %get-tuple-element.48.dst_ref, ...), custom_call_target="tpu_custom_call" | custom-call | tf_op jit(solution)/shard_map/pallas_call | solution.py:25
  143.1 22.6 %all_to_all.50.sums_ref = bf16[4,160,512]{2,1,0:T(8,128)(2,1)} all-to-all(bf16[4,160,512]{2,1,0:T(8,128)(2,1)} %get-tuple-element.55), channel_id=1, replica_groups=mesh['z'=16,'x'=4,'c'=2,'y'=4] {'y'}, dimensions={0} | all-to-all | bytes 1310720 | tf_op jit(solution)/shard_map/all_to_all | solution.py:43
  165.7 5.7 %shard_map.212 = (f32[160,512]{1,0:T(8,128)}, bf16[128,1024]{1,0:T(8,128)(2,1)}, bf16[1024,512]{1,0:T(8,128)(2,1)}, bf16[1024,512]{1,0:T(8,128)(2,1)}, bf16[192,512]{1,0:T(8,128)(2,1)}) custom-call(s32[2]{0:T(128)} %pad_add_fusion.me_ref, bf16[4,160,512]{2,1,0:T(8,128)(2,1)} %all_to_all.50.sums_ref, bf16[4,432,512]{2,1,0:T(8,128)(2,1)} %bitcast.32, ...), custom_call_target="tpu_custom_call" | custom-call | tf_op jit(solution)/shard_map/pallas_call | solution.py:25
  171.4 3.0 %collective-permute-start = (bf16[1024,512]{1,0:T(8,128)(2,1)}, bf16[1024,512]{1,0:T(8,128)(2,1)S(1)}, u32[]{:S(2)}, u32[]{:S(2)}) collective-permute-start(bf16[1024,512]{1,0:T(8,128)(2,1)} %get-tuple-element.62), channel_id=1, source_target_pairs={{0,4},{4,0},{1,5},{5,1},{2,6},{6,2},{3,7},{7,3},{8,12},{12,8},{9,1... | collective-permute-start | bytes 3145736 | tf_op jit(solution)/shard_map/ppermute | solution.py:36
  182.5 6.6 %all-to-all-start.5 = ((bf16[128,2,512]{2,1,0:T(2,128)(2,1)}), bf16[128,2,512]{2,1,0:T(2,128)(2,1)S(1)}, u32[]{:S(2)}, u32[]{:S(2)}) async-start(bf16[128,2,512]{2,1,0:T(2,128)(2,1)} %reshape.210), calls=%async_computation.6 | async-start | bytes 524288 | tf_op jit(solution)/shard_map/all_to_all | solution.py:43
  193.9 7.3 %reduce-scatter.5.cloned.1.call-done.second_ref = bf16[304,512]{1,0:T(8,128)(2,1)} async-done(((bf16[1216,512]{1,0:T(8,128)(2,1)}), bf16[304,512]{1,0:T(8,128)(2,1)}) %reduce-scatter.5.cloned.1.call-update) | async-done | bytes 311312 | tf_op jit(solution)/shard_map/reduce_scatter | solution.py:493
  203.1 6.5 %all-to-all-done.5 = bf16[128,2,512]{2,1,0:T(2,128)(2,1)S(1)} async-done(((bf16[128,2,512]{2,1,0:T(2,128)(2,1)}), bf16[128,2,512]{2,1,0:T(2,128)(2,1)S(1)}, u32[]{:S(2)}, u32[]{:S(2)}) %all-to-all-start.5) | async-done | bytes 262176 | tf_op jit(solution)/shard_map/all_to_all | solution.py:43
  209.6 12.6 %all_to_all.51.in_ref = bf16[4,16,3072]{2,1,0:T(8,128)(2,1)} all-to-all(bf16[4,16,3072]{2,1,0:T(8,128)(2,1)} %bitcast.35), channel_id=1, replica_groups=mesh['z'=16,'x'=4,'c'=2,'y'=4] {'x'}, dimensions={0} | all-to-all | bytes 786432 | tf_op jit(solution)/shard_map/all_to_all | solution.py:43
  224.8 16.5 %all_to_all.52 = bf16[16,2,1536]{2,1,0:T(2,128)(2,1)S(1)} all-to-all(bf16[16,2,1536]{2,1,0:T(2,128)(2,1)S(1)} %reshape.215), channel_id=1, replica_groups=mesh['z'=16,'x'=4,'c'=2,'y'=4] {'z'}, dimensions={0} | all-to-all | bytes 196608 | tf_op jit(solution)/shard_map/all_to_all | solution.py:43
  241.4 15.1 %all_to_all.53 = bf16[16,2,1536]{2,1,0:T(2,128)(2,1)S(1)} all-to-all(bf16[16,2,1536]{2,1,0:T(2,128)(2,1)S(1)} %broadcast_in_dim.29), channel_id=1, replica_groups=mesh['z'=16,'x'=4,'c'=2,'y'=4] {'z'}, dimensions={0} | all-to-all | bytes 196608 | tf_op jit(solution)/shard_map/all_to_all | solution.py:43
  257.5 7.9 %all-to-all-start.9 = ((bf16[8,16,3072]{2,1,0:T(8,128)(2,1)}), bf16[8,16,3072]{2,1,0:T(8,128)(2,1)S(1)}, u32[]{:S(2)}, u32[]{:S(2)}) async-start(bf16[8,16,3072]{2,1,0:T(8,128)(2,1)} %broadcast_in_dim.31), calls=%async_computation.11 | async-start | bytes 1572864 | tf_op jit(solution)/shard_map/all_to_all | solution.py:43
  273.1 4.4 %all-to-all-done.9.in_ref = bf16[8,16,3072]{2,1,0:T(8,128)(2,1)S(1)} async-done(((bf16[8,16,3072]{2,1,0:T(8,128)(2,1)}), bf16[8,16,3072]{2,1,0:T(8,128)(2,1)S(1)}, u32[]{:S(2)}, u32[]{:S(2)}) %all-to-all-start.9) | async-done | bytes 786464 | tf_op jit(solution)/shard_map/all_to_all | solution.py:43
  (59 shorter events, 46.1 us)
Async XLA Ops:
  7.2 46.8 %all-gather.5.cloned.1.call-start = ((), (), s32[]{:S(2)}) async-start(), calls=%async_computation.14 | async-start | bytes 1556480 | tf_op jit(solution)/shard_map/all_gather | solution.py:391
  7.2 25.6 %copy-start.4 = (bf16[128,512]{1,0:T(8,128)(2,1)S(1)}, bf16[128,512]{1,0:T(8,128)(2,1)}, u32[]{:S(2)}) copy-start(bf16[128,512]{1,0:T(8,128)(2,1)} %param.18) | copy-start | bytes 393220
  9.8 98.7 %all-gather.7.cloned.1.call-start = ((), (), s32[]{:S(2)}) async-start(), calls=%async_computation.15 | async-start | bytes 2211840 | tf_op jit(solution)/shard_map/all_gather | solution.py:393
  12.4 40.9 %all-to-all-start = ((bf16[128,2,512]{2,1,0:T(2,128)(2,1)}), bf16[128,2,512]{2,1,0:T(2,128)(2,1)S(1)}, u32[]{:S(2)}, u32[]{:S(2)}) async-start(bf16[128,2,512]{2,1,0:T(2,128)(2,1)} %reshape.204), calls=%async_computation | async-start | bytes 524288 | tf_op jit(solution)/shard_map/all_to_all | solution.py:43
  57.7 14.3 %all-to-all-start.1 = ((bf16[4,160,512]{2,1,0:T(8,128)(2,1)}), bf16[4,160,512]{2,1,0:T(8,128)(2,1)S(1)}, u32[]{:S(2)}, u32[]{:S(2)}) async-start(bf16[4,160,512]{2,1,0:T(8,128)(2,1)} %get-tuple-element.43), calls=%async_computation.1 | async-start | bytes 1310720 | tf_op jit(solution)/shard_map/all_to_all | solution.py:43
  72.0 0.8 copy-start.1
  76.8 31.0 %all-to-all-start.2 = ((bf16[128,2,256]{2,1,0:T(2,128)(2,1)}), bf16[128,2,256]{2,1,0:T(2,128)(2,1)S(1)}, u32[]{:S(2)}, u32[]{:S(2)}) async-start(bf16[128,2,256]{2,1,0:T(2,128)(2,1)} %reshape.206), calls=%async_computation.2 | async-start | bytes 262144 | tf_op jit(solution)/shard_map/all_to_all | solution.py:43
  116.0 23.2 %all-to-all-start.3 = ((bf16[128,2,256]{2,1,0:T(2,128)(2,1)}), bf16[128,2,256]{2,1,0:T(2,128)(2,1)S(1)}, u32[]{:S(2)}, u32[]{:S(2)}) async-start(bf16[128,2,256]{2,1,0:T(2,128)(2,1)} %reshape.208), calls=%async_computation.3 | async-start | bytes 262144 | tf_op jit(solution)/shard_map/all_to_all | solution.py:43
  123.2 66.0 %reduce-scatter.3.cloned.1.call-start = ((), (), s32[]{:S(2)}) async-start(), calls=%async_computation.12 | async-start | bytes 1556480 | tf_op jit(solution)/shard_map/reduce_scatter | solution.py:454
  139.3 61.9 %reduce-scatter.5.cloned.1.call-start = ((), (), s32[]{:S(2)}) async-start(), calls=%async_computation.13 | async-start | bytes 1556480 | tf_op jit(solution)/shard_map/reduce_scatter | solution.py:493
  171.4 5.4 %collective-permute-start = (bf16[1024,512]{1,0:T(8,128)(2,1)}, bf16[1024,512]{1,0:T(8,128)(2,1)S(1)}, u32[]{:S(2)}, u32[]{:S(2)}) collective-permute-start(bf16[1024,512]{1,0:T(8,128)(2,1)} %get-tuple-element.62), channel_id=1, source_target_pairs={{0,4},{4,0},{1,5},{5,1},{2,6},{6,2},{3,7},{7,3},{8,12},{12,8},{9,1... | collective-permute-start | bytes 3145736 | tf_op jit(solution)/shard_map/ppermute | solution.py:36
  176.8 1.0 copy-start.2
  180.7 0.9 copy-start.3
  182.5 27.1 %all-to-all-start.5 = ((bf16[128,2,512]{2,1,0:T(2,128)(2,1)}), bf16[128,2,512]{2,1,0:T(2,128)(2,1)S(1)}, u32[]{:S(2)}, u32[]{:S(2)}) async-start(bf16[128,2,512]{2,1,0:T(2,128)(2,1)} %reshape.210), calls=%async_computation.6 | async-start | bytes 524288 | tf_op jit(solution)/shard_map/all_to_all | solution.py:43
  190.1 3.8 %collective-permute-start.1 = (bf16[128,512]{1,0:T(8,128)(2,1)S(1)}, bf16[128,512]{1,0:T(8,128)(2,1)S(1)}, u32[]{:S(2)}, u32[]{:S(2)}) collective-permute-start(bf16[128,512]{1,0:T(8,128)(2,1)S(1)} %bitcast.46), channel_id=1, source_target_pairs={{0,4},{4,0},{1,5},{5,1},{2,6},{6,2},{3,7},{7,3},{8,12},{12,8},{9,1... | collective-permute-start | bytes 393224 | tf_op jit(solution)/shard_map/ppermute | solution.py:495
  193.9 7.3 %copy-start.5 = (bf16[128,512]{1,0:T(8,128)(2,1)}, bf16[128,512]{1,0:T(8,128)(2,1)S(1)}, u32[]{:S(2)}) copy-start(bf16[128,512]{1,0:T(8,128)(2,1)S(1)} %collective-permute-done.1.given_ref) | copy-start | bytes 393220
  257.5 20.1 %all-to-all-start.9 = ((bf16[8,16,3072]{2,1,0:T(8,128)(2,1)}), bf16[8,16,3072]{2,1,0:T(8,128)(2,1)S(1)}, u32[]{:S(2)}, u32[]{:S(2)}) async-start(bf16[8,16,3072]{2,1,0:T(8,128)(2,1)} %broadcast_in_dim.31), calls=%async_computation.11 | async-start | bytes 1572864 | tf_op jit(solution)/shard_map/all_to_all | solution.py:43
  277.6 0.9 copy-start
Sparse Core Ops, SparseCore 0:
  10.7 41.0 all-gather.4
  53.9 36.3 all-gather.6
  139.4 27.1 reduce-scatter.2
  180.8 20.3 reduce-scatter.4

commit v8 on v6

--- a/solution.py
+++ b/solution.py
@@ -39,10 +39,8 @@
     return call(kernel, [(size, BF)], keep, given, tail)[0]
 
 
-def onward(array, me):
+def onward(blocks):
     n = lax.axis_size("y")
-    size = (array.shape[0] // n, array.shape[1])
-    blocks = call(deal_out_kernel, [(size, BF)] * n, array, me=me)
     return [blocks[0]] + [
         lax.ppermute(blocks[k], "y", [(i, (i + k) % n) for i in range(n)]) for k in range(1, n)
     ]
@@ -465,6 +463,7 @@
         scratch=[pltpu.VMEM((width, 2 * width), BF)],
     )
     first = over_cores(*first)
+    first = call(deal_out_kernel, [((first.shape[0] // feat, width), BF)] * feat, first, me=me)
     node_part, at_src = call(
         bind(owner_kernel, rows),
         [all_sums, one_sum],
@@ -476,7 +475,7 @@
         me=me,
     )
 
-    node_in, first = lax.optimization_barrier((exchange(node_part, "y"), first))
+    node_in, *first = lax.optimization_barrier((exchange(node_part, "y"), *first))
 
     node_grad, slot_out, *second = call(
         bind(backward_kernel, rows, own),
@@ -503,8 +502,8 @@
     )
     slot_back = exchange(slot_out.reshape(dom, caps, width), DOM)
     second = over_cores(*second)
-    first, second = lax.optimization_barrier((first, second))
-    first = onward(first, me)
+    second, *first = lax.optimization_barrier((second, *first))
+    first = onward(first)
     second = lax.psum_scatter(second, "y", scatter_dimension=0, tiled=True)
     (level,) = call(level_kernel, [((half, 6 * width), BF)], second, *first)
     slot_back, level = lax.optimization_barrier((slot_back, level))

time: 288 us -> 289 us (level)
    unnamed x25 -> x31, local copies, waits for them, and re-layouts: 8.83 us -> 8.85 us
where the time goes in v8:
time: 289 us; the launch traced here: 287 us
  starting transfers between devices  79.7 us (28%)
  blocking collectives  64.5 us (22%)
  waiting for transfers between devices  62.4 us (22%)
  Pallas kernels  47 us (16%)
  local copies, waits for them, and re-layouts  17 us (6%)
  between operations  14 us (5%)
    all_to_all x7, starting transfers between devices, exchange(): return lax.all_to_all(array, axes, 0, 0, tiled=True)  65.1 us
    all_to_all x3, blocking collectives, exchange(): return lax.all_to_all(array, axes, 0, 0, tiled=True)  50.3 us
    all_to_all x7, waiting for transfers between devices, exchange(): return lax.all_to_all(array, axes, 0, 0, tiled=True)  49.2 us
    pallas_call x16, Pallas kernels, call(): pl.pallas_call(kernel, out_shape=tuple((jax.ShapeDtypeStruct(s, d) for s,...  47 us
    all_gather x1, blocking collectives, per_device(): full_enc2 = lax.all_gather(w_enc2, 'y', axis=0, tiled=True)  14.1 us
    ppermute x3, waiting for transfers between devices, onward(): lax.ppermute(blocks[k], 'y', [(i, (i + k) % n) for i in range(n)])  10 us
    unnamed x31, local copies, waits for them, and re-layouts  8.85 us
    ppermute x3, starting transfers between devices, onward(): lax.ppermute(blocks[k], 'y', [(i, (i + k) % n) for i in range(n)])  8.42 us
  transfers between devices with their start and end apart: 15, of which 9 were waited for; matrix products, arithmetic and copies ran while one was open for 3% of the time, Pallas kernels for 9%

profile of v8, /device:TPU:1, one launch (start us, length us, event | category | flops | bytes accessed | tf_op | source)
XLA Modules:
  0.0 287.2 jit_solution(2792325219557826201)
XLA Ops:
  12.4 20.4 %all-to-all-start = ((bf16[128,2,512]{2,1,0:T(2,128)(2,1)}), bf16[128,2,512]{2,1,0:T(2,128)(2,1)S(1)}, u32[]{:S(2)}, u32[]{:S(2)}) async-start(bf16[128,2,512]{2,1,0:T(2,128)(2,1)} %reshape.198), calls=%async_computation | async-start | bytes 524288 | tf_op jit(solution)/shard_map/all_to_all | solution.py:50
  32.8 14.1 %all_gather.17.w_ref = bf16[512,512]{1,0:T(8,128)(2,1)} all-gather(bf16[128,512]{1,0:T(8,128)(2,1)S(1)} %copy-done.9), channel_id=1, replica_groups=mesh['z'=16,'x'=4,'c'=2,'y'=4] {'y'}, dimensions={0}, use_global_device_ids=true | all-gather | bytes 655360 | tf_op jit(solution)/shard_map/all_gather | solution.py:403
  47.0 6.3 %all-to-all-done = bf16[128,2,512]{2,1,0:T(2,128)(2,1)S(1)} async-done(((bf16[128,2,512]{2,1,0:T(2,128)(2,1)}), bf16[128,2,512]{2,1,0:T(2,128)(2,1)S(1)}, u32[]{:S(2)}, u32[]{:S(2)}) %all-to-all-start) | async-done | bytes 262176 | tf_op jit(solution)/shard_map/all_to_all | solution.py:50
  54.0 3.6 %shard_map.206 = (bf16[4,160,512]{2,1,0:T(8,128)(2,1)}, f32[256,512]{1,0:T(8,128)}, f32[256,512]{1,0:T(8,128)}, f32[256,1]{1,0:T(8,128)}) custom-call(bf16[128,1024]{1,0:T(8,128)(2,1)} %bitcast.29, s32[2,128]{1,0:T(2,128)} %bitcast.45, bf16[4,304,512]{2,1,0:T(8,128)(2,1)} %bitcast.20, bf16[512,512]{1,0:T(8,128)(2,1)} %all_gather.17.w_ref), custom_call_target="tpu_custom_call" | custom-call | tf_op jit(solution)/shard_map/pallas_call | solution.py:25
  57.6 4.2 %all-to-all-start.1 = ((bf16[4,160,512]{2,1,0:T(8,128)(2,1)}), bf16[4,160,512]{2,1,0:T(8,128)(2,1)S(1)}, u32[]{:S(2)}, u32[]{:S(2)}) async-start(bf16[4,160,512]{2,1,0:T(8,128)(2,1)} %get-tuple-element.58), calls=%async_computation.1 | async-start | bytes 1310720 | tf_op jit(solution)/shard_map/all_to_all | solution.py:50
  63.2 8.7 %all-to-all-done.1.sums_ref = bf16[4,160,512]{2,1,0:T(8,128)(2,1)S(1)} async-done(((bf16[4,160,512]{2,1,0:T(8,128)(2,1)}), bf16[4,160,512]{2,1,0:T(8,128)(2,1)S(1)}, u32[]{:S(2)}, u32[]{:S(2)}) %all-to-all-start.1) | async-done | bytes 655392 | tf_op jit(solution)/shard_map/all_to_all | solution.py:50
  76.8 14.9 %all-to-all-start.2 = ((bf16[128,2,256]{2,1,0:T(2,128)(2,1)}), bf16[128,2,256]{2,1,0:T(2,128)(2,1)S(1)}, u32[]{:S(2)}, u32[]{:S(2)}) async-start(bf16[128,2,256]{2,1,0:T(2,128)(2,1)} %reshape.200), calls=%async_computation.2 | async-start | bytes 262144 | tf_op jit(solution)/shard_map/all_to_all | solution.py:50
  93.1 14.6 %all-to-all-done.2 = bf16[128,2,256]{2,1,0:T(2,128)(2,1)S(1)} async-done(((bf16[128,2,256]{2,1,0:T(2,128)(2,1)}), bf16[128,2,256]{2,1,0:T(2,128)(2,1)S(1)}, u32[]{:S(2)}, u32[]{:S(2)}) %all-to-all-start.2) | async-done | bytes 131104 | tf_op jit(solution)/shard_map/all_to_all | solution.py:50
  108.4 6.0 %shard_map.208 = (bf16[128,512]{1,0:T(8,128)(2,1)}, f32[160,512]{1,0:T(8,128)}, bf16[160,512]{1,0:T(8,128)(2,1)}, f32[160,512]{1,0:T(8,128)}, bf16[640,512]{1,0:T(8,128)(2,1)}, /*index=5*/bf16[640,512]{1,0:T(8,128)(2,1)}) custom-call(bf16[160,512]{1,0:T(8,128)(2,1)} %get-tuple-element.59.latent_ref, bf16[128,512]{1,0:T(8,128)(2,1)} %bitcast.35, ...), custom_call_target="tpu_custom_call" | custom-call | tf_op jit(solution)/shard_map/pallas_call | solution.py:25
  116.0 7.1 %all-to-all-start.3 = ((bf16[128,2,256]{2,1,0:T(2,128)(2,1)}), bf16[128,2,256]{2,1,0:T(2,128)(2,1)S(1)}, u32[]{:S(2)}, u32[]{:S(2)}) async-start(bf16[128,2,256]{2,1,0:T(2,128)(2,1)} %reshape.202), calls=%async_computation.3 | async-start | bytes 262144 | tf_op jit(solution)/shard_map/all_to_all | solution.py:50
  123.1 3.3 %shard_map.210 = (bf16[512,512]{1,0:T(8,128)(2,1)}, bf16[512,512]{1,0:T(8,128)(2,1)}, bf16[192,512]{1,0:T(8,128)(2,1)}) custom-call(s32[2]{0:T(128)} %pad_add_fusion.me_ref, bf16[160,512]{1,0:T(8,128)(2,1)} %get-tuple-element.59.latent_ref, bf16[160,512]{1,0:T(8,128)(2,1)} %get-tuple-element.64.dst_ref, bf16[640,512]{1,0:T(8,128)(2,1)} %get-tuple-element.66.hidden_ref, ...), custom_call_target="tpu_custom_call" | custom-call | tf_op jit(solution)/shard_map/pallas_call | solution.py:25
  129.5 9.7 %all-to-all-done.3 = bf16[128,2,256]{2,1,0:T(2,128)(2,1)S(1)} async-done(((bf16[128,2,256]{2,1,0:T(2,128)(2,1)}), bf16[128,2,256]{2,1,0:T(2,128)(2,1)S(1)}, u32[]{:S(2)}, u32[]{:S(2)}) %all-to-all-start.3) | async-done | bytes 131104 | tf_op jit(solution)/shard_map/all_to_all | solution.py:50
  143.0 3.5 %all-to-all-start.4 = ((bf16[4,160,512]{2,1,0:T(8,128)(2,1)}), bf16[4,160,512]{2,1,0:T(8,128)(2,1)S(1)}, u32[]{:S(2)}, u32[]{:S(2)}) async-start(bf16[4,160,512]{2,1,0:T(8,128)(2,1)} %get-tuple-element.65), calls=%async_computation.4 | async-start | bytes 1310720 | tf_op jit(solution)/shard_map/all_to_all | solution.py:50
  151.6 5.4 %all-to-all-done.4.sums_ref = bf16[4,160,512]{2,1,0:T(8,128)(2,1)S(1)} async-done(((bf16[4,160,512]{2,1,0:T(8,128)(2,1)}), bf16[4,160,512]{2,1,0:T(8,128)(2,1)S(1)}, u32[]{:S(2)}, u32[]{:S(2)}) %all-to-all-start.4) | async-done | bytes 655392 | tf_op jit(solution)/shard_map/all_to_all | solution.py:50
  157.9 5.6 %shard_map.213 = (f32[160,512]{1,0:T(8,128)}, bf16[128,1024]{1,0:T(8,128)(2,1)}, bf16[1024,512]{1,0:T(8,128)(2,1)}, bf16[1024,512]{1,0:T(8,128)(2,1)}, bf16[192,512]{1,0:T(8,128)(2,1)}) custom-call(s32[2]{0:T(128)} %pad_add_fusion.me_ref, bf16[4,160,512]{2,1,0:T(8,128)(2,1)} %copy-done.2, bf16[4,432,512]{2,1,0:T(8,128)(2,1)} %bitcast.28, ...), custom_call_target="tpu_custom_call" | custom-call | tf_op jit(solution)/shard_map/pallas_call | solution.py:25
  174.9 7.0 %all-to-all-start.5 = ((bf16[128,2,512]{2,1,0:T(2,128)(2,1)}), bf16[128,2,512]{2,1,0:T(2,128)(2,1)S(1)}, u32[]{:S(2)}, u32[]{:S(2)}) async-start(bf16[128,2,512]{2,1,0:T(2,128)(2,1)} %reshape.204), calls=%async_computation.5 | async-start | bytes 524288 | tf_op jit(solution)/shard_map/all_to_all | solution.py:50
  184.1 3.7 %collective-permute-start.3 = (bf16[176,512]{1,0:T(8,128)(2,1)S(1)}, bf16[176,512]{1,0:T(8,128)(2,1)S(1)}, u32[]{:S(2)}, u32[]{:S(2)}) collective-permute-start(bf16[176,512]{1,0:T(8,128)(2,1)S(1)} %copy-done.11), channel_id=1, source_target_pairs={{0,2},{1,3},{2,0},{3,1},{4,6},{5,7},{6,4},{7,5},{8,10},{9,11},{10,... | collective-permute-start | bytes 540680 | tf_op jit(solution)/shard_map/ppermute | solution.py:45
  190.4 4.8 %collective-permute-done.2.b1_ref = bf16[176,512]{1,0:T(8,128)(2,1)S(1)} collective-permute-done((bf16[176,512]{1,0:T(8,128)(2,1)S(1)}, bf16[176,512]{1,0:T(8,128)(2,1)S(1)}, u32[]{:S(2)}, u32[]{:S(2)}) %collective-permute-start.2) | collective-permute-done | bytes 180256 | tf_op jit(solution)/shard_map/ppermute | solution.py:45
  195.1 5.2 %collective-permute-done.3.b2_ref = bf16[176,512]{1,0:T(8,128)(2,1)S(1)} collective-permute-done((bf16[176,512]{1,0:T(8,128)(2,1)S(1)}, bf16[176,512]{1,0:T(8,128)(2,1)S(1)}, u32[]{:S(2)}, u32[]{:S(2)}) %collective-permute-start.3) | collective-permute-done | bytes 180256 | tf_op jit(solution)/shard_map/ppermute | solution.py:45
  203.2 11.7 %all_to_all.50.in_ref = bf16[4,16,3072]{2,1,0:T(8,128)(2,1)} all-to-all(bf16[4,16,3072]{2,1,0:T(8,128)(2,1)} %bitcast.31), channel_id=1, replica_groups=mesh['z'=16,'x'=4,'c'=2,'y'=4] {'x'}, dimensions={0} | all-to-all | bytes 786432 | tf_op jit(solution)/shard_map/all_to_all | solution.py:50
  217.5 23.6 %all_to_all.51 = bf16[16,2,1536]{2,1,0:T(2,128)(2,1)S(1)} all-to-all(bf16[16,2,1536]{2,1,0:T(2,128)(2,1)S(1)} %reshape.207), channel_id=1, replica_groups=mesh['z'=16,'x'=4,'c'=2,'y'=4] {'z'}, dimensions={0} | all-to-all | bytes 196608 | tf_op jit(solution)/shard_map/all_to_all | solution.py:50
  241.2 15.1 %all_to_all.52 = bf16[16,2,1536]{2,1,0:T(2,128)(2,1)S(1)} all-to-all(bf16[16,2,1536]{2,1,0:T(2,128)(2,1)S(1)} %broadcast_in_dim.29), channel_id=1, replica_groups=mesh['z'=16,'x'=4,'c'=2,'y'=4] {'z'}, dimensions={0} | all-to-all | bytes 196608 | tf_op jit(solution)/shard_map/all_to_all | solution.py:50
  257.3 7.9 %all-to-all-start.9 = ((bf16[8,16,3072]{2,1,0:T(8,128)(2,1)}), bf16[8,16,3072]{2,1,0:T(8,128)(2,1)S(1)}, u32[]{:S(2)}, u32[]{:S(2)}) async-start(bf16[8,16,3072]{2,1,0:T(8,128)(2,1)} %broadcast_in_dim.31), calls=%async_computation.10 | async-start | bytes 1572864 | tf_op jit(solution)/shard_map/all_to_all | solution.py:50
  273.1 4.3 %all-to-all-done.9.in_ref = bf16[8,16,3072]{2,1,0:T(8,128)(2,1)S(1)} async-done(((bf16[8,16,3072]{2,1,0:T(8,128)(2,1)}), bf16[8,16,3072]{2,1,0:T(8,128)(2,1)S(1)}, u32[]{:S(2)}, u32[]{:S(2)}) %all-to-all-start.9) | async-done | bytes 786464 | tf_op jit(solution)/shard_map/all_to_all | solution.py:50
  (77 shorter events, 62.3 us)
Async XLA Ops:
  7.2 46.8 %all-gather.5.cloned.1.call-start = ((), (), s32[]{:S(2)}) async-start(), calls=%async_computation.12 | async-start | bytes 1556480 | tf_op jit(solution)/shard_map/all_gather | solution.py:402
  7.2 25.6 %copy-start.9 = (bf16[128,512]{1,0:T(8,128)(2,1)S(1)}, bf16[128,512]{1,0:T(8,128)(2,1)}, u32[]{:S(2)}) copy-start(bf16[128,512]{1,0:T(8,128)(2,1)} %param.18) | copy-start | bytes 393220
  9.8 98.6 %all-gather.7.cloned.1.call-start = ((), (), s32[]{:S(2)}) async-start(), calls=%async_computation.13 | async-start | bytes 2211840 | tf_op jit(solution)/shard_map/all_gather | solution.py:404
  12.4 40.9 %all-to-all-start = ((bf16[128,2,512]{2,1,0:T(2,128)(2,1)}), bf16[128,2,512]{2,1,0:T(2,128)(2,1)S(1)}, u32[]{:S(2)}, u32[]{:S(2)}) async-start(bf16[128,2,512]{2,1,0:T(2,128)(2,1)} %reshape.198), calls=%async_computation | async-start | bytes 524288 | tf_op jit(solution)/shard_map/all_to_all | solution.py:50
  57.6 14.3 %all-to-all-start.1 = ((bf16[4,160,512]{2,1,0:T(8,128)(2,1)}), bf16[4,160,512]{2,1,0:T(8,128)(2,1)S(1)}, u32[]{:S(2)}, u32[]{:S(2)}) async-start(bf16[4,160,512]{2,1,0:T(8,128)(2,1)} %get-tuple-element.58), calls=%async_computation.1 | async-start | bytes 1310720 | tf_op jit(solution)/shard_map/all_to_all | solution.py:50
  76.8 31.0 %all-to-all-start.2 = ((bf16[128,2,256]{2,1,0:T(2,128)(2,1)}), bf16[128,2,256]{2,1,0:T(2,128)(2,1)S(1)}, u32[]{:S(2)}, u32[]{:S(2)}) async-start(bf16[128,2,256]{2,1,0:T(2,128)(2,1)} %reshape.200), calls=%async_computation.2 | async-start | bytes 262144 | tf_op jit(solution)/shard_map/all_to_all | solution.py:50
  116.0 23.2 %all-to-all-start.3 = ((bf16[128,2,256]{2,1,0:T(2,128)(2,1)}), bf16[128,2,256]{2,1,0:T(2,128)(2,1)S(1)}, u32[]{:S(2)}, u32[]{:S(2)}) async-start(bf16[128,2,256]{2,1,0:T(2,128)(2,1)} %reshape.202), calls=%async_computation.3 | async-start | bytes 262144 | tf_op jit(solution)/shard_map/all_to_all | solution.py:50
  126.5 20.1 %collective-permute-start = (bf16[512,512]{1,0:T(8,128)(2,1)}, bf16[512,512]{1,0:T(8,128)(2,1)S(1)}, u32[]{:S(2)}, u32[]{:S(2)}) collective-permute-start(bf16[512,512]{1,0:T(8,128)(2,1)} %get-tuple-element.70), channel_id=1, source_target_pairs={{0,4},{4,0},{1,5},{5,1},{2,6},{6,2},{3,7},{7,3},{8,12},{12,8},{9,1... | collective-permute-start | bytes 1572872 | tf_op jit(solution)/shard_map/ppermute | solution.py:36
  143.0 14.1 %all-to-all-start.4 = ((bf16[4,160,512]{2,1,0:T(8,128)(2,1)}), bf16[4,160,512]{2,1,0:T(8,128)(2,1)S(1)}, u32[]{:S(2)}, u32[]{:S(2)}) async-start(bf16[4,160,512]{2,1,0:T(8,128)(2,1)} %get-tuple-element.65), calls=%async_computation.4 | async-start | bytes 1310720 | tf_op jit(solution)/shard_map/all_to_all | solution.py:50
  146.5 53.9 %reduce-scatter.2.cloned.1.call-start = ((), (), s32[]{:S(2)}) async-start(), calls=%async_computation.11 | async-start | bytes 1556480 | tf_op jit(solution)/shard_map/reduce_scatter | solution.py:507
  157.1 0.9 copy-start.2
  163.5 5.6 %collective-permute-start.1 = (bf16[1024,512]{1,0:T(8,128)(2,1)}, bf16[1024,512]{1,0:T(8,128)(2,1)S(1)}, u32[]{:S(2)}, u32[]{:S(2)}) collective-permute-start(bf16[1024,512]{1,0:T(8,128)(2,1)} %get-tuple-element.82), channel_id=1, source_target_pairs={{0,4},{4,0},{1,5},{5,1},{2,6},{6,2},{3,7},{7,3},{8,12},{12,8},{9,1... | collective-permute-start | bytes 3145736 | tf_op jit(solution)/shard_map/ppermute | solution.py:36
  169.2 1.0 copy-start.3
  173.0 0.9 copy-start.8
  173.0 8.9 %copy-start.12 = (bf16[176,512]{1,0:T(8,128)(2,1)S(1)}, bf16[176,512]{1,0:T(8,128)(2,1)}, u32[]{:S(2)}) copy-start(bf16[176,512]{1,0:T(8,128)(2,1)} %get-tuple-element.89) | copy-start | bytes 540676
  173.0 11.1 %copy-start.11 = (bf16[176,512]{1,0:T(8,128)(2,1)S(1)}, bf16[176,512]{1,0:T(8,128)(2,1)}, u32[]{:S(2)}) copy-start(bf16[176,512]{1,0:T(8,128)(2,1)} %get-tuple-element.90) | copy-start | bytes 540676
  173.0 14.8 %copy-start.10 = (bf16[176,512]{1,0:T(8,128)(2,1)S(1)}, bf16[176,512]{1,0:T(8,128)(2,1)}, u32[]{:S(2)}) copy-start(bf16[176,512]{1,0:T(8,128)(2,1)} %get-tuple-element.91) | copy-start | bytes 540676
  174.9 28.3 %all-to-all-start.5 = ((bf16[128,2,512]{2,1,0:T(2,128)(2,1)}), bf16[128,2,512]{2,1,0:T(2,128)(2,1)S(1)}, u32[]{:S(2)}, u32[]{:S(2)}) async-start(bf16[128,2,512]{2,1,0:T(2,128)(2,1)} %reshape.204), calls=%async_computation.5 | async-start | bytes 524288 | tf_op jit(solution)/shard_map/all_to_all | solution.py:50
  181.9 13.2 %collective-permute-start.2 = (bf16[176,512]{1,0:T(8,128)(2,1)S(1)}, bf16[176,512]{1,0:T(8,128)(2,1)S(1)}, u32[]{:S(2)}, u32[]{:S(2)}) collective-permute-start(bf16[176,512]{1,0:T(8,128)(2,1)S(1)} %copy-done.12), channel_id=1, source_target_pairs={{0,1},{1,2},{2,3},{3,0},{4,5},{5,6},{6,7},{7,4},{8,9},{9,10},{10,1... | collective-permute-start | bytes 540680 | tf_op jit(solution)/shard_map/ppermute | solution.py:45
  184.1 16.2 %collective-permute-start.3 = (bf16[176,512]{1,0:T(8,128)(2,1)S(1)}, bf16[176,512]{1,0:T(8,128)(2,1)S(1)}, u32[]{:S(2)}, u32[]{:S(2)}) collective-permute-start(bf16[176,512]{1,0:T(8,128)(2,1)S(1)} %copy-done.11), channel_id=1, source_target_pairs={{0,2},{1,3},{2,0},{3,1},{4,6},{5,7},{6,4},{7,5},{8,10},{9,11},{10,... | collective-permute-start | bytes 540680 | tf_op jit(solution)/shard_map/ppermute | solution.py:45
  187.8 12.5 %collective-permute-start.4 = (bf16[176,512]{1,0:T(8,128)(2,1)S(1)}, bf16[176,512]{1,0:T(8,128)(2,1)S(1)}, u32[]{:S(2)}, u32[]{:S(2)}) collective-permute-start(bf16[176,512]{1,0:T(8,128)(2,1)S(1)} %copy-done.10), channel_id=1, source_target_pairs={{0,3},{1,0},{2,1},{3,2},{4,7},{5,4},{6,5},{7,6},{8,11},{9,8},{10,9... | collective-permute-start | bytes 540680 | tf_op jit(solution)/shard_map/ppermute | solution.py:45
  195.1 5.3 %copy-start.4 = (bf16[176,512]{1,0:T(8,128)(2,1)}, bf16[176,512]{1,0:T(8,128)(2,1)S(1)}, u32[]{:S(2)}) copy-start(bf16[176,512]{1,0:T(8,128)(2,1)S(1)} %collective-permute-done.2.b1_ref) | copy-start | bytes 540676
  257.3 20.1 %all-to-all-start.9 = ((bf16[8,16,3072]{2,1,0:T(8,128)(2,1)}), bf16[8,16,3072]{2,1,0:T(8,128)(2,1)S(1)}, u32[]{:S(2)}, u32[]{:S(2)}) async-start(bf16[8,16,3072]{2,1,0:T(8,128)(2,1)} %broadcast_in_dim.31), calls=%async_computation.10 | async-start | bytes 1572864 | tf_op jit(solution)/shard_map/all_to_all | solution.py:50
  277.4 0.9 copy-start
  (4 other events, 3.0 us)
Sparse Core Ops, SparseCore 0:
  10.7 41.0 all-gather.4
  53.9 36.3 all-gather.6
  173.2 24.1 reduce-scatter.1

commit v9 on v7

--- a/solution.py
+++ b/solution.py
@@ -450,7 +450,6 @@
         messages,
         scratch=[pltpu.VMEM((width, 2 * width), BF)],
     )
-    returned, first = lax.optimization_barrier((returned, first))
     first = lax.psum_scatter(first, "y", scatter_dimension=0, tiled=True)
     node_part, at_src = call(
         bind(owner_kernel, rows),

time: 289 us -> 284 us (0.983)
  blocking collectives: 80.9 us -> 96.7 us
  waiting for transfers between devices: 64.9 us -> 52 us
  starting transfers between devices: 67.1 us -> 60.1 us
    all_to_all x4 -> x5, blocking collectives: 66.7 us -> 82.5 us  [exchange(): return lax.all_to_all(array, axes, 0, 0, tiled=True)]
    all_to_all x6 -> x5, waiting for transfers between devices: 53.4 us -> 40.5 us  [exchange(): return lax.all_to_all(array, axes, 0, 0, tiled=True)]
    all_to_all x6 -> x5, starting transfers between devices: 61.1 us -> 54 us  [exchange(): return lax.all_to_all(array, axes, 0, 0, tiled=True)]
    unnamed x17 -> x19, local copies, waits for them, and re-layouts: 6.48 us -> 7.3 us
  transfers between devices with their start and end apart: 12 -> 11, of which waited for: 9 -> 8; matrix products, arithmetic and copies ran while one was open for 4% -> 4% of each run, Pallas kernels for 10% -> 9%
where the time goes in v9:
time: 284 us; the launch traced here: 283 us
  blocking collectives  96.7 us (34%)
  starting transfers between devices  60.1 us (21%)
  waiting for transfers between devices  52 us (18%)
  Pallas kernels  42.4 us (15%)
  local copies, waits for them, and re-layouts  14.9 us (5%)
  between operations  13.9 us (5%)
    all_to_all x5, blocking collectives, exchange(): return lax.all_to_all(array, axes, 0, 0, tiled=True)  82.5 us
    all_to_all x5, starting transfers between devices, exchange(): return lax.all_to_all(array, axes, 0, 0, tiled=True)  54 us
    pallas_call x14, Pallas kernels, call(): pl.pallas_call(kernel, out_shape=tuple((jax.ShapeDtypeStruct(s, d) for s,...  42.4 us
    all_to_all x5, waiting for transfers between devices, exchange(): return lax.all_to_all(array, axes, 0, 0, tiled=True)  40.5 us
    all_gather x1, blocking collectives, per_device(): full_enc2 = lax.all_gather(w_enc2, 'y', axis=0, tiled=True)  14.1 us
    reduce_scatter x1, waiting for transfers between devices, per_device(): second = lax.psum_scatter(second, 'y', scatter_dimension=0, tiled=True)  7.31 us
    unnamed x19, local copies, waits for them, and re-layouts  7.3 us
  transfers between devices with their start and end apart: 11, of which 8 were waited for; matrix products, arithmetic and copies ran while one was open for 4% of the time, Pallas kernels for 9%

profile of v9, /device:TPU:1, one launch (start us, length us, event | category | flops | bytes accessed | tf_op | source)
XLA Modules:
  0.0 282.7 jit_solution(1093256960441720899)
XLA Ops:
  12.4 20.4 %all-to-all-start = ((bf16[128,2,512]{2,1,0:T(2,128)(2,1)}), bf16[128,2,512]{2,1,0:T(2,128)(2,1)S(1)}, u32[]{:S(2)}, u32[]{:S(2)}) async-start(bf16[128,2,512]{2,1,0:T(2,128)(2,1)} %reshape.204), calls=%async_computation | async-start | bytes 524288 | tf_op jit(solution)/shard_map/all_to_all | solution.py:43
  32.8 14.1 %all_gather.17.w_ref = bf16[512,512]{1,0:T(8,128)(2,1)} all-gather(bf16[128,512]{1,0:T(8,128)(2,1)S(1)} %copy-done.4), channel_id=1, replica_groups=mesh['z'=16,'x'=4,'c'=2,'y'=4] {'y'}, dimensions={0}, use_global_device_ids=true | all-gather | bytes 655360 | tf_op jit(solution)/shard_map/all_gather | solution.py:392
  47.0 6.3 %all-to-all-done = bf16[128,2,512]{2,1,0:T(2,128)(2,1)S(1)} async-done(((bf16[128,2,512]{2,1,0:T(2,128)(2,1)}), bf16[128,2,512]{2,1,0:T(2,128)(2,1)S(1)}, u32[]{:S(2)}, u32[]{:S(2)}) %all-to-all-start) | async-done | bytes 262176 | tf_op jit(solution)/shard_map/all_to_all | solution.py:43
  54.0 3.6 %shard_map.206 = (bf16[4,160,512]{2,1,0:T(8,128)(2,1)}, f32[256,512]{1,0:T(8,128)}, f32[256,512]{1,0:T(8,128)}, f32[256,1]{1,0:T(8,128)}) custom-call(bf16[128,1024]{1,0:T(8,128)(2,1)} %bitcast.33, s32[2,128]{1,0:T(2,128)} %bitcast.51, bf16[4,304,512]{2,1,0:T(8,128)(2,1)} %bitcast.24, bf16[512,512]{1,0:T(8,128)(2,1)} %all_gather.17.w_ref), custom_call_target="tpu_custom_call" | custom-call | tf_op jit(solution)/shard_map/pallas_call | solution.py:25
  57.7 4.2 %all-to-all-start.1 = ((bf16[4,160,512]{2,1,0:T(8,128)(2,1)}), bf16[4,160,512]{2,1,0:T(8,128)(2,1)S(1)}, u32[]{:S(2)}, u32[]{:S(2)}) async-start(bf16[4,160,512]{2,1,0:T(8,128)(2,1)} %get-tuple-element.41), calls=%async_computation.1 | async-start | bytes 1310720 | tf_op jit(solution)/shard_map/all_to_all | solution.py:43
  63.3 8.7 %all-to-all-done.1.sums_ref = bf16[4,160,512]{2,1,0:T(8,128)(2,1)S(1)} async-done(((bf16[4,160,512]{2,1,0:T(8,128)(2,1)}), bf16[4,160,512]{2,1,0:T(8,128)(2,1)S(1)}, u32[]{:S(2)}, u32[]{:S(2)}) %all-to-all-start.1) | async-done | bytes 655392 | tf_op jit(solution)/shard_map/all_to_all | solution.py:43
  76.8 14.9 %all-to-all-start.2 = ((bf16[128,2,256]{2,1,0:T(2,128)(2,1)}), bf16[128,2,256]{2,1,0:T(2,128)(2,1)S(1)}, u32[]{:S(2)}, u32[]{:S(2)}) async-start(bf16[128,2,256]{2,1,0:T(2,128)(2,1)} %reshape.206), calls=%async_computation.2 | async-start | bytes 262144 | tf_op jit(solution)/shard_map/all_to_all | solution.py:43
  93.2 14.6 %all-to-all-done.2 = bf16[128,2,256]{2,1,0:T(2,128)(2,1)S(1)} async-done(((bf16[128,2,256]{2,1,0:T(2,128)(2,1)}), bf16[128,2,256]{2,1,0:T(2,128)(2,1)S(1)}, u32[]{:S(2)}, u32[]{:S(2)}) %all-to-all-start.2) | async-done | bytes 131104 | tf_op jit(solution)/shard_map/all_to_all | solution.py:43
  108.5 6.0 %shard_map.208 = (bf16[128,512]{1,0:T(8,128)(2,1)}, f32[160,512]{1,0:T(8,128)}, bf16[160,512]{1,0:T(8,128)(2,1)}, f32[160,512]{1,0:T(8,128)}, bf16[640,512]{1,0:T(8,128)(2,1)}, /*index=5*/bf16[640,512]{1,0:T(8,128)(2,1)}) custom-call(bf16[160,512]{1,0:T(8,128)(2,1)} %get-tuple-element.42.latent_ref, bf16[128,512]{1,0:T(8,128)(2,1)} %bitcast.40, ...), custom_call_target="tpu_custom_call" | custom-call | tf_op jit(solution)/shard_map/pallas_call | solution.py:25
  114.4 3.3 %shard_map.209 = bf16[1216,512]{1,0:T(8,128)(2,1)} custom-call(bf16[160,512]{1,0:T(8,128)(2,1)} %get-tuple-element.42.latent_ref, bf16[160,512]{1,0:T(8,128)(2,1)} %get-tuple-element.45.dst_ref, bf16[640,512]{1,0:T(8,128)(2,1)} %get-tuple-element.46.hidden_ref, bf16[640,512]{1,0:T(8,128)(2,1)} %get-tuple-element.47.mid_ref, ...), custom_call_target="tpu_custom_call" | custom-call | tf_op jit(solution)/shard_map/pallas_call | solution.py:25
  118.7 23.4 %all_to_all.50 = bf16[128,2,256]{2,1,0:T(2,128)(2,1)S(1)} all-to-all(bf16[128,2,256]{2,1,0:T(2,128)(2,1)S(1)} %reshape.208), channel_id=1, replica_groups=mesh['z'=16,'x'=4,'c'=2,'y'=4] {'z','x','c'}, dimensions={0} | all-to-all | bytes 262144 | tf_op jit(solution)/shard_map/all_to_all | solution.py:43
  142.7 3.1 %shard_map.211 = (bf16[4,160,512]{2,1,0:T(8,128)(2,1)}, bf16[160,512]{1,0:T(8,128)(2,1)}) custom-call(s32[2]{0:T(128)} %pad_add_fusion.me_ref, bf16[128,512]{1,0:T(8,128)(2,1)} %bitcast.41, s32[4,128]{1,0:T(4,128)} %bitcast.48, f32[160,512]{1,0:T(8,128)} %get-tuple-element.50.local_ref, bf16[160,512]{1,0:T(8,128)(2,1)} %get-tuple-element.45.dst_ref, ...), custom_call_target="tpu_custom_call" | custom-call | tf_op jit(solution)/shard_map/pallas_call | solution.py:25
  145.8 15.0 %all_to_all.51.sums_ref = bf16[4,160,512]{2,1,0:T(8,128)(2,1)} all-to-all(bf16[4,160,512]{2,1,0:T(8,128)(2,1)} %get-tuple-element.51), channel_id=1, replica_groups=mesh['z'=16,'x'=4,'c'=2,'y'=4] {'y'}, dimensions={0} | all-to-all | bytes 1310720 | tf_op jit(solution)/shard_map/all_to_all | solution.py:43
  160.8 5.6 %shard_map.212 = (f32[160,512]{1,0:T(8,128)}, bf16[128,1024]{1,0:T(8,128)(2,1)}, bf16[1024,512]{1,0:T(8,128)(2,1)}, bf16[1024,512]{1,0:T(8,128)(2,1)}, bf16[192,512]{1,0:T(8,128)(2,1)}) custom-call(s32[2]{0:T(128)} %pad_add_fusion.me_ref, bf16[4,160,512]{2,1,0:T(8,128)(2,1)} %all_to_all.51.sums_ref, bf16[4,432,512]{2,1,0:T(8,128)(2,1)} %bitcast.32, ...), custom_call_target="tpu_custom_call" | custom-call | tf_op jit(solution)/shard_map/pallas_call | solution.py:25
  166.5 3.1 %collective-permute-start = (bf16[1024,512]{1,0:T(8,128)(2,1)}, bf16[1024,512]{1,0:T(8,128)(2,1)S(1)}, u32[]{:S(2)}, u32[]{:S(2)}) collective-permute-start(bf16[1024,512]{1,0:T(8,128)(2,1)} %get-tuple-element.58), channel_id=1, source_target_pairs={{0,4},{4,0},{1,5},{5,1},{2,6},{6,2},{3,7},{7,3},{8,12},{12,8},{9,1... | collective-permute-start | bytes 3145736 | tf_op jit(solution)/shard_map/ppermute | solution.py:36
  173.1 2.9 %shard_map.213 = bf16[1216,512]{1,0:T(8,128)(2,1)} custom-call(bf16[1024,512]{1,0:T(8,128)(2,1)} %get-tuple-element.57.keep_ref, bf16[1024,512]{1,0:T(8,128)(2,1)} %copy-done.2, bf16[192,512]{1,0:T(8,128)(2,1)} %get-tuple-element.59.tail_ref), custom_call_target="tpu_custom_call" | custom-call | tf_op jit(solution)/shard_map/pallas_call | solution.py:25
  177.8 6.8 %all-to-all-start.5 = ((bf16[128,2,512]{2,1,0:T(2,128)(2,1)}), bf16[128,2,512]{2,1,0:T(2,128)(2,1)S(1)}, u32[]{:S(2)}, u32[]{:S(2)}) async-start(bf16[128,2,512]{2,1,0:T(2,128)(2,1)} %reshape.210), calls=%async_computation.6 | async-start | bytes 524288 | tf_op jit(solution)/shard_map/all_to_all | solution.py:43
  189.3 7.3 %reduce-scatter.5.cloned.1.call-done.second_ref = bf16[304,512]{1,0:T(8,128)(2,1)} async-done(((bf16[1216,512]{1,0:T(8,128)(2,1)}), bf16[304,512]{1,0:T(8,128)(2,1)}) %reduce-scatter.5.cloned.1.call-update) | async-done | bytes 311312 | tf_op jit(solution)/shard_map/reduce_scatter | solution.py:492
  198.6 6.5 %all-to-all-done.5 = bf16[128,2,512]{2,1,0:T(2,128)(2,1)S(1)} async-done(((bf16[128,2,512]{2,1,0:T(2,128)(2,1)}), bf16[128,2,512]{2,1,0:T(2,128)(2,1)S(1)}, u32[]{:S(2)}, u32[]{:S(2)}) %all-to-all-start.5) | async-done | bytes 262176 | tf_op jit(solution)/shard_map/all_to_all | solution.py:43
  205.0 12.6 %all_to_all.52.in_ref = bf16[4,16,3072]{2,1,0:T(8,128)(2,1)} all-to-all(bf16[4,16,3072]{2,1,0:T(8,128)(2,1)} %bitcast.35), channel_id=1, replica_groups=mesh['z'=16,'x'=4,'c'=2,'y'=4] {'x'}, dimensions={0} | all-to-all | bytes 786432 | tf_op jit(solution)/shard_map/all_to_all | solution.py:43
  220.2 16.5 %all_to_all.53 = bf16[16,2,1536]{2,1,0:T(2,128)(2,1)S(1)} all-to-all(bf16[16,2,1536]{2,1,0:T(2,128)(2,1)S(1)} %reshape.215), channel_id=1, replica_groups=mesh['z'=16,'x'=4,'c'=2,'y'=4] {'z'}, dimensions={0} | all-to-all | bytes 196608 | tf_op jit(solution)/shard_map/all_to_all | solution.py:43
  236.8 15.1 %all_to_all.54 = bf16[16,2,1536]{2,1,0:T(2,128)(2,1)S(1)} all-to-all(bf16[16,2,1536]{2,1,0:T(2,128)(2,1)S(1)} %broadcast_in_dim.29), channel_id=1, replica_groups=mesh['z'=16,'x'=4,'c'=2,'y'=4] {'z'}, dimensions={0} | all-to-all | bytes 196608 | tf_op jit(solution)/shard_map/all_to_all | solution.py:43
  252.9 7.8 %all-to-all-start.9 = ((bf16[8,16,3072]{2,1,0:T(8,128)(2,1)}), bf16[8,16,3072]{2,1,0:T(8,128)(2,1)S(1)}, u32[]{:S(2)}, u32[]{:S(2)}) async-start(bf16[8,16,3072]{2,1,0:T(8,128)(2,1)} %broadcast_in_dim.31), calls=%async_computation.11 | async-start | bytes 1572864 | tf_op jit(solution)/shard_map/all_to_all | solution.py:43
  268.5 4.4 %all-to-all-done.9.in_ref = bf16[8,16,3072]{2,1,0:T(8,128)(2,1)S(1)} async-done(((bf16[8,16,3072]{2,1,0:T(8,128)(2,1)}), bf16[8,16,3072]{2,1,0:T(8,128)(2,1)S(1)}, u32[]{:S(2)}, u32[]{:S(2)}) %all-to-all-start.9) | async-done | bytes 786464 | tf_op jit(solution)/shard_map/all_to_all | solution.py:43
  (60 shorter events, 42.6 us)
Async XLA Ops:
  7.2 46.8 %all-gather.5.cloned.1.call-start = ((), (), s32[]{:S(2)}) async-start(), calls=%async_computation.14 | async-start | bytes 1556480 | tf_op jit(solution)/shard_map/all_gather | solution.py:391
  7.2 25.6 %copy-start.4 = (bf16[128,512]{1,0:T(8,128)(2,1)S(1)}, bf16[128,512]{1,0:T(8,128)(2,1)}, u32[]{:S(2)}) copy-start(bf16[128,512]{1,0:T(8,128)(2,1)} %param.18) | copy-start | bytes 393220
  9.8 98.7 %all-gather.7.cloned.1.call-start = ((), (), s32[]{:S(2)}) async-start(), calls=%async_computation.15 | async-start | bytes 2211840 | tf_op jit(solution)/shard_map/all_gather | solution.py:393
  12.4 40.9 %all-to-all-start = ((bf16[128,2,512]{2,1,0:T(2,128)(2,1)}), bf16[128,2,512]{2,1,0:T(2,128)(2,1)S(1)}, u32[]{:S(2)}, u32[]{:S(2)}) async-start(bf16[128,2,512]{2,1,0:T(2,128)(2,1)} %reshape.204), calls=%async_computation | async-start | bytes 524288 | tf_op jit(solution)/shard_map/all_to_all | solution.py:43
  57.7 14.3 %all-to-all-start.1 = ((bf16[4,160,512]{2,1,0:T(8,128)(2,1)}), bf16[4,160,512]{2,1,0:T(8,128)(2,1)S(1)}, u32[]{:S(2)}, u32[]{:S(2)}) async-start(bf16[4,160,512]{2,1,0:T(8,128)(2,1)} %get-tuple-element.41), calls=%async_computation.1 | async-start | bytes 1310720 | tf_op jit(solution)/shard_map/all_to_all | solution.py:43
  72.0 0.8 copy-start.1
  76.8 31.0 %all-to-all-start.2 = ((bf16[128,2,256]{2,1,0:T(2,128)(2,1)}), bf16[128,2,256]{2,1,0:T(2,128)(2,1)S(1)}, u32[]{:S(2)}, u32[]{:S(2)}) async-start(bf16[128,2,256]{2,1,0:T(2,128)(2,1)} %reshape.206), calls=%async_computation.2 | async-start | bytes 262144 | tf_op jit(solution)/shard_map/all_to_all | solution.py:43
  91.7 92.8 %reduce-scatter.3.cloned.1.call-start = ((), (), s32[]{:S(2)}) async-start(), calls=%async_computation.12 | async-start | bytes 1556480 | tf_op jit(solution)/shard_map/reduce_scatter | solution.py:453
  117.7 0.9 copy-start.5
  117.7 78.9 %reduce-scatter.5.cloned.1.call-start = ((), (), s32[]{:S(2)}) async-start(), calls=%async_computation.13 | async-start | bytes 1556480 | tf_op jit(solution)/shard_map/reduce_scatter | solution.py:492
  166.5 5.6 %collective-permute-start = (bf16[1024,512]{1,0:T(8,128)(2,1)}, bf16[1024,512]{1,0:T(8,128)(2,1)S(1)}, u32[]{:S(2)}, u32[]{:S(2)}) collective-permute-start(bf16[1024,512]{1,0:T(8,128)(2,1)} %get-tuple-element.58), channel_id=1, source_target_pairs={{0,4},{4,0},{1,5},{5,1},{2,6},{6,2},{3,7},{7,3},{8,12},{12,8},{9,1... | collective-permute-start | bytes 3145736 | tf_op jit(solution)/shard_map/ppermute | solution.py:36
  172.1 1.0 copy-start.2
  175.9 0.9 copy-start.3
  177.8 27.2 %all-to-all-start.5 = ((bf16[128,2,512]{2,1,0:T(2,128)(2,1)}), bf16[128,2,512]{2,1,0:T(2,128)(2,1)S(1)}, u32[]{:S(2)}, u32[]{:S(2)}) async-start(bf16[128,2,512]{2,1,0:T(2,128)(2,1)} %reshape.210), calls=%async_computation.6 | async-start | bytes 524288 | tf_op jit(solution)/shard_map/all_to_all | solution.py:43
  185.6 3.8 %collective-permute-start.1 = (bf16[128,512]{1,0:T(8,128)(2,1)S(1)}, bf16[128,512]{1,0:T(8,128)(2,1)S(1)}, u32[]{:S(2)}, u32[]{:S(2)}) collective-permute-start(bf16[128,512]{1,0:T(8,128)(2,1)S(1)} %bitcast.46), channel_id=1, source_target_pairs={{0,4},{4,0},{1,5},{5,1},{2,6},{6,2},{3,7},{7,3},{8,12},{12,8},{9,1... | collective-permute-start | bytes 393224 | tf_op jit(solution)/shard_map/ppermute | solution.py:494
  189.3 7.3 %copy-start.6 = (bf16[128,512]{1,0:T(8,128)(2,1)}, bf16[128,512]{1,0:T(8,128)(2,1)S(1)}, u32[]{:S(2)}) copy-start(bf16[128,512]{1,0:T(8,128)(2,1)S(1)} %collective-permute-done.1.given_ref) | copy-start | bytes 393220
  252.9 20.0 %all-to-all-start.9 = ((bf16[8,16,3072]{2,1,0:T(8,128)(2,1)}), bf16[8,16,3072]{2,1,0:T(8,128)(2,1)S(1)}, u32[]{:S(2)}, u32[]{:S(2)}) async-start(bf16[8,16,3072]{2,1,0:T(8,128)(2,1)} %broadcast_in_dim.31), calls=%async_computation.11 | async-start | bytes 1572864 | tf_op jit(solution)/shard_map/all_to_all | solution.py:43
  272.9 0.9 copy-start
Sparse Core Ops, SparseCore 0:
  10.7 41.0 all-gather.4
  53.9 36.3 all-gather.6
  117.9 20.8 reduce-scatter.2
  176.1 20.5 reduce-scatter.4
